TPU v7x, 32 devices: a whole 2x2x4 slice. The times are simulated.
32 devices in a mesh: blk: 8 (over z, core), feat: 4 (over y, x).
Axes of the slice: x: 2, y: 2, z: 4, core: 2. Of those that a mesh axis runs over, the one named last changes fastest.
Arguments:
- grads: float32 [4096, 8192], P('blk', 'feat'), may hold values from -3000 to 3000
Outputs:
- cosine: float32 [4096, 4096], P('blk', 'feat')
All inputs are finite; a program needn't handle non-finite values.
Results may differ from a plain program's by a relative error of at most 0.000053.
Values sent between devices are 32-bit elements; how exact they have to be, the bound alone decides.
A program may use at most 128 MiB of HBM per device.

v0:
```python
import jax
import jax.numpy as jnp
from jax import lax
from jax.sharding import PartitionSpec as P


def passed_along(value, axis, steps):
    count = lax.axis_size(axis)
    pairs = [(source, (source + steps) % count) for source in range(count)]
    return lax.ppermute(value, axis, pairs)


def tile_of(left, right):
    return lax.dot_general(
        left,
        right,
        (((1,), (1,)), ((), ())),
        precision=lax.Precision.HIGHEST,
        preferred_element_type=jnp.float32,
    )


def place(partial_value, piece, column):
    offset = column * piece.shape[1]
    return lax.dynamic_update_slice(partial_value, piece, (jnp.int32(0), offset))


def local(grads):
    rows = grads.shape[0]
    blocks = lax.axis_size("blk")
    mine = lax.axis_index("blk")
    partial_value = jnp.zeros((rows, blocks * rows), jnp.float32)
    partial_value = place(partial_value, tile_of(grads, grads), mine)
    half = blocks // 2
    held = grads
    for step in range(1, half + 1):
        held = passed_along(held, "blk", 1)
        piece = tile_of(grads, held)
        partial_value = place(partial_value, piece, (mine - step) % blocks)
        if step < half:
            back = passed_along(piece.T, "blk", -step)
            partial_value = place(partial_value, back, (mine + step) % blocks)
    gram = lax.psum_scatter(partial_value, "feat", scatter_dimension=1, tiled=True)
    squares = lax.psum(jnp.sum(grads * grads, axis=1), "feat")
    every = lax.all_gather(squares, "blk", axis=0, tiled=True)
    width = gram.shape[1]
    column_sq = lax.dynamic_slice_in_dim(every, lax.axis_index("feat") * width, width)
    row_inverse = 1.0 / jnp.sqrt(squares + 1e-06)
    column_inverse = 1.0 / jnp.sqrt(column_sq + 1e-06)
    return gram * row_inverse[:, None] * column_inverse[None, :]


def solution(mesh):
    placed = (P("blk", "feat"),)
    return jax.shard_map(
        local, mesh=mesh, in_specs=placed, out_specs=P("blk", "feat"), check_vma=False
    )
```

profile of v0, /device:TPU:12, one launch (start us, length us, event | category | flops | bytes accessed | tf_op | source)
XLA Modules:
  0.0 396.6 jit_solution(12250125477740062612)
XLA Ops:
  6.5 0.0 reduce-scatter.2.cloned.1.call-start
  6.5 0.0 collective-permute-start
  6.5 48.1 %collective-permute-done = f32[512,2048]{1,0:T(8,128)S(1)} collective-permute-done((f32[512,2048]{1,0:T(8,128)}, f32[512,2048]{1,0:T(8,128)S(1)}, u32[]{:S(2)}, u32[]{:S(2)}) %collective-permute-start) | collective-permute-done | bytes 4194336 | tf_op jit(solution)/shard_map/ppermute | solution.py:10
  54.7 0.0 copy-start.2
  54.7 1.9 copy-done.2
  56.6 0.0 collective-permute-start.2
  56.6 48.0 %collective-permute-done.2 = f32[512,2048]{1,0:T(8,128)} collective-permute-done((f32[512,2048]{1,0:T(8,128)S(1)}, f32[512,2048]{1,0:T(8,128)}, u32[]{:S(2)}, u32[]{:S(2)}) %collective-permute-start.2) | collective-permute-done | bytes 4194336 | tf_op jit(solution)/shard_map/ppermute | solution.py:10
  104.6 0.0 collective-permute-start.4
  104.7 0.0 copy-start
  104.7 1.0 broadcast_in_dim.2
  105.7 1.2 copy-done
  106.8 0.0 copy-start.3
  106.8 6.9 %convolution_dynamic-update-slice_fusion.1 = f32[512,4096]{1,0:T(8,128)S(1)} fusion(f32[512,4096]{1,0:T(8,128)S(1)} %broadcast_in_dim.2, s32[]{:T(128)S(6)} %select_n.58, f32[512,2048]{1,0:T(8,128)S(1)} %copy-done), kind=kOutput, calls=%fused_computation.3 | convolution fusion | flops 6442450944 | bytes 9437188 | tf_op jit(solution)/shard_map/dot_general | solution.py:14
  113.7 0.0 copy-done.3
  113.7 7.1 %constant_dynamic-update-slice_fusion.5 = (f32[512,4096]{1,0:T(8,128)S(1)}, f32[512,512]{1,0:T(8,128)S(1)}) fusion(f32[512,4096]{1,0:T(8,128)S(1)} %convolution_dynamic-update-slice_fusion.1, s32[]{:T(128)S(6)} %select_n.60, f32[512,2048]{1,0:T(8,128)S(1)} %copy-done, f32[512,2048]{1,0:T(8,128)S(1)} %copy-done.3), kind=kOutput, calls=%fused_computation.11 | convolution fusion | flops 6442450944 | bytes 10485764 | tf_op jit(solution)/shard_map/dot_general | solution.py:14
  120.9 0.0 copy-start.1
  120.9 3.2 copy-done.1
  124.1 1.7 collective-permute-start.1
  125.8 38.3 %collective-permute-done.4 = f32[512,2048]{1,0:T(8,128)} collective-permute-done((f32[512,2048]{1,0:T(8,128)}, f32[512,2048]{1,0:T(8,128)}, u32[]{:S(2)}, u32[]{:S(2)}) %collective-permute-start.4) | collective-permute-done | bytes 4194336 | tf_op jit(solution)/shard_map/ppermute | solution.py:10
  164.1 0.0 collective-permute-start.6
  164.1 0.0 collective-permute-done.1
  164.1 0.3 copy.5
  164.5 1.1 constant_dynamic-update-slice_fusion.4
  165.5 10.4 %constant_dynamic-update-slice_fusion.3 = (f32[512,4096]{1,0:T(8,128)}, f32[512,512]{1,0:T(8,128)S(1)}) fusion(f32[512,4096]{1,0:T(8,128)} %constant_dynamic-update-slice_fusion.4, s32[]{:T(128)S(6)} %select_n.64, f32[512,2048]{1,0:T(8,128)} %param.1, f32[512,2048]{1,0:T(8,128)} %collective-permute-done.2), kind=kOutput, calls=%fused_computation.9 | convolution fusion | flops 6442450944 | bytes 10485764 | tf_op jit(solution)/shard_map/dot_general | solution.py:14
  176.0 5.8 %collective-permute-start.3 = (f32[512,512]{0,1:T(8,128)S(1)}, f32[512,512]{0,1:T(8,128)S(1)}, u32[]{:S(2)}, u32[]{:S(2)}) collective-permute-start(f32[512,512]{0,1:T(8,128)S(1)} %bitcast.17), channel_id=1, source_target_pairs={{0,24},{4,28},{8,0},{12,4},{16,8},{20,12},{24,16},{28,20},{1,25},{... | collective-permute-start | bytes 3145736 | tf_op jit(solution)/shard_map/ppermute | solution.py:10
  181.7 59.1 %collective-permute-done.3 = f32[512,512]{0,1:T(8,128)S(1)} collective-permute-done((f32[512,512]{0,1:T(8,128)S(1)}, f32[512,512]{0,1:T(8,128)S(1)}, u32[]{:S(2)}, u32[]{:S(2)}) %collective-permute-start.3) | collective-permute-done | bytes 1048608 | tf_op jit(solution)/shard_map/ppermute | solution.py:10
  240.9 0.3 copy.6
  241.2 1.1 constant_dynamic-update-slice_fusion.2
  242.3 10.4 %constant_dynamic-update-slice_fusion.1 = (f32[512,4096]{1,0:T(8,128)}, f32[512,512]{1,0:T(8,128)S(1)}) fusion(f32[512,4096]{1,0:T(8,128)} %constant_dynamic-update-slice_fusion.2, s32[]{:T(128)S(6)} %select_n.68, f32[512,2048]{1,0:T(8,128)} %param.1, f32[512,2048]{1,0:T(8,128)} %collective-permute-done.4), kind=kOutput, calls=%fused_computation.7 | convolution fusion | flops 6442450944 | bytes 10485764 | tf_op jit(solution)/shard_map/dot_general | solution.py:14
  252.7 0.0 collective-permute-start.5
  252.7 36.7 %collective-permute-done.5 = f32[512,512]{0,1:T(8,128)S(1)} collective-permute-done((f32[512,512]{0,1:T(8,128)S(1)}, f32[512,512]{0,1:T(8,128)S(1)}, u32[]{:S(2)}, u32[]{:S(2)}) %collective-permute-start.5) | collective-permute-done | bytes 1048608 | tf_op jit(solution)/shard_map/ppermute | solution.py:10
  289.3 0.3 copy.7
  289.7 1.1 constant_dynamic-update-slice_fusion
  290.8 0.0 collective-permute-done.6
  290.8 10.3 %convolution_dynamic-update-slice_fusion = f32[512,4096]{1,0:T(8,128)} fusion(f32[512,4096]{1,0:T(8,128)} %constant_dynamic-update-slice_fusion, s32[]{:T(128)S(6)} %select_n.72, f32[512,2048]{1,0:T(8,128)} %param.1, f32[512,2048]{1,0:T(8,128)} %collective-permute-done.6), kind=kOutput, calls=%fused_computation.2 | convolution fusion | flops 6442450944 | bytes 9437188 | tf_op jit(solution)/shard_map/dot_general | solution.py:14
  301.0 0.0 reduce-scatter.2.cloned.1.call-update
  301.1 2.5 multiply_reduce_fusion
  303.6 9.2 %psum.7 = f32[512]{0:T(512)S(1)} all-reduce(f32[512]{0:T(512)S(1)} %multiply_reduce_fusion), channel_id=1, replica_groups=mesh['blk'=8,'feat'=4] {'feat'}, use_global_device_ids=true, to_apply=%region_2.3 | all-reduce | flops 512 | bytes 4096 | tf_op jit(solution)/shard_map/psum | solution.py:44
  312.8 11.2 %all-gather = f32[8,1,512]{2,1,0:T(1,128)S(1)} all-gather(f32[1,1,512]{2,1,0:T(1,128)S(1)} %bitcast.19), channel_id=1, replica_groups=mesh['blk'=8,'feat'=4] {'blk'}, dimensions={0}, use_global_device_ids=true | all-gather | bytes 18432 | tf_op jit(solution)/shard_map/all_gather | solution.py:45
  324.0 62.6 %reduce-scatter.2.cloned.1.call-done = f32[512,1024]{1,0:T(8,128)} async-done(((f32[512,4096]{1,0:T(8,128)}), f32[512,1024]{1,0:T(8,128)}) %reduce-scatter.2.cloned.1.call-update) | async-done | bytes 2097168 | tf_op jit(solution)/shard_map/reduce_scatter | solution.py:43
  386.6 3.1 multiply_multiply_fusion
  (2 shorter events, 0.0 us)
Async XLA Ops:
  6.5 380.1 %reduce-scatter.2.cloned.1.call-start = ((), (), s32[]{:S(2)}) async-start(), calls=%async_computation.1 | async-start | bytes 10485760 | tf_op jit(solution)/shard_map/reduce_scatter | solution.py:43
  6.5 48.1 %collective-permute-start = (f32[512,2048]{1,0:T(8,128)}, f32[512,2048]{1,0:T(8,128)S(1)}, u32[]{:S(2)}, u32[]{:S(2)}) collective-permute-start(f32[512,2048]{1,0:T(8,128)} %param.1), channel_id=1, source_target_pairs={{0,4},{4,8},{8,12},{12,16},{16,20},{20,24},{24,28},{28,0},{1,5},{5... | collective-permute-start | bytes 12582920 | tf_op jit(solution)/shard_map/ppermute | solution.py:10
  54.7 1.9 copy-start.2
  56.6 48.0 %collective-permute-start.2 = (f32[512,2048]{1,0:T(8,128)S(1)}, f32[512,2048]{1,0:T(8,128)}, u32[]{:S(2)}, u32[]{:S(2)}) collective-permute-start(f32[512,2048]{1,0:T(8,128)S(1)} %collective-permute-done), channel_id=1, source_target_pairs={{0,4},{4,8},{8,12},{12,16},{16,20},{20,24},{24,28},{28,0},{1,5},{5... | collective-permute-start | bytes 12582920 | tf_op jit(solution)/shard_map/ppermute | solution.py:10
  104.6 59.5 %collective-permute-start.4 = (f32[512,2048]{1,0:T(8,128)}, f32[512,2048]{1,0:T(8,128)}, u32[]{:S(2)}, u32[]{:S(2)}) collective-permute-start(f32[512,2048]{1,0:T(8,128)} %collective-permute-done.2), channel_id=1, source_target_pairs={{0,4},{4,8},{8,12},{12,16},{16,20},{20,24},{24,28},{28,0},{1,5},{5... | collective-permute-start | bytes 12582920 | tf_op jit(solution)/shard_map/ppermute | solution.py:10
  104.7 2.2 copy-start
  106.8 6.9 %copy-start.3 = (f32[512,2048]{1,0:T(8,128)S(1)}, f32[512,2048]{1,0:T(8,128)}, u32[]{:S(2)}) copy-start(f32[512,2048]{1,0:T(8,128)} %copy-done.2) | copy-start | bytes 12582916
  120.9 3.2 copy-start.1
  124.1 40.0 %collective-permute-start.1 = (f32[512,512]{0,1:T(8,128)S(1)}, f32[512,512]{0,1:T(8,128)S(1)}, u32[]{:S(2)}, u32[]{:S(2)}) collective-permute-start(f32[512,512]{0,1:T(8,128)S(1)} %bitcast.15), channel_id=1, source_target_pairs={{0,28},{4,0},{8,4},{12,8},{16,12},{20,16},{24,20},{28,24},{1,29},{... | collective-permute-start | bytes 3145736 | tf_op jit(solution)/shard_map/ppermute | solution.py:10
  164.1 126.6 %collective-permute-start.6 = (f32[512,2048]{1,0:T(8,128)}, f32[512,2048]{1,0:T(8,128)}, u32[]{:S(2)}, u32[]{:S(2)}) collective-permute-start(f32[512,2048]{1,0:T(8,128)} %collective-permute-done.4), channel_id=1, source_target_pairs={{0,4},{4,8},{8,12},{12,16},{16,20},{20,24},{24,28},{28,0},{1,5},{5... | collective-permute-start | bytes 12582920 | tf_op jit(solution)/shard_map/ppermute | solution.py:10
  176.0 64.9 %collective-permute-start.3 = (f32[512,512]{0,1:T(8,128)S(1)}, f32[512,512]{0,1:T(8,128)S(1)}, u32[]{:S(2)}, u32[]{:S(2)}) collective-permute-start(f32[512,512]{0,1:T(8,128)S(1)} %bitcast.17), channel_id=1, source_target_pairs={{0,24},{4,28},{8,0},{12,4},{16,8},{20,12},{24,16},{28,20},{1,25},{... | collective-permute-start | bytes 3145736 | tf_op jit(solution)/shard_map/ppermute | solution.py:10
  252.7 36.7 %collective-permute-start.5 = (f32[512,512]{0,1:T(8,128)S(1)}, f32[512,512]{0,1:T(8,128)S(1)}, u32[]{:S(2)}, u32[]{:S(2)}) collective-permute-start(f32[512,512]{0,1:T(8,128)S(1)} %bitcast.16), channel_id=1, source_target_pairs={{0,20},{4,24},{8,28},{12,0},{16,4},{20,8},{24,12},{28,16},{1,21},{... | collective-permute-start | bytes 3145736 | tf_op jit(solution)/shard_map/ppermute | solution.py:10
Sparse Core Ops, SparseCore 0:
  301.2 85.4 reduce-scatter.1
where the time goes:
time: 399 us; the launch traced here: 397 us
  waiting for transfers between devices  293 us (73%)
  matrix products  45.1 us (11%)
  blocking collectives  20.4 us (5%)
  between operations  13.5 us (3%)
  local copies, waits for them, and re-layouts  11.5 us (3%)
  starting transfers between devices  7.52 us (2%)
  other arithmetic  5.7 us (1%)
    ppermute x7, waiting for transfers between devices, passed_along(): return lax.ppermute(value, axis, pairs)  230 us
    reduce_scatter x1, waiting for transfers between devices, local(): lax.psum_scatter(partial_value, 'feat', scatter_dimension=1, tiled=True)  62.6 us
    dot_general x5, matrix products, tile_of(): lax.dot_general(left, right, (((1,), (1,)), ((), ())), precision=lax.Prec...  45.1 us
    all_gather x1, blocking collectives, local(): every = lax.all_gather(squares, 'blk', axis=0, tiled=True)  11.2 us
    psum x1, blocking collectives, local(): squares = lax.psum(jnp.sum(grads * grads, axis=1), 'feat')  9.17 us
  transfers between devices with their start and end apart: 8, of which 6 were waited for; matrix products, arithmetic and copies ran while one was open for 11% of the time, Pallas kernels for 0%

commit v1 on v0

--- a/solution.py
+++ b/solution.py
@@ -50,8 +50,209 @@
     return gram * row_inverse[:, None] * column_inverse[None, :]
 
 
+BOTH = ("blk", "feat")
+
+
+def product(left, right):
+    return lax.dot_general(
+        left,
+        right,
+        (((1,), (1,)), ((), ())),
+        precision=lax.Precision.HIGH,
+        preferred_element_type=jnp.float32,
+    )
+
+
+def where_is(z, core, f):
+    return (2 * z + core) * 4 + f
+
+
+def mirrored(core, value):
+    return value if core == 0 else 3 - value
+
+
+def along(value, moves):
+    pairs = [
+        (2 * mirrored(core, a) + core, 2 * mirrored(core, b) + core)
+        for core in range(2)
+        for a, b in moves
+    ]
+    return lax.ppermute(value, "blk", pairs)
+
+
+def other_core(value):
+    count = lax.axis_size("blk")
+    return lax.ppermute(value, "blk", [(i, i ^ 1) for i in range(count)])
+
+
+def partner(value, bit):
+    return lax.ppermute(value, "feat", [(f, f ^ bit) for f in range(4)])
+
+
+def onto(value, targets, bit_order):
+    first, second = bit_order
+    pairs = [
+        (where_is(z, c, f), where_is(z, c, f ^ first))
+        for z, t in targets.items()
+        for c in range(2)
+        for f in range(4)
+        if (f ^ t) & first
+    ]
+    value = value + lax.ppermute(value, BOTH, pairs)
+    pairs = [
+        (where_is(z, c, t ^ second), where_is(z, c, t))
+        for z, t in targets.items()
+        for c in range(2)
+    ]
+    return value + lax.ppermute(value, BOTH, pairs)
+
+
+def rows_to_target(block, core, targets):
+    rows = block.shape[0] // 2
+    halves = block.reshape(2, rows, block.shape[1])
+    mine = lax.dynamic_index_in_dim(halves, core, 0, False)
+    give = lax.dynamic_index_in_dim(halves, 1 - core, 0, False)
+    mine = mine + other_core(give)
+    width = mine.shape[1] // 2
+    return jnp.concatenate(
+        [onto(mine[:, :width], targets, (1, 2)), onto(mine[:, width:], targets, (2, 1))],
+        axis=1,
+    )
+
+
+PIECES = {
+    (0, 0): (2, 0), (1, 0): (3, 1), (2, 0): (2, 1), (3, 0): (3, 0),
+    (0, 1): (3, 0), (1, 1): (2, 1), (2, 1): (2, 0), (3, 1): (3, 1),
+}
+
+
+def meeting(near_or_far, core, g, k, half):
+    a, b = PIECES[g, k]
+    source = where_is(mirrored(core, 2), core, mirrored(core, g))
+    za, zb = mirrored(core, a), mirrored(core, b)
+    if near_or_far == "near":
+        return (source, where_is(za, half, zb))
+    return (source, where_is(zb, g // 2, za))
+
+
+def scattered(blocks, row_half, g):
+    rows = blocks[2, 0].shape[0] // 2
+    width = blocks[2, 0].shape[1] // 2
+
+    def piece(gg, k):
+        a, b = PIECES[gg, k]
+        h = gg // 2
+        return blocks[a, b][row_half * rows : (row_half + 1) * rows, h * width : (h + 1) * width]
+
+    gy, gx = g // 2, g % 2
+    if row_half == 0:
+        stack = jnp.stack(
+            [jnp.stack([jnp.stack([piece(2 * y + x, k) for k in range(2)]) for x in range(2)]) for y in range(2)]
+        )
+        first, second, bits = gy, gx, (2, 1)
+    else:
+        stack = jnp.stack(
+            [jnp.stack([jnp.stack([piece(2 * y + x, k) for k in range(2)]) for y in range(2)]) for x in range(2)]
+        )
+        first, second, bits = gx, gy, (1, 2)
+    got = partner(lax.dynamic_index_in_dim(stack, 1 - first, 0, False), bits[0])
+    kept = lax.dynamic_index_in_dim(stack, first, 0, False) + got
+    got = partner(lax.dynamic_index_in_dim(kept, 1 - second, 0, False), bits[1])
+    return lax.dynamic_index_in_dim(kept, second, 0, False) + got
+
+
+def met(grads):
+    rows, depth = grads.shape
+    mine, f = lax.axis_index("blk"), lax.axis_index("feat")
+    core, z = mine % 2, mine // 2
+    position = jnp.where(core == 0, z, 3 - z)
+    g = jnp.where(core == 0, f, 3 - f)
+
+    total = lax.axis_size("blk") * rows
+    squares = jnp.sum(grads * grads, axis=1)
+    every = lax.dynamic_update_slice_in_dim(
+        jnp.zeros((total,), jnp.float32), squares, mine * rows, 0
+    )
+    every = lax.psum(every, BOTH)
+
+    half = depth // 2
+    kept = lax.dynamic_slice_in_dim(grads, core * half, half, 1)
+    got = other_core(lax.dynamic_slice_in_dim(grads, (1 - core) * half, half, 1))
+    own = jnp.where(
+        core == 0, jnp.concatenate([kept, got], 0), jnp.concatenate([got, kept], 0)
+    )
+
+    one = along(own, [(0, 1), (1, 2)])
+    own_later, one = lax.optimization_barrier((own, one))
+    zero = along(one, [(1, 2)])
+    three = along(own_later, [(3, 2)])
+
+    diagonal = product(own, own)
+    diagonal = rows_to_target(diagonal, core, {z_: z_ for z_ in range(4)})
+    b21 = product(own, one)
+    b23 = product(own, three)
+    inner = jnp.where(position == 1, b21, b23)
+    inner = rows_to_target(inner, core, {1: 0, 2: 3})
+
+    blocks = {
+        (2, 1): b21,
+        (3, 1): product(three, one),
+        (2, 0): product(own, zero),
+        (3, 0): product(three, zero),
+    }
+    upper = scattered(blocks, 0, g)
+    lower = scattered(blocks, 1, g)
+
+    cross = None
+    for k in range(2):
+        far = jnp.concatenate([upper[k].T, lower[k].T], axis=1)
+        pairs = [meeting("far", c, gg, k, 0) for c in range(2) for gg in range(4)]
+        far = lax.ppermute(far, BOTH, pairs)
+        cross = far if cross is None else cross + far
+    near = []
+    for k in range(2):
+        parts = []
+        for h, value in enumerate((upper, lower)):
+            pairs = [meeting("near", c, gg, k, h) for c in range(2) for gg in range(4)]
+            parts.append(lax.ppermute(value[k], BOTH, pairs))
+        near.append(parts[0] + parts[1])
+    straight = (z - f) * (z - f) == 4
+    left = jnp.where(straight, near[0], near[1])
+    right = jnp.where(straight, near[1], near[0])
+    cross = cross + jnp.concatenate([left, right], axis=1)
+
+    width = inner.shape[1] // 2
+    column_halves = jnp.stack([inner[:, :width].T, inner[:, width:].T])
+    ends = [((1, 0), (0, 1)), ((2, 3), (3, 2))]
+    same = lax.ppermute(
+        lax.dynamic_index_in_dim(column_halves, core, 0, False),
+        BOTH,
+        [(where_is(a, c, b), where_is(p, c, q)) for (a, b), (p, q) in ends for c in range(2)],
+    )
+    swapped = lax.ppermute(
+        lax.dynamic_index_in_dim(column_halves, 1 - core, 0, False),
+        BOTH,
+        [(where_is(a, c, b), where_is(p, 1 - c, q)) for (a, b), (p, q) in ends for c in range(2)],
+    )
+    outer = jnp.concatenate(
+        [jnp.where(core == 0, same, swapped), jnp.where(core == 0, swapped, same)], axis=1
+    )
+
+    is_inner = ((z == 1) & (f == 0)) | ((z == 2) & (f == 3))
+    is_outer = ((z == 0) & (f == 1)) | ((z == 3) & (f == 2))
+    gram = jnp.where(z == f, diagonal, jnp.where(is_inner, inner, jnp.where(is_outer, outer, cross)))
+
+    columns = gram.shape[1]
+    row_sq = lax.dynamic_slice_in_dim(every, mine * rows, rows)
+    column_sq = lax.dynamic_slice_in_dim(every, f * columns, columns)
+    row_inverse = 1.0 / jnp.sqrt(row_sq + 1e-06)
+    column_inverse = 1.0 / jnp.sqrt(column_sq + 1e-06)
+    return gram * row_inverse[:, None] * column_inverse[None, :]
+
+
 def solution(mesh):
     placed = (P("blk", "feat"),)
+    body = met if (mesh.shape["blk"], mesh.shape["feat"]) == (8, 4) else local
     return jax.shard_map(
-        local, mesh=mesh, in_specs=placed, out_specs=P("blk", "feat"), check_vma=False
-    )
+        body, mesh=mesh, in_specs=placed, out_specs=P("blk", "feat"), check_vma=False
+    )

time: 399 us -> 566 us (1.42)
  the two profiles are of different devices: /device:TPU:12 before, /device:TPU:0 now
where the time goes in v1:
time: 566 us; the launch traced here: 555 us
  blocking collectives  208 us (37%)
  waiting for transfers between devices  125 us (22%)
  other arithmetic  65.4 us (12%)
  matrix products  64.3 us (11%)
  starting transfers between devices  62.1 us (11%)
  local copies, waits for them, and re-layouts  30.6 us (5%)
    psum x1, blocking collectives, met(): every = lax.psum(every, BOTH)  208 us
    dot_general x6, matrix products, product(): lax.dot_general(left, right, (((1,), (1,)), ((), ())), precision=lax.Prec...  64.3 us
    ppermute x4, waiting for transfers between devices, partner(): return lax.ppermute(value, 'feat', [(f, f ^ bit) for f in range(4)])  57.1 us
    ppermute x3, waiting for transfers between devices, along(): return lax.ppermute(value, 'blk', pairs)  44.4 us
    ppermute x3, starting transfers between devices, other_core(): return lax.ppermute(value, 'blk', [(i, i ^ 1) for i in range(count)])  19.7 us
    ppermute x3, starting transfers between devices, along(): return lax.ppermute(value, 'blk', pairs)  12.1 us
  transfers between devices with their start and end apart: 26, of which 7 were waited for; matrix products, arithmetic and copies ran while one was open for 24% of the time, Pallas kernels for 0%

profile of v1, /device:TPU:0, one launch (start us, length us, event | category | flops | bytes accessed | tf_op | source)
XLA Modules:
  0.0 555.5 jit_solution(8369050109570315443)
XLA Ops:
  0.0 4.0 constant_dynamic-slice_fusion.1
  4.4 4.1 collective-permute-done
  8.6 5.3 maximum_select_fusion
  13.8 6.8 %collective-permute-start.6 = (f32[1024,1024]{1,0:T(8,128)}, f32[1024,1024]{1,0:T(8,128)}, u32[]{:S(2)}, u32[]{:S(2)}) collective-permute-start(f32[1024,1024]{1,0:T(8,128)} %maximum_select_fusion), channel_id=1, source_target_pairs={{0,8},{8,16},{28,20},{20,12},{1,9},{9,17},{29,21},{21,13},{2,10},{... | collective-permute-start | bytes 12582920 | tf_op jit(solution)/shard_map/ppermute | solution.py:80
  20.7 44.4 %collective-permute-done.6 = f32[1024,1024]{1,0:T(8,128)} collective-permute-done((f32[1024,1024]{1,0:T(8,128)}, f32[1024,1024]{1,0:T(8,128)}, u32[]{:S(2)}, u32[]{:S(2)}) %collective-permute-start.6) | collective-permute-done | bytes 4194336 | tf_op jit(solution)/shard_map/ppermute | solution.py:80
  65.0 2.6 collective-permute-start.7
  67.7 2.7 collective-permute-start.15
  70.3 11.1 %fusion.16 = f32[1024,1024]{1,0:T(8,128)S(1)} fusion(f32[1024,1024]{1,0:T(8,128)} %maximum_select_fusion), kind=kOutput, calls=%fused_computation.93 | convolution fusion | flops 6442450944 | bytes 8388608 | tf_op jit(solution)/shard_map/dot_general | solution.py:57
  81.5 1.8 dynamic-slice_bitcast_fusion.3
  83.2 2.7 collective-permute-start.1
  86.0 10.5 %fusion.17 = f32[1024,1024]{1,0:T(8,128)S(1)} fusion(f32[1024,1024]{1,0:T(8,128)} %maximum_select_fusion, f32[1024,1024]{1,0:T(8,128)} %collective-permute-done.6), kind=kOutput, calls=%fused_computation.94 | convolution fusion | flops 6442450944 | bytes 12582912 | tf_op jit(solution)/shard_map/dot_general | solution.py:57
  97.1 10.5 %fusion.19 = f32[1024,1024]{1,0:T(8,128)S(1)} fusion(f32[1024,1024]{1,0:T(8,128)} %collective-permute-done.7, f32[1024,1024]{1,0:T(8,128)} %collective-permute-done.15), kind=kOutput, calls=%fused_computation.96 | convolution fusion | flops 6442450944 | bytes 12582912 | tf_op jit(solution)/shard_map/dot_general | solution.py:57
  108.0 10.7 %fusion.18 = f32[1024,1024]{1,0:T(8,128)S(1)} fusion(f32[1024,1024]{1,0:T(8,128)} %maximum_select_fusion, f32[1024,1024]{1,0:T(8,128)} %collective-permute-done.15), kind=kOutput, calls=%fused_computation.95 | convolution fusion | flops 6442450944 | bytes 12582912 | tf_op jit(solution)/shard_map/dot_general | solution.py:57
  119.1 10.9 %fusion.20 = f32[1024,1024]{1,0:T(8,128)S(1)} fusion(f32[1024,1024]{1,0:T(8,128)} %collective-permute-done.7, f32[1024,1024]{1,0:T(8,128)} %collective-permute-done.6), kind=kOutput, calls=%fused_computation.97 | convolution fusion | flops 6442450944 | bytes 12582912 | tf_op jit(solution)/shard_map/dot_general | solution.py:57
  133.7 3.2 fusion.6
  137.0 1.5 collective-permute-start.16
  139.9 1.5 copy-done.4
  141.4 3.3 fusion.1
  144.6 1.5 collective-permute-start.18
  146.1 10.7 %broadcast_select_fusion = f32[1024,1024]{1,0:T(8,128)S(1)} fusion(f32[1024,1024]{1,0:T(8,128)S(1)} %fusion.17, pred[]{:T(512)S(6)} %eq.50, f32[1024,1024]{1,0:T(8,128)} %maximum_select_fusion, f32[1024,1024]{1,0:T(8,128)} %collective-permute-done.7), kind=kOutput, calls=%fused_computation.52 | convolution fusion | flops 6443499520 | bytes 16777216 | tf_op jit(solution)/shard_map/dot_general | solution.py:57
  156.9 2.1 copy-done.11
  159.0 1.5 dynamic-slice_bitcast_fusion.2
  160.5 16.5 %collective-permute-start.8 = (f32[512,1024]{1,0:T(8,128)}, f32[512,1024]{1,0:T(8,128)}, u32[]{:S(2)}, u32[]{:S(2)}) collective-permute-start(f32[512,1024]{1,0:T(8,128)} %dynamic-slice_bitcast_fusion.2), channel_id=1, source_target_pairs={{0,4},{4,0},{8,12},{12,8},{16,20},{20,16},{24,28},{28,24},{1,5},{5... | collective-permute-start | bytes 6291464 | tf_op jit(solution)/shard_map/ppermute | solution.py:85
  177.0 2.1 bitcast_add_fusion.3
  181.9 1.7 collective-permute-start.4
  183.6 2.7 bitcast_add_fusion.2
  186.3 1.6 fusion.14
  187.9 1.6 collective-permute-start.9
  189.5 25.1 %collective-permute-done.16 = f32[2,2,512,512]{3,2,1,0:T(8,128)} collective-permute-done((f32[2,2,512,512]{3,2,1,0:T(8,128)}, f32[2,2,512,512]{3,2,1,0:T(8,128)}, u32[]{:S(2)}, u32[]{:S(2)}) %collective-permute-start.16) | collective-permute-done | bytes 4194336 | tf_op jit(solution)/shard_map/ppermute | solution.py:89
  214.6 1.6 collective-permute-start.11
  216.2 3.9 fusion.9
  220.2 1.5 dynamic-slice_bitcast_fusion.1
  224.5 3.8 fusion.4
  228.3 1.6 dynamic-slice_bitcast_fusion
  230.0 1.5 collective-permute-start.19
  231.5 2.0 slice_add_fusion.1
  234.3 10.6 %collective-permute-done.2 = f32[512,512]{1,0:T(8,128)S(1)} collective-permute-done((f32[512,512]{1,0:T(8,128)}, f32[512,512]{1,0:T(8,128)S(1)}, u32[]{:S(2)}, u32[]{:S(2)}) %collective-permute-start.2) | collective-permute-done | bytes 1048608 | tf_op jit(solution)/shard_map/ppermute | solution.py:101
  245.6 3.1 slice_add_fusion.3
  251.8 1.5 fusion.13
  253.3 2.6 copy.2
  255.8 1.6 collective-permute-start.13
  258.8 31.2 %collective-permute-done.17 = f32[2,512,512]{2,1,0:T(8,128)} collective-permute-done((f32[2,512,512]{2,1,0:T(8,128)}, f32[2,512,512]{2,1,0:T(8,128)}, u32[]{:S(2)}, u32[]{:S(2)}) %collective-permute-start.17) | collective-permute-done | bytes 2097184 | tf_op jit(solution)/shard_map/ppermute | solution.py:89
  289.9 1.6 collective-permute-start.14
  291.6 2.7 bitcast_add_fusion.1
  295.8 1.7 collective-permute-start.24
  297.5 2.1 bitcast_add_fusion
  299.6 1.6 slice_bitcast_fusion.21
  301.2 1.5 pad_maximum_fusion
  302.6 1.5 pad_maximum_fusion.1
  304.2 8.3 %collective-permute-done.5 = f32[512,512]{1,0:T(8,128)} collective-permute-done((f32[512,512]{1,0:T(8,128)}, f32[512,512]{1,0:T(8,128)}, u32[]{:S(2)}, u32[]{:S(2)}) %collective-permute-start.5) | collective-permute-done | bytes 1048608 | tf_op jit(solution)/shard_map/ppermute | solution.py:107
  312.4 2.0 collective-permute-start.20
  314.4 2.0 collective-permute-start.21
  316.4 1.7 collective-permute-start.25
  318.1 1.7 collective-permute-start.22
  319.8 1.6 collective-permute-start.23
  321.4 2.5 multiply_reduce_fusion
  324.2 207.9 %psum.7 = f32[4096]{0:T(1024)S(1)} all-reduce(f32[4096]{0:T(1024)S(1)} %dynamic_update_slice.3), channel_id=1, replica_groups=mesh['blk'=8,'feat'=4] {'blk','feat'}, use_global_device_ids=true, to_apply=%region_1.2 | all-reduce | flops 4096 | bytes 32768 | tf_op jit(solution)/shard_map/psum | solution.py:176
  532.2 1.8 add.133
  533.9 2.8 add.131
  536.7 3.1 broadcast_select_fusion.4
  539.9 4.1 broadcast_select_fusion.2
  544.0 4.0 add.148
  548.0 2.9 copy.4
  550.9 4.4 fusion.11
  (74 shorter events, 20.3 us)
Async XLA Ops:
  4.0 4.6 collective-permute-start
  13.8 51.2 %collective-permute-start.6 = (f32[1024,1024]{1,0:T(8,128)}, f32[1024,1024]{1,0:T(8,128)}, u32[]{:S(2)}, u32[]{:S(2)}) collective-permute-start(f32[1024,1024]{1,0:T(8,128)} %maximum_select_fusion), channel_id=1, source_target_pairs={{0,8},{8,16},{28,20},{20,12},{1,9},{9,17},{29,21},{21,13},{2,10},{... | collective-permute-start | bytes 12582920 | tf_op jit(solution)/shard_map/ppermute | solution.py:80
  65.0 32.0 %collective-permute-start.7 = (f32[1024,1024]{1,0:T(8,128)}, f32[1024,1024]{1,0:T(8,128)}, u32[]{:S(2)}, u32[]{:S(2)}) collective-permute-start(f32[1024,1024]{1,0:T(8,128)} %maximum_select_fusion), channel_id=1, source_target_pairs={{24,16},{4,12},{25,17},{5,13},{26,18},{6,14},{27,19},{7,15}} | collective-permute-start | bytes 12582920 | tf_op jit(solution)/shard_map/ppermute | solution.py:80
  67.7 29.4 %collective-permute-start.15 = (f32[1024,1024]{1,0:T(8,128)}, f32[1024,1024]{1,0:T(8,128)}, u32[]{:S(2)}, u32[]{:S(2)}) collective-permute-start(f32[1024,1024]{1,0:T(8,128)} %collective-permute-done.6), channel_id=1, source_target_pairs={{8,16},{20,12},{9,17},{21,13},{10,18},{22,14},{11,19},{23,15}} | collective-permute-start | bytes 12582920 | tf_op jit(solution)/shard_map/ppermute | solution.py:80
  81.5 15.0 %copy-start.13 = (f32[1024,1024]{1,0:T(8,128)}, f32[1024,1024]{1,0:T(8,128)S(1)}, u32[]{:S(2)}) copy-start(f32[1024,1024]{1,0:T(8,128)S(1)} %fusion.16) | copy-start | bytes 12582916
  83.2 93.7 %collective-permute-start.1 = (f32[512,1024]{1,0:T(8,128)}, f32[512,1024]{1,0:T(8,128)S(1)}, u32[]{:S(2)}, u32[]{:S(2)}) collective-permute-start(f32[512,1024]{1,0:T(8,128)} %dynamic-slice_bitcast_fusion.3), channel_id=1, source_target_pairs={{0,4},{4,0},{8,12},{12,8},{16,20},{20,16},{24,28},{28,24},{1,5},{5... | collective-permute-start | bytes 6291464 | tf_op jit(solution)/shard_map/ppermute | solution.py:85
  131.8 1.9 copy-start
  133.7 3.3 copy-start.2
  137.0 77.6 %collective-permute-start.16 = (f32[2,2,512,512]{3,2,1,0:T(8,128)}, f32[2,2,512,512]{3,2,1,0:T(8,128)}, u32[]{:S(2)}, u32[]{:S(2)}) collective-permute-start(f32[2,2,512,512]{3,2,1,0:T(8,128)} %fusion.6), channel_id=1, source_target_pairs={{0,2},{1,3},{2,0},{3,1},{4,6},{5,7},{6,4},{7,5},{8,10},{9,11},{10,... | collective-permute-start | bytes 12582920 | tf_op jit(solution)/shard_map/ppermute | solution.py:89
  139.4 2.0 copy-start.4
  141.4 3.3 copy-start.6
  144.6 77.9 %collective-permute-start.18 = (f32[2,2,512,512]{3,2,1,0:T(8,128)}, f32[2,2,512,512]{3,2,1,0:T(8,128)}, u32[]{:S(2)}, u32[]{:S(2)}) collective-permute-start(f32[2,2,512,512]{3,2,1,0:T(8,128)} %fusion.1), channel_id=1, source_target_pairs={{0,1},{1,0},{2,3},{3,2},{4,5},{5,4},{6,7},{7,6},{8,9},{9,8},{10,11... | collective-permute-start | bytes 12582920 | tf_op jit(solution)/shard_map/ppermute | solution.py:89
  156.9 2.1 copy-start.11
  160.5 23.2 %collective-permute-start.8 = (f32[512,1024]{1,0:T(8,128)}, f32[512,1024]{1,0:T(8,128)}, u32[]{:S(2)}, u32[]{:S(2)}) collective-permute-start(f32[512,1024]{1,0:T(8,128)} %dynamic-slice_bitcast_fusion.2), channel_id=1, source_target_pairs={{0,4},{4,0},{8,12},{12,8},{16,20},{20,16},{24,28},{28,24},{1,5},{5... | collective-permute-start | bytes 6291464 | tf_op jit(solution)/shard_map/ppermute | solution.py:85
  177.0 6.7 %copy-start.12 = (f32[1024,1024]{1,0:T(8,128)S(1)}, f32[1024,1024]{1,0:T(8,128)}, u32[]{:S(2)}) copy-start(f32[1024,1024]{1,0:T(8,128)} %copy-done.11) | copy-start | bytes 12582916
  180.6 64.3 %collective-permute-start.2 = (f32[512,512]{1,0:T(8,128)}, f32[512,512]{1,0:T(8,128)S(1)}, u32[]{:S(2)}, u32[]{:S(2)}) collective-permute-start(f32[512,512]{1,0:T(8,128)} %get-tuple-element.47), channel_id=1, source_target_pairs={{1,0},{3,2},{5,4},{7,6},{8,9},{10,11},{12,13},{14,15},{17,16},{19,... | collective-permute-start | bytes 3145736 | tf_op jit(solution)/shard_map/ppermute | solution.py:101
  181.9 34.3 %copy-start.1 = (f32[1,2,2,512,512]{4,3,2,1,0:T(8,128)S(1)}, f32[1,2,2,512,512]{4,3,2,1,0:T(8,128)}, u32[]{:S(2)}) copy-start(f32[1,2,2,512,512]{4,3,2,1,0:T(8,128)} %copy-done) | copy-start | bytes 12582916
  181.9 34.3 %copy-start.3 = (f32[1,2,2,512,512]{4,3,2,1,0:T(8,128)S(1)}, f32[1,2,2,512,512]{4,3,2,1,0:T(8,128)}, u32[]{:S(2)}) copy-start(f32[1,2,2,512,512]{4,3,2,1,0:T(8,128)} %copy-done.2) | copy-start | bytes 12582916
  181.9 63.7 %collective-permute-start.4 = (f32[512,512]{1,0:T(8,128)}, f32[512,512]{1,0:T(8,128)}, u32[]{:S(2)}, u32[]{:S(2)}) collective-permute-start(f32[512,512]{1,0:T(8,128)} %get-tuple-element.48), channel_id=1, source_target_pairs={{2,0},{3,1},{6,4},{7,5},{10,8},{11,9},{14,12},{15,13},{16,18},{17,... | collective-permute-start | bytes 3145736 | tf_op jit(solution)/shard_map/ppermute | solution.py:101
  187.9 42.1 %collective-permute-start.9 = (f32[512,512]{1,0:T(8,128)}, f32[512,512]{1,0:T(8,128)}, u32[]{:S(2)}, u32[]{:S(2)}) collective-permute-start(f32[512,512]{1,0:T(8,128)} %get-tuple-element.43), channel_id=1, source_target_pairs={{9,8},{11,10},{13,12},{15,14},{16,17},{18,19},{20,21},{22,23}} | collective-permute-start | bytes 3145736 | tf_op jit(solution)/shard_map/ppermute | solution.py:101
  214.6 16.9 %collective-permute-start.11 = (f32[512,512]{1,0:T(8,128)}, f32[512,512]{1,0:T(8,128)}, u32[]{:S(2)}, u32[]{:S(2)}) collective-permute-start(f32[512,512]{1,0:T(8,128)} %get-tuple-element.44), channel_id=1, source_target_pairs={{10,8},{11,9},{14,12},{15,13},{16,18},{17,19},{20,22},{21,23}} | collective-permute-start | bytes 3145736 | tf_op jit(solution)/shard_map/ppermute | solution.py:101
  216.2 7.8 %copy-start.7 = (f32[1,2,2,512,512]{4,3,2,1,0:T(8,128)S(1)}, f32[1,2,2,512,512]{4,3,2,1,0:T(8,128)}, u32[]{:S(2)}) copy-start(f32[1,2,2,512,512]{4,3,2,1,0:T(8,128)} %copy-done.6) | copy-start | bytes 12582916
  220.1 8.2 %copy-start.10 = (f32[2,2,512,512]{3,2,1,0:T(8,128)}, f32[2,2,512,512]{3,2,1,0:T(8,128)S(1)}, u32[]{:S(2)}) copy-start(f32[2,2,512,512]{3,2,1,0:T(8,128)S(1)} %fusion.9) | copy-start | bytes 12582916
  220.1 4.4 copy-start.5
  222.5 67.4 %collective-permute-start.17 = (f32[2,512,512]{2,1,0:T(8,128)}, f32[2,512,512]{2,1,0:T(8,128)}, u32[]{:S(2)}, u32[]{:S(2)}) collective-permute-start(f32[2,512,512]{2,1,0:T(8,128)} %dynamic-slice_bitcast_fusion.1), channel_id=1, source_target_pairs={{0,1},{1,0},{2,3},{3,2},{4,5},{5,4},{6,7},{7,6},{8,9},{9,8},{10,11... | collective-permute-start | bytes 6291464 | tf_op jit(solution)/shard_map/ppermute | solution.py:89
  228.3 5.2 copy-start.8
  230.0 65.8 %collective-permute-start.19 = (f32[2,512,512]{2,1,0:T(8,128)}, f32[2,512,512]{2,1,0:T(8,128)}, u32[]{:S(2)}, u32[]{:S(2)}) collective-permute-start(f32[2,512,512]{2,1,0:T(8,128)} %dynamic-slice_bitcast_fusion), channel_id=1, source_target_pairs={{0,2},{1,3},{2,0},{3,1},{4,6},{5,7},{6,4},{7,5},{8,10},{9,11},{10,... | collective-permute-start | bytes 6291464 | tf_op jit(solution)/shard_map/ppermute | solution.py:89
  233.5 16.5 %collective-permute-start.12 = (f32[512,512]{1,0:T(8,128)S(1)}, f32[512,512]{1,0:T(8,128)S(1)}, u32[]{:S(2)}, u32[]{:S(2)}) collective-permute-start(f32[512,512]{1,0:T(8,128)S(1)} %get-tuple-element.42), channel_id=1, source_target_pairs={{9,8},{13,12},{18,19},{22,23}} | collective-permute-start | bytes 3145736 | tf_op jit(solution)/shard_map/ppermute | solution.py:107
  244.9 6.7 %collective-permute-start.10 = (f32[512,512]{1,0:T(8,128)S(1)}, f32[512,512]{1,0:T(8,128)S(1)}, u32[]{:S(2)}, u32[]{:S(2)}) collective-permute-start(f32[512,512]{1,0:T(8,128)S(1)} %get-tuple-element.41), channel_id=1, source_target_pairs={{10,8},{14,12},{17,19},{21,23}} | collective-permute-start | bytes 3145736 | tf_op jit(solution)/shard_map/ppermute | solution.py:107
  248.7 63.7 %collective-permute-start.5 = (f32[512,512]{1,0:T(8,128)}, f32[512,512]{1,0:T(8,128)}, u32[]{:S(2)}, u32[]{:S(2)}) collective-permute-start(f32[512,512]{1,0:T(8,128)} %get-tuple-element.46), channel_id=1, source_target_pairs={{1,0},{5,4},{8,9},{12,13},{19,18},{23,22},{26,27},{30,31}} | collective-permute-start | bytes 3145736 | tf_op jit(solution)/shard_map/ppermute | solution.py:107
  250.0 64.4 %collective-permute-start.3 = (f32[512,512]{1,0:T(8,128)}, f32[512,512]{1,0:T(8,128)}, u32[]{:S(2)}, u32[]{:S(2)}) collective-permute-start(f32[512,512]{1,0:T(8,128)} %get-tuple-element.45), channel_id=1, source_target_pairs={{2,0},{6,4},{11,9},{15,13},{16,18},{20,22},{25,27},{29,31}} | collective-permute-start | bytes 3145736 | tf_op jit(solution)/shard_map/ppermute | solution.py:107
  255.8 60.6 %collective-permute-start.13 = (f32[512,512]{1,0:T(8,128)}, f32[512,512]{1,0:T(8,128)}, u32[]{:S(2)}, u32[]{:S(2)}) collective-permute-start(f32[512,512]{1,0:T(8,128)} %bitcast.133), channel_id=1, source_target_pairs={{8,1},{12,5},{19,26},{23,30}} | collective-permute-start | bytes 3145736 | tf_op jit(solution)/shard_map/ppermute | solution.py:227
  289.9 28.1 %collective-permute-start.14 = (f32[512,512]{1,0:T(8,128)}, f32[512,512]{1,0:T(8,128)}, u32[]{:S(2)}, u32[]{:S(2)}) collective-permute-start(f32[512,512]{1,0:T(8,128)} %bitcast.132), channel_id=1, source_target_pairs={{8,5},{12,1},{19,30},{23,26}} | collective-permute-start | bytes 3145736 | tf_op jit(solution)/shard_map/ppermute | solution.py:232
  294.3 3.2 copy-start.9
  295.8 24.0 %collective-permute-start.24 = (f32[512,512]{1,0:T(8,128)S(1)}, f32[512,512]{1,0:T(8,128)}, u32[]{:S(2)}, u32[]{:S(2)}) collective-permute-start(f32[512,512]{1,0:T(8,128)S(1)} %get-tuple-element.36), channel_id=1, source_target_pairs={{16,24},{17,17},{18,16},{19,25},{15,3},{14,10},{13,11},{12,2}} | collective-permute-start | bytes 3145736 | tf_op jit(solution)/shard_map/ppermute | solution.py:217
  312.4 231.5 %collective-permute-start.20 = (f32[512,1024]{0,1:T(8,128)}, f32[512,1024]{0,1:T(8,128)}, u32[]{:S(2)}, u32[]{:S(2)}) collective-permute-start(f32[512,1024]{0,1:T(8,128)} %pad_maximum_fusion), channel_id=1, source_target_pairs={{16,2},{17,11},{18,14},{19,7},{15,25},{14,16},{13,21},{12,28}} | collective-permute-start | bytes 6291464 | tf_op jit(solution)/shard_map/ppermute | solution.py:210
  314.4 229.5 %collective-permute-start.21 = (f32[512,1024]{0,1:T(8,128)}, f32[512,1024]{0,1:T(8,128)}, u32[]{:S(2)}, u32[]{:S(2)}) collective-permute-start(f32[512,1024]{0,1:T(8,128)} %pad_maximum_fusion.1), channel_id=1, source_target_pairs={{16,3},{17,10},{18,6},{19,15},{15,24},{14,17},{13,29},{12,20}} | collective-permute-start | bytes 6291464 | tf_op jit(solution)/shard_map/ppermute | solution.py:210
  316.4 223.4 %collective-permute-start.25 = (f32[512,512]{1,0:T(8,128)}, f32[512,512]{1,0:T(8,128)}, u32[]{:S(2)}, u32[]{:S(2)}) collective-permute-start(f32[512,512]{1,0:T(8,128)} %get-tuple-element.32), channel_id=1, source_target_pairs={{16,28},{17,21},{18,20},{19,29},{15,7},{14,14},{13,15},{12,6}} | collective-permute-start | bytes 3145736 | tf_op jit(solution)/shard_map/ppermute | solution.py:217
  318.1 221.8 %collective-permute-start.22 = (f32[512,512]{1,0:T(8,128)}, f32[512,512]{1,0:T(8,128)}, u32[]{:S(2)}, u32[]{:S(2)}) collective-permute-start(f32[512,512]{1,0:T(8,128)} %get-tuple-element.33), channel_id=1, source_target_pairs={{16,16},{17,25},{18,17},{19,24},{15,11},{14,2},{13,10},{12,3}} | collective-permute-start | bytes 3145736 | tf_op jit(solution)/shard_map/ppermute | solution.py:217
  319.8 220.1 %collective-permute-start.23 = (f32[512,512]{1,0:T(8,128)}, f32[512,512]{1,0:T(8,128)}, u32[]{:S(2)}, u32[]{:S(2)}) collective-permute-start(f32[512,512]{1,0:T(8,128)} %get-tuple-element.29), channel_id=1, source_target_pairs={{16,20},{17,29},{18,21},{19,28},{15,15},{14,6},{13,14},{12,7}} | collective-permute-start | bytes 3145736 | tf_op jit(solution)/shard_map/ppermute | solution.py:217

commit v2 on v1

--- a/solution.py
+++ b/solution.py
@@ -89,34 +89,43 @@
     return lax.ppermute(value, "feat", [(f, f ^ bit) for f in range(4)])
 
 
-def onto(value, targets, bit_order):
-    first, second = bit_order
+def first_sum(value, targets, bit):
     pairs = [
-        (where_is(z, c, f), where_is(z, c, f ^ first))
+        (where_is(z, c, f), where_is(z, c, f ^ bit))
         for z, t in targets.items()
         for c in range(2)
         for f in range(4)
-        if (f ^ t) & first
+        if (f ^ t) & bit
     ]
-    value = value + lax.ppermute(value, BOTH, pairs)
+    return value + lax.ppermute(value, BOTH, pairs)
+
+
+def second_sum(value, targets, bit):
     pairs = [
-        (where_is(z, c, t ^ second), where_is(z, c, t))
+        (where_is(z, c, t ^ bit), where_is(z, c, t))
         for z, t in targets.items()
         for c in range(2)
     ]
     return value + lax.ppermute(value, BOTH, pairs)
 
 
-def rows_to_target(block, core, targets):
+def own_rows(block, core):
     rows = block.shape[0] // 2
     halves = block.reshape(2, rows, block.shape[1])
     mine = lax.dynamic_index_in_dim(halves, core, 0, False)
     give = lax.dynamic_index_in_dim(halves, 1 - core, 0, False)
     mine = mine + other_core(give)
     width = mine.shape[1] // 2
+    return mine[:, :width], mine[:, width:]
+
+
+def first_sums(pair, targets):
+    return first_sum(pair[0], targets, 1), first_sum(pair[1], targets, 2)
+
+
+def second_sums(pair, targets):
     return jnp.concatenate(
-        [onto(mine[:, :width], targets, (1, 2)), onto(mine[:, width:], targets, (2, 1))],
-        axis=1,
+        [second_sum(pair[0], targets, 2), second_sum(pair[1], targets, 1)], axis=1
     )
 
 
@@ -149,15 +158,19 @@
         stack = jnp.stack(
             [jnp.stack([jnp.stack([piece(2 * y + x, k) for k in range(2)]) for x in range(2)]) for y in range(2)]
         )
-        first, second, bits = gy, gx, (2, 1)
+        first, bits = gy, (2, 1)
     else:
         stack = jnp.stack(
             [jnp.stack([jnp.stack([piece(2 * y + x, k) for k in range(2)]) for y in range(2)]) for x in range(2)]
         )
-        first, second, bits = gx, gy, (1, 2)
+        first, bits = gx, (1, 2)
     got = partner(lax.dynamic_index_in_dim(stack, 1 - first, 0, False), bits[0])
-    kept = lax.dynamic_index_in_dim(stack, first, 0, False) + got
-    got = partner(lax.dynamic_index_in_dim(kept, 1 - second, 0, False), bits[1])
+    return lax.dynamic_index_in_dim(stack, first, 0, False) + got
+
+
+def scattered_on(kept, row_half, g):
+    second, bit = (g % 2, 1) if row_half == 0 else (g // 2, 2)
+    got = partner(lax.dynamic_index_in_dim(kept, 1 - second, 0, False), bit)
     return lax.dynamic_index_in_dim(kept, second, 0, False) + got
 
 
@@ -173,7 +186,6 @@
     every = lax.dynamic_update_slice_in_dim(
         jnp.zeros((total,), jnp.float32), squares, mine * rows, 0
     )
-    every = lax.psum(every, BOTH)
 
     half = depth // 2
     kept = lax.dynamic_slice_in_dim(grads, core * half, half, 1)
@@ -183,16 +195,15 @@
     )
 
     one = along(own, [(0, 1), (1, 2)])
-    own_later, one = lax.optimization_barrier((own, one))
+    every = lax.psum(every, BOTH)
+    on_diagonal = {z_: z_ for z_ in range(4)}
+    diagonal = first_sums(own_rows(product(own, own), core), on_diagonal)
+    own, one, every, diagonal = lax.optimization_barrier((own, one, every, diagonal))
     zero = along(one, [(1, 2)])
-    three = along(own_later, [(3, 2)])
-
-    diagonal = product(own, own)
-    diagonal = rows_to_target(diagonal, core, {z_: z_ for z_ in range(4)})
+    three = along(own, [(3, 2)])
     b21 = product(own, one)
-    b23 = product(own, three)
-    inner = jnp.where(position == 1, b21, b23)
-    inner = rows_to_target(inner, core, {1: 0, 2: 3})
+    diagonal = second_sums(diagonal, on_diagonal)
+    zero, three, b21, diagonal = lax.optimization_barrier((zero, three, b21, diagonal))
 
     blocks = {
         (2, 1): b21,
@@ -202,6 +213,16 @@
     }
     upper = scattered(blocks, 0, g)
     lower = scattered(blocks, 1, g)
+    blocks, three = lax.optimization_barrier((blocks, three))
+    b23 = product(own, three)
+    inner_to = {1: 0, 2: 3}
+    inner = own_rows(jnp.where(position == 1, blocks[2, 1], b23), core)
+    upper, lower, inner = lax.optimization_barrier((upper, lower, inner))
+    upper = scattered_on(upper, 0, g)
+    lower = scattered_on(lower, 1, g)
+    inner = first_sums(inner, inner_to)
+    upper, lower, inner = lax.optimization_barrier((upper, lower, inner))
+    inner = second_sums(inner, inner_to)
 
     cross = None
     for k in range(2):

time: 566 us -> 523 us (0.924)
  the two profiles are of different devices: /device:TPU:0 before, /device:TPU:2 now
where the time goes in v2:
time: 523 us; the launch traced here: 516 us
  waiting for transfers between devices  260 us (50%)
  matrix products  64 us (12%)
  blocking collectives  57.8 us (11%)
  other arithmetic  56 us (11%)
  starting transfers between devices  50.6 us (10%)
  local copies, waits for them, and re-layouts  26.8 us (5%)
    ppermute x1, waiting for transfers between devices, met(): lax.ppermute(lax.dynamic_index_in_dim(column_halves, core, 0, False), BOT...  108 us
    ppermute x4, waiting for transfers between devices, partner(): return lax.ppermute(value, 'feat', [(f, f ^ bit) for f in range(4)])  81 us
    dot_general x6, matrix products, product(): lax.dot_general(left, right, (((1,), (1,)), ((), ())), precision=lax.Prec...  64 us
    psum x1, blocking collectives, met(): every = lax.psum(every, BOTH)  57.8 us
    ppermute x1, waiting for transfers between devices, met(): lax.ppermute(lax.dynamic_index_in_dim(column_halves, 1 - core, 0, False),...  48.8 us
    ppermute x3, starting transfers between devices, other_core(): return lax.ppermute(value, 'blk', [(i, i ^ 1) for i in range(count)])  14 us
    ppermute x3, waiting for transfers between devices, other_core(): return lax.ppermute(value, 'blk', [(i, i ^ 1) for i in range(count)])  12.8 us
    ppermute x3, starting transfers between devices, along(): return lax.ppermute(value, 'blk', pairs)  10.9 us
  transfers between devices with their start and end apart: 26, of which 9 were waited for; matrix products, arithmetic and copies ran while one was open for 14% of the time, Pallas kernels for 0%

profile of v2, /device:TPU:2, one launch (start us, length us, event | category | flops | bytes accessed | tf_op | source)
XLA Modules:
  0.0 515.7 jit_solution(16636263251341231653)
XLA Ops:
  0.0 4.0 constant_dynamic-slice_fusion.1
  4.0 4.5 collective-permute-done
  8.5 5.2 maximum_select_fusion
  13.6 11.0 %fusion.17 = f32[1024,1024]{1,0:T(8,128)S(1)} fusion(f32[1024,1024]{1,0:T(8,128)} %maximum_select_fusion), kind=kOutput, calls=%fused_computation.92 | convolution fusion | flops 6442450944 | bytes 8388608 | tf_op jit(solution)/shard_map/dot_general | solution.py:57
  24.7 5.5 %collective-permute-start.1 = (f32[1024,1024]{1,0:T(8,128)}, f32[1024,1024]{1,0:T(8,128)}, u32[]{:S(2)}, u32[]{:S(2)}) collective-permute-start(f32[1024,1024]{1,0:T(8,128)} %maximum_select_fusion), channel_id=1, source_target_pairs={{0,8},{8,16},{28,20},{20,12},{1,9},{9,17},{29,21},{21,13},{2,10},{... | collective-permute-start | bytes 12582920 | tf_op jit(solution)/shard_map/ppermute | solution.py:80
  30.4 4.3 collective-permute-done.2
  34.7 2.6 bitcast_add_fusion.3
  37.3 1.5 fusion.16
  38.8 2.5 collective-permute-start.3
  41.3 1.3 collective-permute-start.4
  42.6 2.5 multiply_reduce_fusion
  45.4 57.8 %psum.7 = f32[4096]{0:T(1024)S(1)} all-reduce(f32[4096]{0:T(1024)S(1)} %dynamic_update_slice.3), channel_id=1, replica_groups=mesh['blk'=8,'feat'=4] {'blk','feat'}, use_global_device_ids=true, to_apply=%region_1.2 | all-reduce | flops 4096 | bytes 32768 | tf_op jit(solution)/shard_map/psum | solution.py:198
  103.2 1.0 copy-done.15
  104.2 3.0 slice_add_fusion
  107.2 2.7 collective-permute-start.5
  109.9 2.7 collective-permute-start.6
  113.3 2.7 collective-permute-start.8
  116.1 10.5 %fusion.18 = f32[1024,1024]{1,0:T(8,128)S(1)} fusion(f32[1024,1024]{1,0:T(8,128)} %maximum_select_fusion, f32[1024,1024]{1,0:T(8,128)} %collective-permute-done.1), kind=kOutput, calls=%fused_computation.93 | convolution fusion | flops 6442450944 | bytes 12582912 | tf_op jit(solution)/shard_map/dot_general | solution.py:57
  126.6 2.2 add.133
  128.8 8.9 %collective-permute-done.8 = f32[512,512]{1,0:T(8,128)S(1)} collective-permute-done((f32[512,512]{1,0:T(8,128)S(1)}, f32[512,512]{1,0:T(8,128)S(1)}, u32[]{:S(2)}, u32[]{:S(2)}) %collective-permute-start.8) | collective-permute-done | bytes 1048608 | tf_op jit(solution)/shard_map/ppermute | solution.py:109
  138.0 1.5 pad_maximum_fusion
  139.4 10.4 %fusion.19 = f32[1024,1024]{1,0:T(8,128)S(1)} fusion(f32[1024,1024]{1,0:T(8,128)} %maximum_select_fusion, f32[1024,1024]{1,0:T(8,128)} %collective-permute-done.5), kind=kOutput, calls=%fused_computation.94 | convolution fusion | flops 6442450944 | bytes 12582912 | tf_op jit(solution)/shard_map/dot_general | solution.py:57
  149.9 10.5 %fusion.20 = f32[1024,1024]{1,0:T(8,128)S(1)} fusion(f32[1024,1024]{1,0:T(8,128)} %collective-permute-done.6, f32[1024,1024]{1,0:T(8,128)} %collective-permute-done.5), kind=kOutput, calls=%fused_computation.95 | convolution fusion | flops 6442450944 | bytes 12582912 | tf_op jit(solution)/shard_map/dot_general | solution.py:57
  160.3 10.6 %fusion.21 = f32[1024,1024]{1,0:T(8,128)S(1)} fusion(f32[1024,1024]{1,0:T(8,128)} %collective-permute-done.6, f32[1024,1024]{1,0:T(8,128)} %collective-permute-done.1), kind=kOutput, calls=%fused_computation.96 | convolution fusion | flops 6442450944 | bytes 12582912 | tf_op jit(solution)/shard_map/dot_general | solution.py:57
  175.1 1.1 copy-done
  176.2 3.2 fusion.1
  179.5 2.8 collective-permute-start.10
  183.7 1.5 copy-done.4
  185.2 3.4 fusion.6
  188.6 11.0 %broadcast_select_fusion = f32[1024,1024]{1,0:T(8,128)S(1)} fusion(f32[1024,1024]{1,0:T(8,128)} %copy-done.9, pred[]{:T(512)S(6)} %eq.50, f32[1024,1024]{1,0:T(8,128)} %maximum_select_fusion, f32[1024,1024]{1,0:T(8,128)} %collective-permute-done.6), kind=kOutput, calls=%fused_computation.53 | convolution fusion | flops 6443499520 | bytes 16777216 | tf_op jit(solution)/shard_map/dot_general | solution.py:57
  199.6 2.0 copy-done.8
  201.5 1.5 dynamic-slice_bitcast_fusion.2
  203.0 13.9 %collective-permute-start.11 = (f32[512,1024]{1,0:T(8,128)}, f32[512,1024]{1,0:T(8,128)S(1)}, u32[]{:S(2)}, u32[]{:S(2)}) collective-permute-start(f32[512,1024]{1,0:T(8,128)} %dynamic-slice_bitcast_fusion.2), channel_id=1, source_target_pairs={{0,4},{4,0},{8,12},{12,8},{16,20},{20,16},{24,28},{28,24},{1,5},{5... | collective-permute-start | bytes 6291464 | tf_op jit(solution)/shard_map/ppermute | solution.py:85
  216.9 4.0 collective-permute-done.11
  220.9 2.0 bitcast_add_fusion.2
  222.9 1.2 fusion.15
  224.1 36.9 %collective-permute-done.10 = f32[2,2,512,512]{3,2,1,0:T(8,128)} collective-permute-done((f32[2,2,512,512]{3,2,1,0:T(8,128)}, f32[2,2,512,512]{3,2,1,0:T(8,128)}, u32[]{:S(2)}, u32[]{:S(2)}) %collective-permute-start.10) | collective-permute-done | bytes 4194336 | tf_op jit(solution)/shard_map/ppermute | solution.py:89
  261.0 3.8 fusion.4
  264.8 5.2 %collective-permute-done.9 = f32[2,2,512,512]{3,2,1,0:T(8,128)} collective-permute-done((f32[2,2,512,512]{3,2,1,0:T(8,128)}, f32[2,2,512,512]{3,2,1,0:T(8,128)}, u32[]{:S(2)}, u32[]{:S(2)}) %collective-permute-start.9) | collective-permute-done | bytes 4194336 | tf_op jit(solution)/shard_map/ppermute | solution.py:89
  270.1 3.8 fusion.9
  275.8 0.7 collective-permute-start.14
  277.0 38.9 %collective-permute-done.13 = f32[2,512,512]{2,1,0:T(8,128)S(1)} collective-permute-done((f32[2,512,512]{2,1,0:T(8,128)S(1)}, f32[2,512,512]{2,1,0:T(8,128)S(1)}, u32[]{:S(2)}, u32[]{:S(2)}) %collective-permute-start.13) | collective-permute-done | bytes 2097184 | tf_op jit(solution)/shard_map/ppermute | solution.py:89
  316.8 1.5 slice_bitcast_fusion.23
  319.0 0.7 collective-permute-start.16
  320.5 1.6 slice_bitcast_fusion.21
  322.1 1.9 collective-permute-start.23
  324.0 1.5 pad_maximum_fusion.2
  325.6 2.0 collective-permute-start.21
  327.5 1.6 pad_maximum_fusion.1
  329.1 2.0 collective-permute-start.20
  331.1 1.6 collective-permute-start.24
  332.8 1.7 collective-permute-start.25
  334.9 1.5 fusion.14
  336.4 2.5 copy.2
  338.9 1.3 copy.3
  340.2 1.3 collective-permute-start.18
  341.5 1.3 collective-permute-start.19
  342.9 3.6 broadcast_select_fusion.2
  346.6 4.1 add.149
  350.6 2.9 copy.4
  353.5 108.0 %collective-permute-done.18 = f32[512,512]{1,0:T(8,128)} collective-permute-done((f32[512,512]{1,0:T(8,128)}, f32[512,512]{1,0:T(8,128)}, u32[]{:S(2)}, u32[]{:S(2)}) %collective-permute-start.18) | collective-permute-done | bytes 1048608 | tf_op jit(solution)/shard_map/ppermute | solution.py:248
  461.5 48.8 %collective-permute-done.19 = f32[512,512]{1,0:T(8,128)} collective-permute-done((f32[512,512]{1,0:T(8,128)}, f32[512,512]{1,0:T(8,128)}, u32[]{:S(2)}, u32[]{:S(2)}) %collective-permute-start.19) | collective-permute-done | bytes 1048608 | tf_op jit(solution)/shard_map/ppermute | solution.py:253
  510.3 1.8 broadcast_select_fusion.4
  512.1 3.2 fusion.12
  (80 shorter events, 12.1 us)
Async XLA Ops:
  4.0 4.5 collective-permute-start
  24.6 5.5 %copy-start.12 = (f32[1024,1024]{1,0:T(8,128)}, f32[1024,1024]{1,0:T(8,128)S(1)}, u32[]{:S(2)}) copy-start(f32[1024,1024]{1,0:T(8,128)S(1)} %fusion.17) | copy-start | bytes 12582916
  24.7 82.5 %collective-permute-start.1 = (f32[1024,1024]{1,0:T(8,128)}, f32[1024,1024]{1,0:T(8,128)}, u32[]{:S(2)}, u32[]{:S(2)}) collective-permute-start(f32[1024,1024]{1,0:T(8,128)} %maximum_select_fusion), channel_id=1, source_target_pairs={{0,8},{8,16},{28,20},{20,12},{1,9},{9,17},{29,21},{21,13},{2,10},{... | collective-permute-start | bytes 12582920 | tf_op jit(solution)/shard_map/ppermute | solution.py:80
  30.3 4.4 collective-permute-start.2
  38.8 64.4 %collective-permute-start.3 = (f32[512,512]{1,0:T(8,128)}, f32[512,512]{1,0:T(8,128)S(1)}, u32[]{:S(2)}, u32[]{:S(2)}) collective-permute-start(f32[512,512]{1,0:T(8,128)} %get-tuple-element.80), channel_id=1, source_target_pairs={{1,0},{3,2},{5,4},{7,6},{8,9},{10,11},{12,13},{14,15},{17,16},{19,... | collective-permute-start | bytes 3145736 | tf_op jit(solution)/shard_map/ppermute | solution.py:100
  41.3 62.9 %collective-permute-start.4 = (f32[512,512]{1,0:T(8,128)}, f32[512,512]{1,0:T(8,128)}, u32[]{:S(2)}, u32[]{:S(2)}) collective-permute-start(f32[512,512]{1,0:T(8,128)} %get-tuple-element.79), channel_id=1, source_target_pairs={{2,0},{3,1},{6,4},{7,5},{10,8},{11,9},{14,12},{15,13},{16,18},{17,... | collective-permute-start | bytes 3145736 | tf_op jit(solution)/shard_map/ppermute | solution.py:100
  103.2 1.0 copy-start.15
  107.2 32.2 %collective-permute-start.5 = (f32[1024,1024]{1,0:T(8,128)}, f32[1024,1024]{1,0:T(8,128)}, u32[]{:S(2)}, u32[]{:S(2)}) collective-permute-start(f32[1024,1024]{1,0:T(8,128)} %collective-permute-done.1), channel_id=1, source_target_pairs={{8,16},{20,12},{9,17},{21,13},{10,18},{22,14},{11,19},{23,15}} | collective-permute-start | bytes 12582920 | tf_op jit(solution)/shard_map/ppermute | solution.py:80
  109.9 29.5 %collective-permute-start.6 = (f32[1024,1024]{1,0:T(8,128)}, f32[1024,1024]{1,0:T(8,128)}, u32[]{:S(2)}, u32[]{:S(2)}) collective-permute-start(f32[1024,1024]{1,0:T(8,128)} %maximum_select_fusion), channel_id=1, source_target_pairs={{24,16},{4,12},{25,17},{5,13},{26,18},{6,14},{27,19},{7,15}} | collective-permute-start | bytes 12582920 | tf_op jit(solution)/shard_map/ppermute | solution.py:80
  112.6 14.0 %collective-permute-start.7 = (f32[512,512]{1,0:T(8,128)}, f32[512,512]{1,0:T(8,128)S(1)}, u32[]{:S(2)}, u32[]{:S(2)}) collective-permute-start(f32[512,512]{1,0:T(8,128)} %get-tuple-element.26), channel_id=1, source_target_pairs={{2,0},{6,4},{11,9},{15,13},{16,18},{20,22},{25,27},{29,31}} | collective-permute-start | bytes 3145736 | tf_op jit(solution)/shard_map/ppermute | solution.py:109
  113.3 24.5 %collective-permute-start.8 = (f32[512,512]{1,0:T(8,128)S(1)}, f32[512,512]{1,0:T(8,128)S(1)}, u32[]{:S(2)}, u32[]{:S(2)}) collective-permute-start(f32[512,512]{1,0:T(8,128)S(1)} %get-tuple-element.27), channel_id=1, source_target_pairs={{1,0},{5,4},{8,9},{12,13},{19,18},{23,22},{26,27},{30,31}} | collective-permute-start | bytes 3145736 | tf_op jit(solution)/shard_map/ppermute | solution.py:109
  126.6 45.3 %copy-start.9 = (f32[1024,1024]{1,0:T(8,128)}, f32[1024,1024]{1,0:T(8,128)S(1)}, u32[]{:S(2)}) copy-start(f32[1024,1024]{1,0:T(8,128)S(1)} %fusion.18) | copy-start | bytes 12582916
  174.2 2.1 copy-start
  176.2 3.2 copy-start.2
  179.5 81.6 %collective-permute-start.10 = (f32[2,2,512,512]{3,2,1,0:T(8,128)}, f32[2,2,512,512]{3,2,1,0:T(8,128)}, u32[]{:S(2)}, u32[]{:S(2)}) collective-permute-start(f32[2,2,512,512]{3,2,1,0:T(8,128)} %fusion.1), channel_id=1, source_target_pairs={{0,1},{1,0},{2,3},{3,2},{4,5},{5,4},{6,7},{7,6},{8,9},{9,8},{10,11... | collective-permute-start | bytes 12582920 | tf_op jit(solution)/shard_map/ppermute | solution.py:89
  183.2 2.0 copy-start.4
  185.2 3.4 copy-start.6
  188.6 81.5 %collective-permute-start.9 = (f32[2,2,512,512]{3,2,1,0:T(8,128)}, f32[2,2,512,512]{3,2,1,0:T(8,128)}, u32[]{:S(2)}, u32[]{:S(2)}) collective-permute-start(f32[2,2,512,512]{3,2,1,0:T(8,128)} %fusion.6), channel_id=1, source_target_pairs={{0,2},{1,3},{2,0},{3,1},{4,6},{5,7},{6,4},{7,5},{8,10},{9,11},{10,... | collective-permute-start | bytes 12582920 | tf_op jit(solution)/shard_map/ppermute | solution.py:89
  199.6 2.0 copy-start.8
  203.0 17.9 %collective-permute-start.11 = (f32[512,1024]{1,0:T(8,128)}, f32[512,1024]{1,0:T(8,128)S(1)}, u32[]{:S(2)}, u32[]{:S(2)}) collective-permute-start(f32[512,1024]{1,0:T(8,128)} %dynamic-slice_bitcast_fusion.2), channel_id=1, source_target_pairs={{0,4},{4,0},{8,12},{12,8},{16,20},{20,16},{24,28},{28,24},{1,5},{5... | collective-permute-start | bytes 6291464 | tf_op jit(solution)/shard_map/ppermute | solution.py:85
  216.9 44.1 %copy-start.1 = (f32[1,2,2,512,512]{4,3,2,1,0:T(8,128)S(1)}, f32[1,2,2,512,512]{4,3,2,1,0:T(8,128)}, u32[]{:S(2)}) copy-start(f32[1,2,2,512,512]{4,3,2,1,0:T(8,128)} %copy-done) | copy-start | bytes 12582916
  216.9 44.1 %copy-start.3 = (f32[1,2,2,512,512]{4,3,2,1,0:T(8,128)S(1)}, f32[1,2,2,512,512]{4,3,2,1,0:T(8,128)}, u32[]{:S(2)}) copy-start(f32[1,2,2,512,512]{4,3,2,1,0:T(8,128)} %copy-done.2) | copy-start | bytes 12582916
  224.1 46.0 %copy-start.5 = (f32[1,2,2,512,512]{4,3,2,1,0:T(8,128)S(1)}, f32[1,2,2,512,512]{4,3,2,1,0:T(8,128)}, u32[]{:S(2)}) copy-start(f32[1,2,2,512,512]{4,3,2,1,0:T(8,128)} %copy-done.4) | copy-start | bytes 12582916
  224.1 46.0 %copy-start.7 = (f32[1,2,2,512,512]{4,3,2,1,0:T(8,128)S(1)}, f32[1,2,2,512,512]{4,3,2,1,0:T(8,128)}, u32[]{:S(2)}) copy-start(f32[1,2,2,512,512]{4,3,2,1,0:T(8,128)} %copy-done.6) | copy-start | bytes 12582916
  273.8 1.2 copy-start.13
  274.0 41.8 %collective-permute-start.13 = (f32[2,512,512]{2,1,0:T(8,128)S(1)}, f32[2,512,512]{2,1,0:T(8,128)S(1)}, u32[]{:S(2)}, u32[]{:S(2)}) collective-permute-start(f32[2,512,512]{2,1,0:T(8,128)S(1)} %dynamic-slice_bitcast_fusion), channel_id=1, source_target_pairs={{0,2},{1,3},{2,0},{3,1},{4,6},{5,7},{6,4},{7,5},{8,10},{9,11},{10,... | collective-permute-start | bytes 6291464 | tf_op jit(solution)/shard_map/ppermute | solution.py:89
  274.3 42.0 %collective-permute-start.12 = (f32[2,512,512]{2,1,0:T(8,128)S(1)}, f32[2,512,512]{2,1,0:T(8,128)S(1)}, u32[]{:S(2)}, u32[]{:S(2)}) collective-permute-start(f32[2,512,512]{2,1,0:T(8,128)S(1)} %dynamic-slice_bitcast_fusion.1), channel_id=1, source_target_pairs={{0,1},{1,0},{2,3},{3,2},{4,5},{5,4},{6,7},{7,6},{8,9},{9,8},{10,11... | collective-permute-start | bytes 6291464 | tf_op jit(solution)/shard_map/ppermute | solution.py:89
  275.1 1.5 collective-permute-start.15
  275.8 1.0 collective-permute-start.14
  318.3 10.8 %collective-permute-start.22 = (f32[512,512]{1,0:T(8,128)S(1)}, f32[512,512]{1,0:T(8,128)S(1)}, u32[]{:S(2)}, u32[]{:S(2)}) collective-permute-start(f32[512,512]{1,0:T(8,128)S(1)} %get-tuple-element.67), channel_id=1, source_target_pairs={{16,16},{17,25},{18,17},{19,24},{15,11},{14,2},{13,10},{12,3}} | collective-permute-start | bytes 3145736 | tf_op jit(solution)/shard_map/ppermute | solution.py:238
  319.0 12.1 %collective-permute-start.16 = (f32[512,512]{1,0:T(8,128)S(1)}, f32[512,512]{1,0:T(8,128)S(1)}, u32[]{:S(2)}, u32[]{:S(2)}) collective-permute-start(f32[512,512]{1,0:T(8,128)S(1)} %add.145), channel_id=1, source_target_pairs={{10,8},{14,12},{17,19},{21,23}} | collective-permute-start | bytes 3145736 | tf_op jit(solution)/shard_map/ppermute | solution.py:109
  319.8 13.0 %collective-permute-start.17 = (f32[512,512]{1,0:T(8,128)S(1)}, f32[512,512]{1,0:T(8,128)S(1)}, u32[]{:S(2)}, u32[]{:S(2)}) collective-permute-start(f32[512,512]{1,0:T(8,128)S(1)} %add.146), channel_id=1, source_target_pairs={{9,8},{13,12},{18,19},{22,23}} | collective-permute-start | bytes 3145736 | tf_op jit(solution)/shard_map/ppermute | solution.py:109
  322.1 18.1 %collective-permute-start.23 = (f32[512,512]{1,0:T(8,128)}, f32[512,512]{1,0:T(8,128)}, u32[]{:S(2)}, u32[]{:S(2)}) collective-permute-start(f32[512,512]{1,0:T(8,128)} %get-tuple-element.63), channel_id=1, source_target_pairs={{16,20},{17,29},{18,21},{19,28},{15,15},{14,6},{13,14},{12,7}} | collective-permute-start | bytes 3145736 | tf_op jit(solution)/shard_map/ppermute | solution.py:238
  325.6 21.0 %collective-permute-start.21 = (f32[512,1024]{0,1:T(8,128)}, f32[512,1024]{0,1:T(8,128)}, u32[]{:S(2)}, u32[]{:S(2)}) collective-permute-start(f32[512,1024]{0,1:T(8,128)} %pad_maximum_fusion.2), channel_id=1, source_target_pairs={{16,3},{17,10},{18,6},{19,15},{15,24},{14,17},{13,29},{12,20}} | collective-permute-start | bytes 6291464 | tf_op jit(solution)/shard_map/ppermute | solution.py:231
  329.1 7.2 %copy-start.14 = (f32[512,512]{1,0:T(8,128)}, f32[512,512]{1,0:T(8,128)S(1)}, u32[]{:S(2)}) copy-start(f32[512,512]{1,0:T(8,128)S(1)} %collective-permute-done.22) | copy-start | bytes 3145732
  329.1 17.4 %collective-permute-start.20 = (f32[512,1024]{0,1:T(8,128)}, f32[512,1024]{0,1:T(8,128)}, u32[]{:S(2)}, u32[]{:S(2)}) collective-permute-start(f32[512,1024]{0,1:T(8,128)} %pad_maximum_fusion.1), channel_id=1, source_target_pairs={{16,2},{17,11},{18,14},{19,7},{15,25},{14,16},{13,21},{12,28}} | collective-permute-start | bytes 6291464 | tf_op jit(solution)/shard_map/ppermute | solution.py:231
  331.1 10.3 %collective-permute-start.24 = (f32[512,512]{1,0:T(8,128)}, f32[512,512]{1,0:T(8,128)}, u32[]{:S(2)}, u32[]{:S(2)}) collective-permute-start(f32[512,512]{1,0:T(8,128)} %get-tuple-element.70), channel_id=1, source_target_pairs={{16,24},{17,17},{18,16},{19,25},{15,3},{14,10},{13,11},{12,2}} | collective-permute-start | bytes 3145736 | tf_op jit(solution)/shard_map/ppermute | solution.py:238
  332.8 10.1 %collective-permute-start.25 = (f32[512,512]{1,0:T(8,128)}, f32[512,512]{1,0:T(8,128)}, u32[]{:S(2)}, u32[]{:S(2)}) collective-permute-start(f32[512,512]{1,0:T(8,128)} %get-tuple-element.66), channel_id=1, source_target_pairs={{16,28},{17,21},{18,20},{19,29},{15,7},{14,14},{13,15},{12,6}} | collective-permute-start | bytes 3145736 | tf_op jit(solution)/shard_map/ppermute | solution.py:238
  340.2 121.3 %collective-permute-start.18 = (f32[512,512]{1,0:T(8,128)}, f32[512,512]{1,0:T(8,128)}, u32[]{:S(2)}, u32[]{:S(2)}) collective-permute-start(f32[512,512]{1,0:T(8,128)} %bitcast.133), channel_id=1, source_target_pairs={{8,1},{12,5},{19,26},{23,30}} | collective-permute-start | bytes 3145736 | tf_op jit(solution)/shard_map/ppermute | solution.py:248
  341.5 168.8 %collective-permute-start.19 = (f32[512,512]{1,0:T(8,128)}, f32[512,512]{1,0:T(8,128)}, u32[]{:S(2)}, u32[]{:S(2)}) collective-permute-start(f32[512,512]{1,0:T(8,128)} %bitcast.132), channel_id=1, source_target_pairs={{8,5},{12,1},{19,30},{23,26}} | collective-permute-start | bytes 3145736 | tf_op jit(solution)/shard_map/ppermute | solution.py:253
  353.5 158.6 %copy-start.10 = (f32[512,1024]{1,0:T(8,128)S(1)}, f32[512,1024]{1,0:T(8,128)}, u32[]{:S(2)}) copy-start(f32[512,1024]{1,0:T(8,128)} %pad_maximum_fusion) | copy-start | bytes 6291460
  353.5 158.6 %copy-start.11 = (f32[512,1024]{1,0:T(8,128)S(1)}, f32[512,1024]{1,0:T(8,128)}, u32[]{:S(2)}) copy-start(f32[512,1024]{1,0:T(8,128)} %copy.4) | copy-start | bytes 6291460

commit v3 on v0

--- a/solution.py
+++ b/solution.py
@@ -15,7 +15,7 @@
         left,
         right,
         (((1,), (1,)), ((), ())),
-        precision=lax.Precision.HIGHEST,
+        precision=lax.Precision.HIGH,
         preferred_element_type=jnp.float32,
     )
 
@@ -29,20 +29,23 @@
     rows = grads.shape[0]
     blocks = lax.axis_size("blk")
     mine = lax.axis_index("blk")
+    half = blocks // 2
+    held = passed_along(grads, "blk", 1)
+    squares = lax.psum(jnp.sum(grads * grads, axis=1), "feat")
+    every = lax.all_gather(squares, "blk", axis=0, tiled=True)
+    piece = tile_of(grads, grads)
+    held, squares, every, piece = lax.optimization_barrier((held, squares, every, piece))
     partial_value = jnp.zeros((rows, blocks * rows), jnp.float32)
-    partial_value = place(partial_value, tile_of(grads, grads), mine)
-    half = blocks // 2
-    held = grads
+    partial_value = place(partial_value, piece, mine)
     for step in range(1, half + 1):
-        held = passed_along(held, "blk", 1)
         piece = tile_of(grads, held)
         partial_value = place(partial_value, piece, (mine - step) % blocks)
         if step < half:
+            coming = passed_along(held, "blk", 1)
             back = passed_along(piece.T, "blk", -step)
+            held, back = lax.optimization_barrier((coming, back))
             partial_value = place(partial_value, back, (mine + step) % blocks)
     gram = lax.psum_scatter(partial_value, "feat", scatter_dimension=1, tiled=True)
-    squares = lax.psum(jnp.sum(grads * grads, axis=1), "feat")
-    every = lax.all_gather(squares, "blk", axis=0, tiled=True)
     width = gram.shape[1]
     column_sq = lax.dynamic_slice_in_dim(every, lax.axis_index("feat") * width, width)
     row_inverse = 1.0 / jnp.sqrt(squares + 1e-06)

time: 399 us -> 393 us (0.985)
  blocking collectives: 20.4 us -> 52 us
  waiting for transfers between devices: 293 us -> 265 us
  matrix products: 45.1 us -> 27.2 us
  local copies, waits for them, and re-layouts: 11.5 us -> 18.7 us
    ppermute x7, waiting for transfers between devices: 230 us -> 180 us  [passed_along(): return lax.ppermute(value, axis, pairs)]
    all_gather x1, blocking collectives: 11.2 us -> 43.1 us  [local(): every = lax.all_gather(squares, 'blk', axis=0, tiled=True)]
    reduce_scatter x1, waiting for transfers between devices: 62.6 us -> 85.5 us  [local(): lax.psum_scatter(partial_value, 'feat', scatter_dimension=1, tiled=True)]
    dot_general x5, matrix products: 45.1 us -> 27.2 us  [tile_of(): lax.dot_general(left, right, (((1,), (1,)), ((), ())), precision=lax.Prec...]
    dynamic_update_slice x3 -> x8, local copies, waits for them, and re-layouts: 3.22 us -> 11.2 us  [place(): lax.dynamic_update_slice(partial_value, piece, (jnp.int32(0), offset))]
    unnamed x8 -> x16, local copies, waits for them, and re-layouts: 6.34 us -> 1 us
  transfers between devices with their start and end apart: 8 -> 8, of which waited for: 6 -> 5; matrix products, arithmetic and copies ran while one was open for 11% -> 10% of each run, Pallas kernels for 0% -> 0%
where the time goes in v3:
time: 393 us; the launch traced here: 391 us
  waiting for transfers between devices  265 us (67%)
  blocking collectives  52 us (13%)
  matrix products  27.2 us (7%)
  local copies, waits for them, and re-layouts  18.7 us (5%)
  between operations  13.5 us (3%)
  starting transfers between devices  8.68 us (2%)
  other arithmetic  5.7 us (1%)
    ppermute x7, waiting for transfers between devices, passed_along(): return lax.ppermute(value, axis, pairs)  180 us
    reduce_scatter x1, waiting for transfers between devices, local(): lax.psum_scatter(partial_value, 'feat', scatter_dimension=1, tiled=True)  85.5 us
    all_gather x1, blocking collectives, local(): every = lax.all_gather(squares, 'blk', axis=0, tiled=True)  43.1 us
    dot_general x5, matrix products, tile_of(): lax.dot_general(left, right, (((1,), (1,)), ((), ())), precision=lax.Prec...  27.2 us
    dynamic_update_slice x8, local copies, waits for them, and re-layouts, place(): lax.dynamic_update_slice(partial_value, piece, (jnp.int32(0), offset))  11.2 us
    psum x1, blocking collectives, local(): squares = lax.psum(jnp.sum(grads * grads, axis=1), 'feat')  8.96 us
    ppermute x7, starting transfers between devices, passed_along(): return lax.ppermute(value, axis, pairs)  8.67 us
  transfers between devices with their start and end apart: 8, of which 5 were waited for; matrix products, arithmetic and copies ran while one was open for 10% of the time, Pallas kernels for 0%

profile of v3, /device:TPU:12, one launch (start us, length us, event | category | flops | bytes accessed | tf_op | source)
XLA Modules:
  0.0 391.1 jit_solution(5866216837154755625)
XLA Ops:
  6.5 0.0 reduce-scatter.2.cloned.1.call-start
  6.5 0.0 collective-permute-start
  6.5 2.5 multiply_reduce_fusion
  9.1 9.0 %psum.7 = f32[512]{0:T(512)S(1)} all-reduce(f32[512]{0:T(512)S(1)} %multiply_reduce_fusion), channel_id=1, replica_groups=mesh['blk'=8,'feat'=4] {'feat'}, use_global_device_ids=true, to_apply=%region_1.0 | all-reduce | flops 512 | bytes 4096 | tf_op jit(solution)/shard_map/psum | solution.py:34
  18.0 43.1 %all-gather = f32[8,1,512]{2,1,0:T(1,128)S(1)} all-gather(f32[1,1,512]{2,1,0:T(1,128)S(1)} %bitcast.21), channel_id=1, replica_groups=mesh['blk'=8,'feat'=4] {'blk'}, dimensions={0}, use_global_device_ids=true | all-gather | bytes 18432 | tf_op jit(solution)/shard_map/all_gather | solution.py:35
  61.1 0.0 copy-start
  61.1 7.6 %fusion = f32[512,512]{1,0:T(8,128)S(1)} fusion(f32[512,2048]{1,0:T(8,128)} %param.1), kind=kOutput, calls=%fused_computation.13 | convolution fusion | flops 3221225472 | bytes 5242880 | tf_op jit(solution)/shard_map/dot_general | solution.py:14
  68.7 0.0 collective-permute-done
  68.7 0.3 collective-permute-start.1
  69.0 0.0 copy-done
  69.0 5.4 %fusion.1 = f32[512,512]{1,0:T(8,128)S(1)} fusion(f32[512,2048]{1,0:T(8,128)} %collective-permute-done, f32[512,2048]{1,0:T(8,128)S(1)} %copy-done), kind=kOutput, calls=%fused_computation.14 | convolution fusion | flops 3221225472 | bytes 9437184 | tf_op jit(solution)/shard_map/dot_general | solution.py:14
  74.4 1.6 collective-permute-start.2
  76.0 24.4 %collective-permute-done.2 = f32[512,512]{1,0:T(8,128)S(1)} collective-permute-done((f32[512,512]{1,0:T(8,128)S(1)}, f32[512,512]{1,0:T(8,128)S(1)}, u32[]{:S(2)}, u32[]{:S(2)}) %collective-permute-start.2) | collective-permute-done | bytes 1048608 | tf_op jit(solution)/shard_map/ppermute | solution.py:10
  100.4 0.0 copy-start.5
  100.4 27.8 %collective-permute-done.1 = f32[512,2048]{1,0:T(8,128)S(1)} collective-permute-done((f32[512,2048]{1,0:T(8,128)}, f32[512,2048]{1,0:T(8,128)S(1)}, u32[]{:S(2)}, u32[]{:S(2)}) %collective-permute-start.1) | collective-permute-done | bytes 4194336 | tf_op jit(solution)/shard_map/ppermute | solution.py:10
  128.2 0.0 collective-permute-start.3
  128.2 3.5 fusion.2
  131.6 0.0 copy-done.5
  131.7 0.0 copy-start.2
  131.7 2.9 collective-permute-start.4
  134.6 67.2 %collective-permute-done.4 = f32[512,512]{1,0:T(8,128)S(1)} collective-permute-done((f32[512,512]{1,0:T(8,128)S(1)}, f32[512,512]{1,0:T(8,128)S(1)}, u32[]{:S(2)}, u32[]{:S(2)}) %collective-permute-start.4) | collective-permute-done | bytes 1048608 | tf_op jit(solution)/shard_map/ppermute | solution.py:10
  201.8 0.0 copy-start.6
  201.8 0.0 collective-permute-done.3
  201.8 1.0 copy-done.6
  202.8 0.0 collective-permute-start.5
  202.8 5.4 %fusion.3 = f32[512,512]{1,0:T(8,128)S(1)} fusion(f32[512,2048]{1,0:T(8,128)} %collective-permute-done.3, f32[512,2048]{1,0:T(8,128)S(1)} %copy-done), kind=kOutput, calls=%fused_computation.16 | convolution fusion | flops 3221225472 | bytes 9437184 | tf_op jit(solution)/shard_map/dot_general | solution.py:14
  208.1 0.0 copy-done.2
  208.2 3.8 collective-permute-start.6
  212.0 1.3 copy.6
  213.3 0.0 copy-start.4
  213.3 4.3 %broadcast_in_dim.2 = f32[512,4096]{1,0:T(8,128)} broadcast(f32[]{:T(128)} %constant.58.clone.1), dimensions={} | broadcast | bytes 8388612 | tf_op jit(solution)/shard_map/broadcast_in_dim | solution.py:38
  217.6 0.0 copy-start.3
  217.6 1.1 constant_dynamic-update-slice_fusion.7
  218.6 0.0 copy-done.4
  218.6 1.1 constant_dynamic-update-slice_fusion.6
  219.7 0.0 copy-done.3
  219.7 0.3 copy.7
  220.1 0.0 copy-start.7
  220.1 2.4 constant_dynamic-update-slice_fusion.5
  222.4 1.1 constant_dynamic-update-slice_fusion.4
  223.5 0.3 copy.8
  223.8 0.0 copy-done.7
  223.8 0.0 copy-start.1
  223.9 1.1 constant_dynamic-update-slice_fusion.3
  224.9 1.1 constant_dynamic-update-slice_fusion.2
  226.1 60.4 %collective-permute-done.6 = f32[512,512]{1,0:T(8,128)} collective-permute-done((f32[512,512]{1,0:T(8,128)S(1)}, f32[512,512]{1,0:T(8,128)}, u32[]{:S(2)}, u32[]{:S(2)}) %collective-permute-start.6) | collective-permute-done | bytes 1048608 | tf_op jit(solution)/shard_map/ppermute | solution.py:10
  286.5 0.0 collective-permute-done.5
  286.5 0.0 copy-done.1
  286.5 5.4 %convolution_bitcast_fusion = f32[512,512]{0,1:T(8,128)S(1)} fusion(f32[512,2048]{1,0:T(8,128)} %collective-permute-done.5, f32[512,2048]{1,0:T(8,128)S(1)} %copy-done.1), kind=kOutput, calls=%fused_computation.2 | convolution fusion | flops 3221225472 | bytes 9437184 | tf_op jit(solution)/shard_map/dot_general | solution.py:14
  291.8 0.3 copy.9
  292.2 2.3 constant_dynamic-update-slice_fusion.1
  294.5 1.1 constant_dynamic-update-slice_fusion
  295.6 0.0 reduce-scatter.2.cloned.1.call-update
  295.6 85.5 %reduce-scatter.2.cloned.1.call-done = f32[512,1024]{1,0:T(8,128)} async-done(((f32[512,4096]{1,0:T(8,128)}), f32[512,1024]{1,0:T(8,128)}) %reduce-scatter.2.cloned.1.call-update) | async-done | bytes 2097168 | tf_op jit(solution)/shard_map/reduce_scatter | solution.py:48
  381.1 3.1 multiply_multiply_fusion
  (2 shorter events, 0.0 us)
Async XLA Ops:
  6.5 374.6 %reduce-scatter.2.cloned.1.call-start = ((), (), s32[]{:S(2)}) async-start(), calls=%async_computation.1 | async-start | bytes 10485760 | tf_op jit(solution)/shard_map/reduce_scatter | solution.py:48
  6.5 62.2 %collective-permute-start = (f32[512,2048]{1,0:T(8,128)}, f32[512,2048]{1,0:T(8,128)}, u32[]{:S(2)}, u32[]{:S(2)}) collective-permute-start(f32[512,2048]{1,0:T(8,128)} %param.1), channel_id=1, source_target_pairs={{0,4},{4,8},{8,12},{12,16},{16,20},{20,24},{24,28},{28,0},{1,5},{5... | collective-permute-start | bytes 12582920 | tf_op jit(solution)/shard_map/ppermute | solution.py:10
  61.1 7.9 %copy-start = (f32[512,2048]{1,0:T(8,128)S(1)}, f32[512,2048]{1,0:T(8,128)}, u32[]{:S(2)}) copy-start(f32[512,2048]{1,0:T(8,128)} %param.1) | copy-start | bytes 12582916
  68.7 59.4 %collective-permute-start.1 = (f32[512,2048]{1,0:T(8,128)}, f32[512,2048]{1,0:T(8,128)S(1)}, u32[]{:S(2)}, u32[]{:S(2)}) collective-permute-start(f32[512,2048]{1,0:T(8,128)} %collective-permute-done), channel_id=1, source_target_pairs={{0,4},{4,8},{8,12},{12,16},{16,20},{20,24},{24,28},{28,0},{1,5},{5... | collective-permute-start | bytes 12582920 | tf_op jit(solution)/shard_map/ppermute | solution.py:10
  74.4 26.0 %collective-permute-start.2 = (f32[512,512]{1,0:T(8,128)S(1)}, f32[512,512]{1,0:T(8,128)S(1)}, u32[]{:S(2)}, u32[]{:S(2)}) collective-permute-start(f32[512,512]{1,0:T(8,128)S(1)} %fusion.1), channel_id=1, source_target_pairs={{0,28},{4,0},{8,4},{12,8},{16,12},{20,16},{24,20},{28,24},{1,29},{... | collective-permute-start | bytes 3145736 | tf_op jit(solution)/shard_map/ppermute | solution.py:10
  100.4 31.3 %copy-start.5 = (f32[512,512]{1,0:T(8,128)}, f32[512,512]{1,0:T(8,128)S(1)}, u32[]{:S(2)}) copy-start(f32[512,512]{1,0:T(8,128)S(1)} %collective-permute-done.2) | copy-start | bytes 3145732
  128.2 73.6 %collective-permute-start.3 = (f32[512,2048]{1,0:T(8,128)S(1)}, f32[512,2048]{1,0:T(8,128)}, u32[]{:S(2)}, u32[]{:S(2)}) collective-permute-start(f32[512,2048]{1,0:T(8,128)S(1)} %collective-permute-done.1), channel_id=1, source_target_pairs={{0,4},{4,8},{8,12},{12,16},{16,20},{20,24},{24,28},{28,0},{1,5},{5... | collective-permute-start | bytes 12582920 | tf_op jit(solution)/shard_map/ppermute | solution.py:10
  131.7 76.5 %copy-start.2 = (f32[512,512]{1,0:T(8,128)}, f32[512,512]{1,0:T(8,128)S(1)}, u32[]{:S(2)}) copy-start(f32[512,512]{1,0:T(8,128)S(1)} %fusion.2) | copy-start | bytes 3145732
  131.7 70.1 %collective-permute-start.4 = (f32[512,512]{1,0:T(8,128)S(1)}, f32[512,512]{1,0:T(8,128)S(1)}, u32[]{:S(2)}, u32[]{:S(2)}) collective-permute-start(f32[512,512]{1,0:T(8,128)S(1)} %fusion.2), channel_id=1, source_target_pairs={{0,24},{4,28},{8,0},{12,4},{16,8},{20,12},{24,16},{28,20},{1,25},{... | collective-permute-start | bytes 3145736 | tf_op jit(solution)/shard_map/ppermute | solution.py:10
  201.8 1.0 copy-start.6
  202.8 83.7 %collective-permute-start.5 = (f32[512,2048]{1,0:T(8,128)}, f32[512,2048]{1,0:T(8,128)}, u32[]{:S(2)}, u32[]{:S(2)}) collective-permute-start(f32[512,2048]{1,0:T(8,128)} %collective-permute-done.3), channel_id=1, source_target_pairs={{0,4},{4,8},{8,12},{12,16},{16,20},{20,24},{24,28},{28,0},{1,5},{5... | collective-permute-start | bytes 12582920 | tf_op jit(solution)/shard_map/ppermute | solution.py:10
  208.2 78.3 %collective-permute-start.6 = (f32[512,512]{1,0:T(8,128)S(1)}, f32[512,512]{1,0:T(8,128)}, u32[]{:S(2)}, u32[]{:S(2)}) collective-permute-start(f32[512,512]{1,0:T(8,128)S(1)} %fusion.3), channel_id=1, source_target_pairs={{0,20},{4,24},{8,28},{12,0},{16,4},{20,8},{24,12},{28,16},{1,21},{... | collective-permute-start | bytes 3145736 | tf_op jit(solution)/shard_map/ppermute | solution.py:10
  213.3 5.3 %copy-start.4 = (f32[512,512]{1,0:T(8,128)S(1)}, f32[512,512]{1,0:T(8,128)}, u32[]{:S(2)}) copy-start(f32[512,512]{1,0:T(8,128)} %copy.6) | copy-start | bytes 3145732
  217.6 2.1 copy-start.3
  220.1 3.8 copy-start.7
  223.8 62.6 %copy-start.1 = (f32[512,2048]{1,0:T(8,128)S(1)}, f32[512,2048]{1,0:T(8,128)}, u32[]{:S(2)}) copy-start(f32[512,2048]{1,0:T(8,128)} %param.1) | copy-start | bytes 12582916
Sparse Core Ops, SparseCore 0:
  295.7 85.3 reduce-scatter.1

commit v4 on v3

v4 whole, which is shorter than its diff:
```python
import jax
import jax.numpy as jnp
from jax import lax
from jax.sharding import PartitionSpec as P


def passed_along(value, axis, steps):
    count = lax.axis_size(axis)
    pairs = [(source, (source + steps) % count) for source in range(count)]
    return lax.ppermute(value, axis, pairs)


def tile_of(left, right):
    return lax.dot_general(
        left,
        right,
        (((1,), (1,)), ((), ())),
        precision=lax.Precision.HIGH,
        preferred_element_type=jnp.float32,
    )


def summed_at(piece, shift):
    blocks, feats = lax.axis_size("blk"), lax.axis_size("feat")
    per = blocks // feats
    bits = [1 << i for i in range(feats.bit_length() - 1)]
    half = piece.shape[1] // 2
    sums = []
    for value, order in ((piece[:, :half], bits), (piece[:, half:], bits[::-1])):
        done = 0
        for bit in order:
            pairs = []
            for block in range(blocks):
                target = (block + shift) % blocks // per
                pairs += [
                    (block * feats + f, block * feats + (f ^ bit))
                    for f in range(feats)
                    if (f ^ target) & bit and not (f ^ target) & done
                ]
            value = value + lax.ppermute(value, ("blk", "feat"), pairs)
            done |= bit
        sums.append(value)
    return jnp.concatenate(sums, axis=1)


def local(grads):
    blocks, feats = lax.axis_size("blk"), lax.axis_size("feat")
    mine, column = lax.axis_index("blk"), lax.axis_index("feat")
    half = blocks // 2
    sums = {}
    held = passed_along(grads, "blk", 1)
    squares = lax.psum(jnp.sum(grads * grads, axis=1), "feat")
    every = lax.all_gather(squares, "blk", axis=0, tiled=True)
    piece = tile_of(grads, grads)
    held, squares, every, piece = lax.optimization_barrier((held, squares, every, piece))
    waiting = (0, piece)
    for step in range(1, half + 1):
        piece = tile_of(grads, held)
        shift = (blocks - step) % blocks
        if step < half:
            coming = passed_along(held, "blk", 1)
            back = passed_along(piece.T, "blk", -step)
            sums[waiting[0]] = summed_at(waiting[1], waiting[0])
            sums[shift] = summed_at(piece, shift)
            held, back, sums[waiting[0]], sums[shift] = lax.optimization_barrier(
                (coming, back, sums[waiting[0]], sums[shift])
            )
            waiting = (step, back)
        else:
            sums[waiting[0]] = summed_at(waiting[1], waiting[0])
            sums[shift] = summed_at(piece, shift)
    per = blocks // feats
    columns = []
    for q in range(per):
        wanted = (column * per + q - mine) % blocks
        chosen = sums[0]
        for shift in range(1, blocks):
            chosen = jnp.where(wanted == shift, sums[shift], chosen)
        columns.append(chosen)
    gram = jnp.concatenate(columns, axis=1)
    width = gram.shape[1]
    column_sq = lax.dynamic_slice_in_dim(every, column * width, width)
    row_inverse = 1.0 / jnp.sqrt(squares + 1e-06)
    column_inverse = 1.0 / jnp.sqrt(column_sq + 1e-06)
    return gram * row_inverse[:, None] * column_inverse[None, :]


def solution(mesh):
    placed = (P("blk", "feat"),)
    return jax.shard_map(
        local, mesh=mesh, in_specs=placed, out_specs=P("blk", "feat"), check_vma=False
    )
```

time: 393 us -> 328 us (0.83)
  waiting for transfers between devices: 265 us -> 137 us
  starting transfers between devices: 8.68 us -> 70.6 us
  other arithmetic: 5.7 us -> 24.1 us
  between operations: 13.5 us -> 0.73 us
  local copies, waits for them, and re-layouts: 18.7 us -> 7.97 us
  matrix products: 27.2 us -> 32 us
    ppermute x7, waiting for transfers between devices: 180 us -> 78 us  [passed_along(): return lax.ppermute(value, axis, pairs)]
    reduce_scatter x1 -> x0, waiting for transfers between devices: 85.5 us -> none  [local(): lax.psum_scatter(partial_value, 'feat', scatter_dimension=1, tiled=True)]
    ppermute x0 -> x32, starting transfers between devices: none -> 67.1 us  [summed_at(): value = value + lax.ppermute(value, ('blk', 'feat'), pairs)]
    ppermute x0 -> x32, waiting for transfers between devices: none -> 59.4 us  [summed_at(): value = value + lax.ppermute(value, ('blk', 'feat'), pairs)]
    add x0 -> x24, other arithmetic: none -> 13.3 us  [summed_at(): value = value + lax.ppermute(value, ('blk', 'feat'), pairs)]
    dynamic_update_slice x8 -> x0, local copies, waits for them, and re-layouts: 11.2 us -> none  [place(): lax.dynamic_update_slice(partial_value, piece, (jnp.int32(0), offset))]
    ppermute x7, starting transfers between devices: 8.67 us -> 3.51 us  [passed_along(): return lax.ppermute(value, axis, pairs)]
    dot_general x5, matrix products: 27.2 us -> 32 us  [tile_of(): lax.dot_general(left, right, (((1,), (1,)), ((), ())), precision=lax.Prec...]
  transfers between devices with their start and end apart: 8 -> 39, of which waited for: 5 -> 18; matrix products, arithmetic and copies ran while one was open for 10% -> 18% of each run, Pallas kernels for 0% -> 0%
where the time goes in v4:
time: 328 us; the launch traced here: 325 us
  waiting for transfers between devices  137 us (42%)
  starting transfers between devices  70.6 us (22%)
  blocking collectives  52 us (16%)
  matrix products  32 us (10%)
  other arithmetic  24.1 us (7%)
  local copies, waits for them, and re-layouts  7.97 us (2%)
    ppermute x7, waiting for transfers between devices, passed_along(): return lax.ppermute(value, axis, pairs)  78 us
    ppermute x32, starting transfers between devices, summed_at(): value = value + lax.ppermute(value, ('blk', 'feat'), pairs)  67.1 us
    ppermute x32, waiting for transfers between devices, summed_at(): value = value + lax.ppermute(value, ('blk', 'feat'), pairs)  59.4 us
    all_gather x1, blocking collectives, local(): every = lax.all_gather(squares, 'blk', axis=0, tiled=True)  43.1 us
    dot_general x5, matrix products, tile_of(): lax.dot_general(left, right, (((1,), (1,)), ((), ())), precision=lax.Prec...  32 us
    add x24, other arithmetic, summed_at(): value = value + lax.ppermute(value, ('blk', 'feat'), pairs)  13.3 us
    psum x1, blocking collectives, local(): squares = lax.psum(jnp.sum(grads * grads, axis=1), 'feat')  8.96 us
  transfers between devices with their start and end apart: 39, of which 18 were waited for; matrix products, arithmetic and copies ran while one was open for 18% of the time, Pallas kernels for 0%

profile of v4, /device:TPU:12, one launch (start us, length us, event | category | flops | bytes accessed | tf_op | source)
XLA Modules:
  0.0 324.8 jit_solution(9134142431873296224)
XLA Ops:
  0.0 2.5 multiply_reduce_fusion
  2.5 9.0 %psum.7 = f32[512]{0:T(512)S(1)} all-reduce(f32[512]{0:T(512)S(1)} %multiply_reduce_fusion), channel_id=1, replica_groups=mesh['blk'=8,'feat'=4] {'feat'}, use_global_device_ids=true, to_apply=%region_1.0 | all-reduce | flops 512 | bytes 4096 | tf_op jit(solution)/shard_map/psum | solution.py:52
  11.5 43.1 %all-gather = f32[8,1,512]{2,1,0:T(1,128)S(1)} all-gather(f32[1,1,512]{2,1,0:T(1,128)S(1)} %bitcast.24), channel_id=1, replica_groups=mesh['blk'=8,'feat'=4] {'blk'}, dimensions={0}, use_global_device_ids=true | all-gather | bytes 18432 | tf_op jit(solution)/shard_map/all_gather | solution.py:53
  54.6 7.6 %fusion.9 = f32[512,512]{1,0:T(8,128)S(1)} fusion(f32[512,2048]{1,0:T(8,128)} %param.1), kind=kOutput, calls=%fused_computation.40 | convolution fusion | flops 3221225472 | bytes 5242880 | tf_op jit(solution)/shard_map/dot_general | solution.py:14
  63.5 4.2 %collective-permute-start.3 = (f32[512,256]{1,0:T(8,128)}, f32[512,256]{1,0:T(8,128)}, u32[]{:S(2)}, u32[]{:S(2)}) collective-permute-start(f32[512,256]{1,0:T(8,128)} %get-tuple-element.67), channel_id=1, source_target_pairs={{1,0},{3,2},{5,4},{7,6},{8,9},{10,11},{12,13},{14,15},{17,16},{19,... | collective-permute-start | bytes 1572872 | tf_op jit(solution)/shard_map/ppermute | solution.py:40
  67.7 3.2 collective-permute-start.5
  70.9 5.4 %fusion.10 = f32[512,512]{1,0:T(8,128)S(1)} fusion(f32[512,2048]{1,0:T(8,128)} %collective-permute-done, f32[512,2048]{1,0:T(8,128)S(1)} %copy-done), kind=kOutput, calls=%fused_computation.41 | convolution fusion | flops 3221225472 | bytes 9437184 | tf_op jit(solution)/shard_map/dot_general | solution.py:14
  76.7 1.3 collective-permute-start.7
  78.0 1.3 collective-permute-start.9
  79.4 3.4 %collective-permute-done.5 = f32[512,256]{1,0:T(8,128)} collective-permute-done((f32[512,256]{1,0:T(8,128)}, f32[512,256]{1,0:T(8,128)}, u32[]{:S(2)}, u32[]{:S(2)}) %collective-permute-start.5) | collective-permute-done | bytes 524320 | tf_op jit(solution)/shard_map/ppermute | solution.py:40
  82.7 1.3 slice_add_fusion.15
  84.8 3.0 collective-permute-done.7
  88.5 4.2 %collective-permute-done.9 = f32[512,256]{1,0:T(8,128)S(1)} collective-permute-done((f32[512,256]{1,0:T(8,128)S(1)}, f32[512,256]{1,0:T(8,128)S(1)}, u32[]{:S(2)}, u32[]{:S(2)}) %collective-permute-start.9) | collective-permute-done | bytes 524320 | tf_op jit(solution)/shard_map/ppermute | solution.py:40
  93.6 6.8 %collective-permute-start.8 = (f32[512,256]{1,0:T(8,128)S(1)}, f32[512,256]{1,0:T(8,128)S(1)}, u32[]{:S(2)}, u32[]{:S(2)}) collective-permute-start(f32[512,256]{1,0:T(8,128)S(1)} %get-tuple-element.61), channel_id=1, source_target_pairs={{1,3},{6,4},{10,8},{15,13},{19,17},{20,22},{24,26},{29,31}} | collective-permute-start | bytes 1572872 | tf_op jit(solution)/shard_map/ppermute | solution.py:40
  100.6 6.4 %collective-permute-done.8 = f32[512,256]{1,0:T(8,128)S(1)} collective-permute-done((f32[512,256]{1,0:T(8,128)S(1)}, f32[512,256]{1,0:T(8,128)S(1)}, u32[]{:S(2)}, u32[]{:S(2)}) %collective-permute-start.8) | collective-permute-done | bytes 524320 | tf_op jit(solution)/shard_map/ppermute | solution.py:40
  107.4 3.6 %collective-permute-done.2 = f32[512,512]{1,0:T(8,128)S(1)} collective-permute-done((f32[512,512]{1,0:T(8,128)S(1)}, f32[512,512]{1,0:T(8,128)S(1)}, u32[]{:S(2)}, u32[]{:S(2)}) %collective-permute-start.2) | collective-permute-done | bytes 1048608 | tf_op jit(solution)/shard_map/ppermute | solution.py:10
  111.0 10.7 %collective-permute-done.1 = f32[512,2048]{1,0:T(8,128)} collective-permute-done((f32[512,2048]{1,0:T(8,128)}, f32[512,2048]{1,0:T(8,128)}, u32[]{:S(2)}, u32[]{:S(2)}) %collective-permute-start.1) | collective-permute-done | bytes 4194336 | tf_op jit(solution)/shard_map/ppermute | solution.py:10
  122.8 4.2 %collective-permute-start.13 = (f32[512,256]{1,0:T(8,128)}, f32[512,256]{1,0:T(8,128)}, u32[]{:S(2)}, u32[]{:S(2)}) collective-permute-start(f32[512,256]{1,0:T(8,128)} %get-tuple-element.59), channel_id=1, source_target_pairs={{1,0},{3,2},{4,5},{6,7},{8,9},{10,11},{13,12},{15,14},{17,16},{19,... | collective-permute-start | bytes 1572872 | tf_op jit(solution)/shard_map/ppermute | solution.py:40
  127.0 4.9 %collective-permute-start.15 = (f32[512,256]{1,0:T(8,128)}, f32[512,256]{1,0:T(8,128)}, u32[]{:S(2)}, u32[]{:S(2)}) collective-permute-start(f32[512,256]{1,0:T(8,128)} %get-tuple-element.60), channel_id=1, source_target_pairs={{2,0},{3,1},{6,4},{7,5},{10,8},{11,9},{12,14},{13,15},{16,18},{17,... | collective-permute-start | bytes 1572872 | tf_op jit(solution)/shard_map/ppermute | solution.py:40
  131.9 6.6 %fusion.11 = f32[512,512]{1,0:T(8,128)} fusion(f32[512,2048]{1,0:T(8,128)} %collective-permute-done.1, f32[512,2048]{1,0:T(8,128)S(1)} %copy-done.1), kind=kOutput, calls=%fused_computation.42 | convolution fusion | flops 3221225472 | bytes 9437184 | tf_op jit(solution)/shard_map/dot_general | solution.py:14
  138.6 1.6 copy.7
  140.2 1.4 collective-permute-start.17
  141.6 1.5 collective-permute-start.19
  143.2 1.7 slice_add_fusion.13
  145.5 2.7 collective-permute-start.12
  148.2 7.0 %collective-permute-done.17 = f32[512,256]{1,0:T(8,128)S(1)} collective-permute-done((f32[512,256]{1,0:T(8,128)S(1)}, f32[512,256]{1,0:T(8,128)S(1)}, u32[]{:S(2)}, u32[]{:S(2)}) %collective-permute-start.17) | collective-permute-done | bytes 524320 | tf_op jit(solution)/shard_map/ppermute | solution.py:40
  156.8 1.3 collective-permute-start.18
  158.4 11.7 %collective-permute-done.18 = f32[512,256]{1,0:T(8,128)S(1)} collective-permute-done((f32[512,256]{1,0:T(8,128)S(1)}, f32[512,256]{1,0:T(8,128)S(1)}, u32[]{:S(2)}, u32[]{:S(2)}) %collective-permute-start.18) | collective-permute-done | bytes 524320 | tf_op jit(solution)/shard_map/ppermute | solution.py:40
  172.5 23.1 %collective-permute-done.12 = f32[512,512]{1,0:T(8,128)S(1)} collective-permute-done((f32[512,512]{1,0:T(8,128)S(1)}, f32[512,512]{1,0:T(8,128)S(1)}, u32[]{:S(2)}, u32[]{:S(2)}) %collective-permute-start.12) | collective-permute-done | bytes 1048608 | tf_op jit(solution)/shard_map/ppermute | solution.py:10
  197.6 1.3 collective-permute-start.23
  198.9 1.3 collective-permute-start.25
  200.2 6.6 %fusion.12 = f32[512,512]{1,0:T(8,128)} fusion(f32[512,2048]{1,0:T(8,128)} %collective-permute-done.11, f32[512,2048]{1,0:T(8,128)S(1)} %copy-done.2), kind=kOutput, calls=%fused_computation.43 | convolution fusion | flops 3221225472 | bytes 9437184 | tf_op jit(solution)/shard_map/dot_general | solution.py:14
  206.9 1.6 copy.8
  208.5 5.5 %collective-permute-start.27 = (f32[512,256]{1,0:T(8,128)S(1)}, f32[512,256]{1,0:T(8,128)S(1)}, u32[]{:S(2)}, u32[]{:S(2)}) collective-permute-start(f32[512,256]{1,0:T(8,128)S(1)} %get-tuple-element.47), channel_id=1, source_target_pairs={{1,0},{3,2},{4,5},{6,7},{8,9},{10,11},{13,12},{15,14},{17,16},{19,... | collective-permute-start | bytes 1572872 | tf_op jit(solution)/shard_map/ppermute | solution.py:40
  214.1 1.3 collective-permute-start.29
  215.4 1.7 slice_add_fusion.11
  217.0 1.3 collective-permute-start.26
  218.8 1.9 collective-permute-done.27
  220.7 1.3 collective-permute-start.24
  222.0 4.0 %collective-permute-done.29 = f32[512,256]{1,0:T(8,128)S(1)} collective-permute-done((f32[512,256]{1,0:T(8,128)S(1)}, f32[512,256]{1,0:T(8,128)S(1)}, u32[]{:S(2)}, u32[]{:S(2)}) %collective-permute-start.29) | collective-permute-done | bytes 524320 | tf_op jit(solution)/shard_map/ppermute | solution.py:40
  226.1 1.3 collective-permute-start.30
  227.4 5.7 %collective-permute-done.26 = f32[512,256]{1,0:T(8,128)S(1)} collective-permute-done((f32[512,256]{1,0:T(8,128)S(1)}, f32[512,256]{1,0:T(8,128)S(1)}, u32[]{:S(2)}, u32[]{:S(2)}) %collective-permute-start.26) | collective-permute-done | bytes 524320 | tf_op jit(solution)/shard_map/ppermute | solution.py:40
  233.9 2.2 collective-permute-done.24
  236.4 1.1 pad_maximum_fusion.4
  237.5 1.1 pad_maximum_fusion.5
  238.6 40.5 %collective-permute-done.22 = f32[512,512]{1,0:T(8,128)S(1)} collective-permute-done((f32[512,512]{1,0:T(8,128)S(1)}, f32[512,512]{1,0:T(8,128)S(1)}, u32[]{:S(2)}, u32[]{:S(2)}) %collective-permute-start.22) | collective-permute-done | bytes 1048608 | tf_op jit(solution)/shard_map/ppermute | solution.py:10
  279.2 1.3 collective-permute-start.35
  280.5 1.3 collective-permute-start.37
  281.9 5.8 %convolution_bitcast_fusion = f32[512,512]{1,0:T(8,128)S(1)} fusion(f32[512,2048]{1,0:T(8,128)} %collective-permute-done.21, f32[512,2048]{1,0:T(8,128)S(1)} %copy-done.3), kind=kOutput, calls=%fused_computation.3 | convolution fusion | flops 3221225472 | bytes 9437184 | tf_op jit(solution)/shard_map/dot_general | solution.py:14
  287.7 4.6 %collective-permute-start.31 = (f32[512,256]{1,0:T(8,128)S(1)}, f32[512,256]{1,0:T(8,128)S(1)}, u32[]{:S(2)}, u32[]{:S(2)}) collective-permute-start(f32[512,256]{1,0:T(8,128)S(1)} %get-tuple-element.39), channel_id=1, source_target_pairs={{1,0},{3,2},{5,4},{7,6},{8,9},{10,11},{12,13},{14,15},{17,16},{19,... | collective-permute-start | bytes 1572872 | tf_op jit(solution)/shard_map/ppermute | solution.py:40
  292.3 1.3 collective-permute-start.33
  293.6 3.1 collective-permute-done.37
  297.8 1.3 collective-permute-start.38
  299.1 1.4 collective-permute-start.36
  300.5 3.5 %collective-permute-done.31 = f32[512,256]{1,0:T(8,128)S(1)} collective-permute-done((f32[512,256]{1,0:T(8,128)S(1)}, f32[512,256]{1,0:T(8,128)S(1)}, u32[]{:S(2)}, u32[]{:S(2)}) %collective-permute-start.31) | collective-permute-done | bytes 524320 | tf_op jit(solution)/shard_map/ppermute | solution.py:40
  304.1 1.2 collective-permute-done.33
  306.4 6.2 %collective-permute-start.34 = (f32[512,256]{1,0:T(8,128)}, f32[512,256]{1,0:T(8,128)}, u32[]{:S(2)}, u32[]{:S(2)}) collective-permute-start(f32[512,256]{1,0:T(8,128)} %get-tuple-element.38), channel_id=1, source_target_pairs={{3,2},{7,6},{10,11},{14,15},{17,16},{21,20},{24,25},{28,29}} | collective-permute-start | bytes 1572872 | tf_op jit(solution)/shard_map/ppermute | solution.py:40
  312.6 1.5 collective-permute-start.32
  314.1 1.4 add.155
  315.5 1.3 add.153
  316.8 2.0 collective-permute-done.34
  318.8 1.3 add.151
  320.1 1.3 add.149
  323.2 1.6 fusion
  (92 shorter events, 18.4 us)
Async XLA Ops:
  0.0 62.2 %collective-permute-start = (f32[512,2048]{1,0:T(8,128)}, f32[512,2048]{1,0:T(8,128)}, u32[]{:S(2)}, u32[]{:S(2)}) collective-permute-start(f32[512,2048]{1,0:T(8,128)} %param.1), channel_id=1, source_target_pairs={{0,4},{4,8},{8,12},{12,16},{16,20},{20,24},{24,28},{28,0},{1,5},{5... | collective-permute-start | bytes 12582920 | tf_op jit(solution)/shard_map/ppermute | solution.py:10
  54.6 16.4 %copy-start = (f32[512,2048]{1,0:T(8,128)S(1)}, f32[512,2048]{1,0:T(8,128)}, u32[]{:S(2)}) copy-start(f32[512,2048]{1,0:T(8,128)} %param.1) | copy-start | bytes 12582916
  62.2 59.5 %collective-permute-start.1 = (f32[512,2048]{1,0:T(8,128)}, f32[512,2048]{1,0:T(8,128)}, u32[]{:S(2)}, u32[]{:S(2)}) collective-permute-start(f32[512,2048]{1,0:T(8,128)} %collective-permute-done), channel_id=1, source_target_pairs={{0,4},{4,8},{8,12},{12,16},{16,20},{20,24},{24,28},{28,0},{1,5},{5... | collective-permute-start | bytes 12582920 | tf_op jit(solution)/shard_map/ppermute | solution.py:10
  63.5 15.8 %collective-permute-start.3 = (f32[512,256]{1,0:T(8,128)}, f32[512,256]{1,0:T(8,128)}, u32[]{:S(2)}, u32[]{:S(2)}) collective-permute-start(f32[512,256]{1,0:T(8,128)} %get-tuple-element.67), channel_id=1, source_target_pairs={{1,0},{3,2},{5,4},{7,6},{8,9},{10,11},{12,13},{14,15},{17,16},{19,... | collective-permute-start | bytes 1572872 | tf_op jit(solution)/shard_map/ppermute | solution.py:40
  67.7 15.0 %collective-permute-start.5 = (f32[512,256]{1,0:T(8,128)}, f32[512,256]{1,0:T(8,128)}, u32[]{:S(2)}, u32[]{:S(2)}) collective-permute-start(f32[512,256]{1,0:T(8,128)} %get-tuple-element.68), channel_id=1, source_target_pairs={{2,0},{3,1},{6,4},{7,5},{10,8},{11,9},{14,12},{15,13},{16,18},{17,... | collective-permute-start | bytes 1572872 | tf_op jit(solution)/shard_map/ppermute | solution.py:40
  76.7 11.1 %collective-permute-start.7 = (f32[512,256]{1,0:T(8,128)S(1)}, f32[512,256]{1,0:T(8,128)S(1)}, u32[]{:S(2)}, u32[]{:S(2)}) collective-permute-start(f32[512,256]{1,0:T(8,128)S(1)} %get-tuple-element.63), channel_id=1, source_target_pairs={{0,1},{2,3},{5,4},{7,6},{9,8},{11,10},{12,13},{14,15},{16,17},{18,... | collective-permute-start | bytes 1572872 | tf_op jit(solution)/shard_map/ppermute | solution.py:40
  78.0 14.7 %collective-permute-start.9 = (f32[512,256]{1,0:T(8,128)S(1)}, f32[512,256]{1,0:T(8,128)S(1)}, u32[]{:S(2)}, u32[]{:S(2)}) collective-permute-start(f32[512,256]{1,0:T(8,128)S(1)} %get-tuple-element.64), channel_id=1, source_target_pairs={{0,2},{1,3},{6,4},{7,5},{10,8},{11,9},{14,12},{15,13},{18,16},{19,... | collective-permute-start | bytes 1572872 | tf_op jit(solution)/shard_map/ppermute | solution.py:40
  84.1 9.5 %collective-permute-start.6 = (f32[512,256]{1,0:T(8,128)S(1)}, f32[512,256]{1,0:T(8,128)S(1)}, u32[]{:S(2)}, u32[]{:S(2)}) collective-permute-start(f32[512,256]{1,0:T(8,128)S(1)} %get-tuple-element.66), channel_id=1, source_target_pairs={{1,0},{5,4},{8,9},{12,13},{19,18},{23,22},{26,27},{30,31}} | collective-permute-start | bytes 1572872 | tf_op jit(solution)/shard_map/ppermute | solution.py:40
  84.8 26.2 %collective-permute-start.2 = (f32[512,512]{1,0:T(8,128)S(1)}, f32[512,512]{1,0:T(8,128)S(1)}, u32[]{:S(2)}, u32[]{:S(2)}) collective-permute-start(f32[512,512]{1,0:T(8,128)S(1)} %fusion.10), channel_id=1, source_target_pairs={{0,28},{4,0},{8,4},{12,8},{16,12},{20,16},{24,20},{28,24},{1,29},{... | collective-permute-start | bytes 3145736 | tf_op jit(solution)/shard_map/ppermute | solution.py:10
  87.8 12.6 %collective-permute-start.4 = (f32[512,256]{1,0:T(8,128)S(1)}, f32[512,256]{1,0:T(8,128)S(1)}, u32[]{:S(2)}, u32[]{:S(2)}) collective-permute-start(f32[512,256]{1,0:T(8,128)S(1)} %get-tuple-element.65), channel_id=1, source_target_pairs={{2,0},{6,4},{11,9},{15,13},{16,18},{20,22},{25,27},{29,31}} | collective-permute-start | bytes 1572872 | tf_op jit(solution)/shard_map/ppermute | solution.py:40
  92.9 7.7 %collective-permute-start.10 = (f32[512,256]{1,0:T(8,128)S(1)}, f32[512,256]{1,0:T(8,128)S(1)}, u32[]{:S(2)}, u32[]{:S(2)}) collective-permute-start(f32[512,256]{1,0:T(8,128)S(1)} %get-tuple-element.62), channel_id=1, source_target_pairs={{2,3},{5,4},{9,8},{12,13},{16,17},{23,22},{27,26},{30,31}} | collective-permute-start | bytes 1572872 | tf_op jit(solution)/shard_map/ppermute | solution.py:40
  93.6 13.4 %collective-permute-start.8 = (f32[512,256]{1,0:T(8,128)S(1)}, f32[512,256]{1,0:T(8,128)S(1)}, u32[]{:S(2)}, u32[]{:S(2)}) collective-permute-start(f32[512,256]{1,0:T(8,128)S(1)} %get-tuple-element.61), channel_id=1, source_target_pairs={{1,3},{6,4},{10,8},{15,13},{19,17},{20,22},{24,26},{29,31}} | collective-permute-start | bytes 1572872 | tf_op jit(solution)/shard_map/ppermute | solution.py:40
  100.6 31.3 %copy-start.1 = (f32[512,2048]{1,0:T(8,128)S(1)}, f32[512,2048]{1,0:T(8,128)}, u32[]{:S(2)}) copy-start(f32[512,2048]{1,0:T(8,128)} %param.1) | copy-start | bytes 12582916
  111.0 10.7 %copy-start.8 = (f32[512,512]{1,0:T(8,128)}, f32[512,512]{1,0:T(8,128)S(1)}, u32[]{:S(2)}) copy-start(f32[512,512]{1,0:T(8,128)S(1)} %collective-permute-done.2) | copy-start | bytes 3145732
  121.8 73.9 %collective-permute-start.11 = (f32[512,2048]{1,0:T(8,128)}, f32[512,2048]{1,0:T(8,128)}, u32[]{:S(2)}, u32[]{:S(2)}) collective-permute-start(f32[512,2048]{1,0:T(8,128)} %collective-permute-done.1), channel_id=1, source_target_pairs={{0,4},{4,8},{8,12},{12,16},{16,20},{20,24},{24,28},{28,0},{1,5},{5... | collective-permute-start | bytes 12582920 | tf_op jit(solution)/shard_map/ppermute | solution.py:10
  122.8 20.3 %collective-permute-start.13 = (f32[512,256]{1,0:T(8,128)}, f32[512,256]{1,0:T(8,128)}, u32[]{:S(2)}, u32[]{:S(2)}) collective-permute-start(f32[512,256]{1,0:T(8,128)} %get-tuple-element.59), channel_id=1, source_target_pairs={{1,0},{3,2},{4,5},{6,7},{8,9},{10,11},{13,12},{15,14},{17,16},{19,... | collective-permute-start | bytes 1572872 | tf_op jit(solution)/shard_map/ppermute | solution.py:40
  127.0 16.1 %collective-permute-start.15 = (f32[512,256]{1,0:T(8,128)}, f32[512,256]{1,0:T(8,128)}, u32[]{:S(2)}, u32[]{:S(2)}) collective-permute-start(f32[512,256]{1,0:T(8,128)} %get-tuple-element.60), channel_id=1, source_target_pairs={{2,0},{3,1},{6,4},{7,5},{10,8},{11,9},{12,14},{13,15},{16,18},{17,... | collective-permute-start | bytes 1572872 | tf_op jit(solution)/shard_map/ppermute | solution.py:40
  140.1 5.4 %copy-start.10 = (f32[512,512]{1,0:T(8,128)S(1)}, f32[512,512]{1,0:T(8,128)}, u32[]{:S(2)}) copy-start(f32[512,512]{1,0:T(8,128)} %fusion.11) | copy-start | bytes 3145732
  140.2 15.1 %collective-permute-start.17 = (f32[512,256]{1,0:T(8,128)S(1)}, f32[512,256]{1,0:T(8,128)S(1)}, u32[]{:S(2)}, u32[]{:S(2)}) collective-permute-start(f32[512,256]{1,0:T(8,128)S(1)} %get-tuple-element.55), channel_id=1, source_target_pairs={{0,1},{2,3},{4,5},{6,7},{9,8},{11,10},{13,12},{15,14},{16,17},{18,... | collective-permute-start | bytes 1572872 | tf_op jit(solution)/shard_map/ppermute | solution.py:40
  141.6 14.3 %collective-permute-start.19 = (f32[512,256]{1,0:T(8,128)S(1)}, f32[512,256]{1,0:T(8,128)S(1)}, u32[]{:S(2)}, u32[]{:S(2)}) collective-permute-start(f32[512,256]{1,0:T(8,128)S(1)} %get-tuple-element.56), channel_id=1, source_target_pairs={{0,2},{1,3},{4,6},{5,7},{10,8},{11,9},{14,12},{15,13},{18,16},{19,... | collective-permute-start | bytes 1572872 | tf_op jit(solution)/shard_map/ppermute | solution.py:40
  144.8 12.0 %collective-permute-start.16 = (f32[512,256]{1,0:T(8,128)S(1)}, f32[512,256]{1,0:T(8,128)S(1)}, u32[]{:S(2)}, u32[]{:S(2)}) collective-permute-start(f32[512,256]{1,0:T(8,128)S(1)} %get-tuple-element.58), channel_id=1, source_target_pairs={{1,0},{4,5},{8,9},{15,14},{19,18},{22,23},{26,27},{29,28}} | collective-permute-start | bytes 1572872 | tf_op jit(solution)/shard_map/ppermute | solution.py:40
  145.5 50.1 %collective-permute-start.12 = (f32[512,512]{1,0:T(8,128)S(1)}, f32[512,512]{1,0:T(8,128)S(1)}, u32[]{:S(2)}, u32[]{:S(2)}) collective-permute-start(f32[512,512]{1,0:T(8,128)S(1)} %copy-done.10), channel_id=1, source_target_pairs={{0,24},{4,28},{8,0},{12,4},{16,8},{20,12},{24,16},{28,20},{1,25},{... | collective-permute-start | bytes 3145736 | tf_op jit(solution)/shard_map/ppermute | solution.py:10
  155.3 3.0 collective-permute-start.14
  156.1 2.2 collective-permute-start.20
  156.8 13.3 %collective-permute-start.18 = (f32[512,256]{1,0:T(8,128)S(1)}, f32[512,256]{1,0:T(8,128)S(1)}, u32[]{:S(2)}, u32[]{:S(2)}) collective-permute-start(f32[512,256]{1,0:T(8,128)S(1)} %get-tuple-element.53), channel_id=1, source_target_pairs={{1,3},{5,7},{10,8},{14,12},{19,17},{23,21},{24,26},{28,30}} | collective-permute-start | bytes 1572872 | tf_op jit(solution)/shard_map/ppermute | solution.py:40
  158.4 41.8 %copy-start.2 = (f32[512,2048]{1,0:T(8,128)S(1)}, f32[512,2048]{1,0:T(8,128)}, u32[]{:S(2)}) copy-start(f32[512,2048]{1,0:T(8,128)} %param.1) | copy-start | bytes 12582916
  195.6 1.0 copy-start.9
  195.6 83.6 %collective-permute-start.21 = (f32[512,2048]{1,0:T(8,128)}, f32[512,2048]{1,0:T(8,128)}, u32[]{:S(2)}, u32[]{:S(2)}) collective-permute-start(f32[512,2048]{1,0:T(8,128)} %collective-permute-done.11), channel_id=1, source_target_pairs={{0,4},{4,8},{8,12},{12,16},{16,20},{20,24},{24,28},{28,0},{1,5},{5... | collective-permute-start | bytes 12582920 | tf_op jit(solution)/shard_map/ppermute | solution.py:10
  197.6 17.7 %collective-permute-start.23 = (f32[512,256]{1,0:T(8,128)}, f32[512,256]{1,0:T(8,128)}, u32[]{:S(2)}, u32[]{:S(2)}) collective-permute-start(f32[512,256]{1,0:T(8,128)} %get-tuple-element.51), channel_id=1, source_target_pairs={{0,1},{2,3},{4,5},{6,7},{9,8},{11,10},{13,12},{15,14},{16,17},{18,... | collective-permute-start | bytes 1572872 | tf_op jit(solution)/shard_map/ppermute | solution.py:40
  198.9 16.5 %collective-permute-start.25 = (f32[512,256]{1,0:T(8,128)}, f32[512,256]{1,0:T(8,128)}, u32[]{:S(2)}, u32[]{:S(2)}) collective-permute-start(f32[512,256]{1,0:T(8,128)} %get-tuple-element.52), channel_id=1, source_target_pairs={{2,0},{3,1},{6,4},{7,5},{8,10},{9,11},{12,14},{13,15},{16,18},{17,... | collective-permute-start | bytes 1572872 | tf_op jit(solution)/shard_map/ppermute | solution.py:40
  208.4 9.9 %copy-start.11 = (f32[512,512]{1,0:T(8,128)S(1)}, f32[512,512]{1,0:T(8,128)}, u32[]{:S(2)}) copy-start(f32[512,512]{1,0:T(8,128)} %fusion.12) | copy-start | bytes 3145732
  208.5 12.2 %collective-permute-start.27 = (f32[512,256]{1,0:T(8,128)S(1)}, f32[512,256]{1,0:T(8,128)S(1)}, u32[]{:S(2)}, u32[]{:S(2)}) collective-permute-start(f32[512,256]{1,0:T(8,128)S(1)} %get-tuple-element.47), channel_id=1, source_target_pairs={{1,0},{3,2},{4,5},{6,7},{8,9},{10,11},{13,12},{15,14},{17,16},{19,... | collective-permute-start | bytes 1572872 | tf_op jit(solution)/shard_map/ppermute | solution.py:40
  214.1 11.9 %collective-permute-start.29 = (f32[512,256]{1,0:T(8,128)S(1)}, f32[512,256]{1,0:T(8,128)S(1)}, u32[]{:S(2)}, u32[]{:S(2)}) collective-permute-start(f32[512,256]{1,0:T(8,128)S(1)} %get-tuple-element.48), channel_id=1, source_target_pairs={{0,2},{1,3},{4,6},{5,7},{8,10},{9,11},{14,12},{15,13},{18,16},{19,... | collective-permute-start | bytes 1572872 | tf_op jit(solution)/shard_map/ppermute | solution.py:40
  217.0 16.1 %collective-permute-start.26 = (f32[512,256]{1,0:T(8,128)S(1)}, f32[512,256]{1,0:T(8,128)S(1)}, u32[]{:S(2)}, u32[]{:S(2)}) collective-permute-start(f32[512,256]{1,0:T(8,128)S(1)} %get-tuple-element.50), channel_id=1, source_target_pairs={{0,1},{4,5},{11,10},{15,14},{18,19},{22,23},{25,24},{29,28}} | collective-permute-start | bytes 1572872 | tf_op jit(solution)/shard_map/ppermute | solution.py:40
  218.3 60.8 %collective-permute-start.22 = (f32[512,512]{1,0:T(8,128)S(1)}, f32[512,512]{1,0:T(8,128)S(1)}, u32[]{:S(2)}, u32[]{:S(2)}) collective-permute-start(f32[512,512]{1,0:T(8,128)S(1)} %copy-done.11), channel_id=1, source_target_pairs={{0,20},{4,24},{8,28},{12,0},{16,4},{20,8},{24,12},{28,16},{1,21},{... | collective-permute-start | bytes 3145736 | tf_op jit(solution)/shard_map/ppermute | solution.py:10
  220.7 15.4 %collective-permute-start.24 = (f32[512,256]{1,0:T(8,128)S(1)}, f32[512,256]{1,0:T(8,128)S(1)}, u32[]{:S(2)}, u32[]{:S(2)}) collective-permute-start(f32[512,256]{1,0:T(8,128)S(1)} %get-tuple-element.49), channel_id=1, source_target_pairs={{3,1},{7,5},{8,10},{12,14},{17,19},{21,23},{26,24},{30,28}} | collective-permute-start | bytes 1572872 | tf_op jit(solution)/shard_map/ppermute | solution.py:40
  226.1 10.1 %collective-permute-start.30 = (f32[512,256]{1,0:T(8,128)S(1)}, f32[512,256]{1,0:T(8,128)S(1)}, u32[]{:S(2)}, u32[]{:S(2)}) collective-permute-start(f32[512,256]{1,0:T(8,128)S(1)} %get-tuple-element.46), channel_id=1, source_target_pairs={{3,2},{6,7},{10,11},{13,12},{17,16},{20,21},{24,25},{31,30}} | collective-permute-start | bytes 1572872 | tf_op jit(solution)/shard_map/ppermute | solution.py:40
  233.1 3.2 collective-permute-start.28
  236.3 45.6 %copy-start.3 = (f32[512,2048]{1,0:T(8,128)S(1)}, f32[512,2048]{1,0:T(8,128)}, u32[]{:S(2)}) copy-start(f32[512,2048]{1,0:T(8,128)} %param.1) | copy-start | bytes 12582916
  279.2 14.4 %collective-permute-start.35 = (f32[512,256]{1,0:T(8,128)S(1)}, f32[512,256]{1,0:T(8,128)S(1)}, u32[]{:S(2)}, u32[]{:S(2)}) collective-permute-start(f32[512,256]{1,0:T(8,128)S(1)} %get-tuple-element.43), channel_id=1, source_target_pairs={{0,1},{2,3},{5,4},{7,6},{9,8},{11,10},{12,13},{14,15},{16,17},{18,... | collective-permute-start | bytes 1572872 | tf_op jit(solution)/shard_map/ppermute | solution.py:40
  280.5 16.2 %collective-permute-start.37 = (f32[512,256]{1,0:T(8,128)S(1)}, f32[512,256]{1,0:T(8,128)S(1)}, u32[]{:S(2)}, u32[]{:S(2)}) collective-permute-start(f32[512,256]{1,0:T(8,128)S(1)} %get-tuple-element.44), channel_id=1, source_target_pairs={{2,0},{3,1},{4,6},{5,7},{8,10},{9,11},{12,14},{13,15},{16,18},{17,... | collective-permute-start | bytes 1572872 | tf_op jit(solution)/shard_map/ppermute | solution.py:40
  287.7 16.4 %collective-permute-start.31 = (f32[512,256]{1,0:T(8,128)S(1)}, f32[512,256]{1,0:T(8,128)S(1)}, u32[]{:S(2)}, u32[]{:S(2)}) collective-permute-start(f32[512,256]{1,0:T(8,128)S(1)} %get-tuple-element.39), channel_id=1, source_target_pairs={{1,0},{3,2},{5,4},{7,6},{8,9},{10,11},{12,13},{14,15},{17,16},{19,... | collective-permute-start | bytes 1572872 | tf_op jit(solution)/shard_map/ppermute | solution.py:40
  292.3 13.0 %collective-permute-start.33 = (f32[512,256]{1,0:T(8,128)S(1)}, f32[512,256]{1,0:T(8,128)S(1)}, u32[]{:S(2)}, u32[]{:S(2)}) collective-permute-start(f32[512,256]{1,0:T(8,128)S(1)} %get-tuple-element.40), channel_id=1, source_target_pairs={{0,2},{1,3},{4,6},{5,7},{8,10},{9,11},{12,14},{13,15},{18,16},{19,... | collective-permute-start | bytes 1572872 | tf_op jit(solution)/shard_map/ppermute | solution.py:40
  297.8 16.3 %collective-permute-start.38 = (f32[512,256]{1,0:T(8,128)}, f32[512,256]{1,0:T(8,128)}, u32[]{:S(2)}, u32[]{:S(2)}) collective-permute-start(f32[512,256]{1,0:T(8,128)} %get-tuple-element.42), channel_id=1, source_target_pairs={{0,1},{7,6},{11,10},{14,15},{18,19},{21,20},{25,24},{28,29}} | collective-permute-start | bytes 1572872 | tf_op jit(solution)/shard_map/ppermute | solution.py:40
  299.1 22.2 %copy-start.4 = (f32[512,512]{1,0:T(8,128)S(1)}, f32[512,512]{1,0:T(8,128)}, u32[]{:S(2)}) copy-start(f32[512,512]{1,0:T(8,128)} %pad_maximum_fusion.2) | copy-start | bytes 3145732
  299.1 16.4 %collective-permute-start.36 = (f32[512,256]{1,0:T(8,128)}, f32[512,256]{1,0:T(8,128)}, u32[]{:S(2)}, u32[]{:S(2)}) collective-permute-start(f32[512,256]{1,0:T(8,128)} %get-tuple-element.41), channel_id=1, source_target_pairs={{3,1},{4,6},{8,10},{13,15},{17,19},{22,20},{26,24},{31,29}} | collective-permute-start | bytes 1572872 | tf_op jit(solution)/shard_map/ppermute | solution.py:40
  306.4 12.4 %collective-permute-start.34 = (f32[512,256]{1,0:T(8,128)}, f32[512,256]{1,0:T(8,128)}, u32[]{:S(2)}, u32[]{:S(2)}) collective-permute-start(f32[512,256]{1,0:T(8,128)} %get-tuple-element.38), channel_id=1, source_target_pairs={{3,2},{7,6},{10,11},{14,15},{17,16},{21,20},{24,25},{28,29}} | collective-permute-start | bytes 1572872 | tf_op jit(solution)/shard_map/ppermute | solution.py:40
  312.6 7.5 %collective-permute-start.32 = (f32[512,256]{1,0:T(8,128)}, f32[512,256]{1,0:T(8,128)}, u32[]{:S(2)}, u32[]{:S(2)}) collective-permute-start(f32[512,256]{1,0:T(8,128)} %get-tuple-element.37), channel_id=1, source_target_pairs={{0,2},{4,6},{9,11},{13,15},{18,16},{22,20},{27,25},{31,29}} | collective-permute-start | bytes 1572872 | tf_op jit(solution)/shard_map/ppermute | solution.py:40
  314.1 7.3 %copy-start.5 = (f32[512,512]{1,0:T(8,128)S(1)}, f32[512,512]{1,0:T(8,128)}, u32[]{:S(2)}) copy-start(f32[512,512]{1,0:T(8,128)} %pad_maximum_fusion.3) | copy-start | bytes 3145732
  314.1 7.3 %copy-start.6 = (f32[512,512]{1,0:T(8,128)S(1)}, f32[512,512]{1,0:T(8,128)}, u32[]{:S(2)}) copy-start(f32[512,512]{1,0:T(8,128)} %pad_maximum_fusion.4) | copy-start | bytes 3145732
  314.1 7.3 %copy-start.7 = (f32[512,512]{1,0:T(8,128)S(1)}, f32[512,512]{1,0:T(8,128)}, u32[]{:S(2)}) copy-start(f32[512,512]{1,0:T(8,128)} %pad_maximum_fusion.5) | copy-start | bytes 3145732

commit v5 on v4

--- a/solution.py
+++ b/solution.py
@@ -4,9 +4,18 @@
 from jax.sharding import PartitionSpec as P
 
 
+def position_of(block, count):
+    return (block // 2) * (1 - block % 2) + (count - 1 - block // 2) * (block % 2)
+
+
+def ring_order(count):
+    return sorted(range(count), key=lambda block: position_of(block, count))
+
+
 def passed_along(value, axis, steps):
     count = lax.axis_size(axis)
-    pairs = [(source, (source + steps) % count) for source in range(count)]
+    order = ring_order(count)
+    pairs = [(order[p], order[(p + steps) % count]) for p in range(count)]
     return lax.ppermute(value, axis, pairs)
 
 
@@ -25,13 +34,14 @@
     per = blocks // feats
     bits = [1 << i for i in range(feats.bit_length() - 1)]
     half = piece.shape[1] // 2
+    order_of = ring_order(blocks)
     sums = []
     for value, order in ((piece[:, :half], bits), (piece[:, half:], bits[::-1])):
         done = 0
         for bit in order:
             pairs = []
             for block in range(blocks):
-                target = (block + shift) % blocks // per
+                target = order_of[(position_of(block, blocks) + shift) % blocks] // per
                 pairs += [
                     (block * feats + f, block * feats + (f ^ bit))
                     for f in range(feats)
@@ -62,17 +72,23 @@
             back = passed_along(piece.T, "blk", -step)
             sums[waiting[0]] = summed_at(waiting[1], waiting[0])
             sums[shift] = summed_at(piece, shift)
+            if step == half - 1:
+                sums[step] = summed_at(back, step)
+                coming, sums = lax.optimization_barrier((coming, sums))
+                held = coming
+                continue
             held, back, sums[waiting[0]], sums[shift] = lax.optimization_barrier(
                 (coming, back, sums[waiting[0]], sums[shift])
             )
             waiting = (step, back)
         else:
-            sums[waiting[0]] = summed_at(waiting[1], waiting[0])
             sums[shift] = summed_at(piece, shift)
     per = blocks // feats
     columns = []
     for q in range(per):
-        wanted = (column * per + q - mine) % blocks
+        wanted = (
+            position_of(column * per + q, blocks) - position_of(mine, blocks)
+        ) % blocks
         chosen = sums[0]
         for shift in range(1, blocks):
             chosen = jnp.where(wanted == shift, sums[shift], chosen)

time: 328 us -> 343 us (1.046)
  starting transfers between devices: 70.6 us -> 82.8 us
    ppermute x7, starting transfers between devices: 3.51 us -> 19.4 us  [passed_along(): return lax.ppermute(value, axis, pairs)]
    ppermute x7, waiting for transfers between devices: 78 us -> 82.7 us  [passed_along(): return lax.ppermute(value, axis, pairs)]
    ppermute x32, starting transfers between devices: 67.1 us -> 63.4 us  [summed_at(): value = value + lax.ppermute(value, ('blk', 'feat'), pairs)]
    ppermute x32, waiting for transfers between devices: 59.4 us -> 55.9 us  [summed_at(): value = value + lax.ppermute(value, ('blk', 'feat'), pairs)]
  transfers between devices with their start and end apart: 39 -> 39, of which waited for: 18 -> 15; matrix products, arithmetic and copies ran while one was open for 18% -> 15% of each run, Pallas kernels for 0% -> 0%
where the time goes in v5:
time: 343 us; the launch traced here: 340 us
  waiting for transfers between devices  139 us (41%)
  starting transfers between devices  82.8 us (24%)
  blocking collectives  52.8 us (15%)
  matrix products  32.1 us (9%)
  other arithmetic  22.8 us (7%)
  local copies, waits for them, and re-layouts  9.56 us (3%)
    ppermute x7, waiting for transfers between devices, passed_along(): return lax.ppermute(value, axis, pairs)  82.7 us
    ppermute x32, starting transfers between devices, summed_at(): value = value + lax.ppermute(value, ('blk', 'feat'), pairs)  63.4 us
    ppermute x32, waiting for transfers between devices, summed_at(): value = value + lax.ppermute(value, ('blk', 'feat'), pairs)  55.9 us
    all_gather x1, blocking collectives, local(): every = lax.all_gather(squares, 'blk', axis=0, tiled=True)  43.9 us
    dot_general x5, matrix products, tile_of(): lax.dot_general(left, right, (((1,), (1,)), ((), ())), precision=lax.Prec...  32.1 us
    ppermute x7, starting transfers between devices, passed_along(): return lax.ppermute(value, axis, pairs)  19.4 us
    add x24, other arithmetic, summed_at(): value = value + lax.ppermute(value, ('blk', 'feat'), pairs)  10.7 us
    psum x1, blocking collectives, local(): squares = lax.psum(jnp.sum(grads * grads, axis=1), 'feat')  8.96 us
  transfers between devices with their start and end apart: 39, of which 15 were waited for; matrix products, arithmetic and copies ran while one was open for 15% of the time, Pallas kernels for 0%

profile of v5, /device:TPU:12, one launch (start us, length us, event | category | flops | bytes accessed | tf_op | source)
XLA Modules:
  0.0 339.6 jit_solution(1638257627489758895)
XLA Ops:
  0.0 1.6 collective-permute-start
  1.6 2.6 multiply_reduce_fusion
  4.1 9.0 %psum.7 = f32[512]{0:T(512)S(1)} all-reduce(f32[512]{0:T(512)S(1)} %multiply_reduce_fusion), channel_id=1, replica_groups=mesh['blk'=8,'feat'=4] {'feat'}, use_global_device_ids=true, to_apply=%region_1.0 | all-reduce | flops 512 | bytes 4096 | tf_op jit(solution)/shard_map/psum | solution.py:62
  13.1 43.9 %all-gather = f32[8,1,512]{2,1,0:T(1,128)S(1)} all-gather(f32[1,1,512]{2,1,0:T(1,128)S(1)} %bitcast.24), channel_id=1, replica_groups=mesh['blk'=8,'feat'=4] {'blk'}, dimensions={0}, use_global_device_ids=true | all-gather | bytes 18432 | tf_op jit(solution)/shard_map/all_gather | solution.py:63
  57.0 7.6 %fusion.9 = f32[512,512]{1,0:T(8,128)S(1)} fusion(f32[512,2048]{1,0:T(8,128)} %param.1), kind=kOutput, calls=%fused_computation.40 | convolution fusion | flops 3221225472 | bytes 5242880 | tf_op jit(solution)/shard_map/dot_general | solution.py:23
  65.7 4.2 %collective-permute-start.3 = (f32[512,256]{1,0:T(8,128)}, f32[512,256]{1,0:T(8,128)}, u32[]{:S(2)}, u32[]{:S(2)}) collective-permute-start(f32[512,256]{1,0:T(8,128)} %get-tuple-element.75), channel_id=1, source_target_pairs={{1,0},{3,2},{5,4},{7,6},{8,9},{10,11},{12,13},{14,15},{17,16},{19,... | collective-permute-start | bytes 1572872 | tf_op jit(solution)/shard_map/ppermute | solution.py:50
  69.9 3.2 collective-permute-start.5
  73.1 5.4 %fusion.10 = f32[512,512]{1,0:T(8,128)S(1)} fusion(f32[512,2048]{1,0:T(8,128)} %collective-permute-done, f32[512,2048]{1,0:T(8,128)S(1)} %copy-done), kind=kOutput, calls=%fused_computation.41 | convolution fusion | flops 3221225472 | bytes 9437184 | tf_op jit(solution)/shard_map/dot_general | solution.py:23
  78.9 1.3 collective-permute-start.7
  80.2 1.3 collective-permute-start.9
  81.6 2.6 collective-permute-done.5
  84.1 1.3 slice_add_fusion.15
  86.2 8.3 %collective-permute-done.7 = f32[512,256]{1,0:T(8,128)S(1)} collective-permute-done((f32[512,256]{1,0:T(8,128)S(1)}, f32[512,256]{1,0:T(8,128)S(1)}, u32[]{:S(2)}, u32[]{:S(2)}) %collective-permute-start.7) | collective-permute-done | bytes 524320 | tf_op jit(solution)/shard_map/ppermute | solution.py:50
  96.1 6.6 %collective-permute-start.8 = (f32[512,256]{1,0:T(8,128)S(1)}, f32[512,256]{1,0:T(8,128)S(1)}, u32[]{:S(2)}, u32[]{:S(2)}) collective-permute-start(f32[512,256]{1,0:T(8,128)S(1)} %get-tuple-element.69), channel_id=1, source_target_pairs={{2,0},{7,5},{10,8},{12,14},{19,17},{21,23},{24,26},{29,31}} | collective-permute-start | bytes 1572872 | tf_op jit(solution)/shard_map/ppermute | solution.py:50
  103.0 6.4 %collective-permute-done.8 = f32[512,256]{1,0:T(8,128)S(1)} collective-permute-done((f32[512,256]{1,0:T(8,128)S(1)}, f32[512,256]{1,0:T(8,128)S(1)}, u32[]{:S(2)}, u32[]{:S(2)}) %collective-permute-start.8) | collective-permute-done | bytes 524320 | tf_op jit(solution)/shard_map/ppermute | solution.py:50
  109.8 3.5 %collective-permute-done.2 = f32[512,512]{1,0:T(8,128)S(1)} collective-permute-done((f32[512,512]{1,0:T(8,128)S(1)}, f32[512,512]{1,0:T(8,128)S(1)}, u32[]{:S(2)}, u32[]{:S(2)}) %collective-permute-start.2) | collective-permute-done | bytes 1048608 | tf_op jit(solution)/shard_map/ppermute | solution.py:19
  113.3 11.4 %collective-permute-done.1 = f32[512,2048]{1,0:T(8,128)} collective-permute-done((f32[512,2048]{1,0:T(8,128)}, f32[512,2048]{1,0:T(8,128)}, u32[]{:S(2)}, u32[]{:S(2)}) %collective-permute-start.1) | collective-permute-done | bytes 4194336 | tf_op jit(solution)/shard_map/ppermute | solution.py:19
  125.8 1.3 collective-permute-start.13
  127.0 1.3 collective-permute-start.15
  128.4 6.6 %fusion.11 = f32[512,512]{1,0:T(8,128)} fusion(f32[512,2048]{1,0:T(8,128)} %collective-permute-done.1, f32[512,2048]{1,0:T(8,128)S(1)} %copy-done.1), kind=kOutput, calls=%fused_computation.42 | convolution fusion | flops 3221225472 | bytes 9437184 | tf_op jit(solution)/shard_map/dot_general | solution.py:23
  135.0 1.6 copy.7
  136.6 1.4 collective-permute-start.17
  138.1 5.4 %collective-permute-start.19 = (f32[512,256]{1,0:T(8,128)S(1)}, f32[512,256]{1,0:T(8,128)S(1)}, u32[]{:S(2)}, u32[]{:S(2)}) collective-permute-start(f32[512,256]{1,0:T(8,128)S(1)} %get-tuple-element.64), channel_id=1, source_target_pairs={{2,0},{3,1},{4,6},{5,7},{10,8},{11,9},{12,14},{13,15},{18,16},{19,... | collective-permute-start | bytes 1572872 | tf_op jit(solution)/shard_map/ppermute | solution.py:50
  143.5 1.7 slice_add_fusion.13
  145.1 1.3 collective-permute-start.16
  146.4 10.3 %collective-permute-start.12 = (f32[512,512]{1,0:T(8,128)S(1)}, f32[512,512]{1,0:T(8,128)}, u32[]{:S(2)}, u32[]{:S(2)}) collective-permute-start(f32[512,512]{1,0:T(8,128)S(1)} %copy-done.10), channel_id=1, source_target_pairs={{0,12},{8,4},{16,0},{24,8},{28,16},{20,24},{12,28},{4,20},{1,13},{... | collective-permute-start | bytes 3145736 | tf_op jit(solution)/shard_map/ppermute | solution.py:19
  156.8 1.3 collective-permute-start.14
  158.9 5.2 %collective-permute-start.18 = (f32[512,256]{1,0:T(8,128)S(1)}, f32[512,256]{1,0:T(8,128)S(1)}, u32[]{:S(2)}, u32[]{:S(2)}) collective-permute-start(f32[512,256]{1,0:T(8,128)S(1)} %get-tuple-element.61), channel_id=1, source_target_pairs={{3,1},{4,6},{10,8},{13,15},{18,16},{21,23},{27,25},{28,30}} | collective-permute-start | bytes 1572872 | tf_op jit(solution)/shard_map/ppermute | solution.py:50
  164.2 3.6 %collective-permute-done.14 = f32[512,256]{1,0:T(8,128)S(1)} collective-permute-done((f32[512,256]{1,0:T(8,128)S(1)}, f32[512,256]{1,0:T(8,128)S(1)}, u32[]{:S(2)}, u32[]{:S(2)}) %collective-permute-start.14) | collective-permute-done | bytes 524320 | tf_op jit(solution)/shard_map/ppermute | solution.py:50
  168.0 2.8 collective-permute-done.18
  173.1 17.1 %collective-permute-done.12 = f32[512,512]{1,0:T(8,128)} collective-permute-done((f32[512,512]{1,0:T(8,128)S(1)}, f32[512,512]{1,0:T(8,128)}, u32[]{:S(2)}, u32[]{:S(2)}) %collective-permute-start.12) | collective-permute-done | bytes 1048608 | tf_op jit(solution)/shard_map/ppermute | solution.py:19
  190.2 3.3 collective-permute-done.11
  193.5 2.5 collective-permute-start.21
  196.0 6.7 %fusion.12 = f32[512,512]{1,0:T(8,128)} fusion(f32[512,2048]{1,0:T(8,128)} %collective-permute-done.11, f32[512,2048]{1,0:T(8,128)S(1)} %copy-done.2), kind=kOutput, calls=%fused_computation.43 | convolution fusion | flops 3221225472 | bytes 9437184 | tf_op jit(solution)/shard_map/dot_general | solution.py:23
  202.7 5.0 %collective-permute-start.26 = (f32[512,512]{1,0:T(8,128)}, f32[512,512]{1,0:T(8,128)}, u32[]{:S(2)}, u32[]{:S(2)}) collective-permute-start(f32[512,512]{1,0:T(8,128)} %fusion.12), channel_id=1, source_target_pairs={{0,20},{8,12},{16,4},{24,0},{28,8},{20,16},{12,24},{4,28},{1,21},{... | collective-permute-start | bytes 3145736 | tf_op jit(solution)/shard_map/ppermute | solution.py:19
  207.7 1.6 copy.8
  209.3 1.3 fusion.4
  210.5 3.4 %collective-permute-start.22 = (f32[512,256]{1,0:T(8,128)S(1)}, f32[512,256]{1,0:T(8,128)S(1)}, u32[]{:S(2)}, u32[]{:S(2)}) collective-permute-start(f32[512,256]{1,0:T(8,128)S(1)} %get-tuple-element.59), channel_id=1, source_target_pairs={{1,0},{3,2},{4,5},{6,7},{8,9},{10,11},{13,12},{15,14},{16,17},{18,... | collective-permute-start | bytes 1572872 | tf_op jit(solution)/shard_map/ppermute | solution.py:50
  213.9 1.3 collective-permute-start.24
  215.3 1.3 collective-permute-start.31
  216.7 47.3 %collective-permute-done.26 = f32[512,512]{1,0:T(8,128)} collective-permute-done((f32[512,512]{1,0:T(8,128)}, f32[512,512]{1,0:T(8,128)}, u32[]{:S(2)}, u32[]{:S(2)}) %collective-permute-start.26) | collective-permute-done | bytes 1048608 | tf_op jit(solution)/shard_map/ppermute | solution.py:19
  264.0 2.4 collective-permute-start.33
  266.4 1.3 fusion.3
  267.7 3.4 %collective-permute-start.27 = (f32[512,256]{1,0:T(8,128)S(1)}, f32[512,256]{1,0:T(8,128)S(1)}, u32[]{:S(2)}, u32[]{:S(2)}) collective-permute-start(f32[512,256]{1,0:T(8,128)S(1)} %get-tuple-element.55), channel_id=1, source_target_pairs={{0,1},{2,3},{5,4},{7,6},{8,9},{10,11},{12,13},{14,15},{17,16},{19,... | collective-permute-start | bytes 1572872 | tf_op jit(solution)/shard_map/ppermute | solution.py:50
  271.2 1.3 collective-permute-start.29
  272.5 1.3 slice_add_fusion.11
  273.8 1.3 collective-permute-start.25
  276.0 1.8 collective-permute-done.27
  278.5 3.7 %collective-permute-done.29 = f32[512,256]{1,0:T(8,128)S(1)} collective-permute-done((f32[512,256]{1,0:T(8,128)S(1)}, f32[512,256]{1,0:T(8,128)S(1)}, u32[]{:S(2)}, u32[]{:S(2)}) %collective-permute-start.29) | collective-permute-done | bytes 524320 | tf_op jit(solution)/shard_map/ppermute | solution.py:50
  282.9 1.3 slice_add_fusion.5
  284.3 4.1 %collective-permute-start.30 = (f32[512,256]{1,0:T(8,128)S(1)}, f32[512,256]{1,0:T(8,128)S(1)}, u32[]{:S(2)}, u32[]{:S(2)}) collective-permute-start(f32[512,256]{1,0:T(8,128)S(1)} %get-tuple-element.54), channel_id=1, source_target_pairs={{2,3},{7,6},{10,11},{12,13},{19,18},{21,20},{24,25},{29,28}} | collective-permute-start | bytes 1572872 | tf_op jit(solution)/shard_map/ppermute | solution.py:50
  289.4 1.2 pad_maximum_fusion.4
  291.8 3.3 collective-permute-done.30
  296.3 5.8 %convolution_bitcast_fusion = f32[512,512]{1,0:T(8,128)S(1)} fusion(f32[512,2048]{1,0:T(8,128)} %collective-permute-done.21, f32[512,2048]{1,0:T(8,128)S(1)} %copy-done.3), kind=kOutput, calls=%fused_computation.3 | convolution fusion | flops 3221225472 | bytes 9437184 | tf_op jit(solution)/shard_map/dot_general | solution.py:23
  302.2 1.4 collective-permute-start.35
  303.6 1.3 collective-permute-start.37
  304.9 13.5 %collective-permute-done.35 = f32[512,256]{1,0:T(8,128)S(1)} collective-permute-done((f32[512,256]{1,0:T(8,128)S(1)}, f32[512,256]{1,0:T(8,128)S(1)}, u32[]{:S(2)}, u32[]{:S(2)}) %collective-permute-start.35) | collective-permute-done | bytes 524320 | tf_op jit(solution)/shard_map/ppermute | solution.py:50
  318.4 1.1 slice_add_fusion.1
  319.6 1.3 collective-permute-start.38
  320.9 1.5 collective-permute-start.36
  322.5 9.8 %collective-permute-done.38 = f32[512,256]{1,0:T(8,128)} collective-permute-done((f32[512,256]{1,0:T(8,128)}, f32[512,256]{1,0:T(8,128)}, u32[]{:S(2)}, u32[]{:S(2)}) %collective-permute-start.38) | collective-permute-done | bytes 524320 | tf_op jit(solution)/shard_map/ppermute | solution.py:50
  332.3 1.3 add.186
  333.6 1.3 add.184
  338.0 1.6 fusion
  (91 shorter events, 17.7 us)
Async XLA Ops:
  0.0 64.6 %collective-permute-start = (f32[512,2048]{1,0:T(8,128)}, f32[512,2048]{1,0:T(8,128)}, u32[]{:S(2)}, u32[]{:S(2)}) collective-permute-start(f32[512,2048]{1,0:T(8,128)} %param.1), channel_id=1, source_target_pairs={{0,8},{8,16},{16,24},{24,28},{28,20},{20,12},{12,4},{4,0},{1,9},{9... | collective-permute-start | bytes 12582920 | tf_op jit(solution)/shard_map/ppermute | solution.py:19
  57.0 16.1 %copy-start = (f32[512,2048]{1,0:T(8,128)S(1)}, f32[512,2048]{1,0:T(8,128)}, u32[]{:S(2)}) copy-start(f32[512,2048]{1,0:T(8,128)} %param.1) | copy-start | bytes 12582916
  64.6 60.1 %collective-permute-start.1 = (f32[512,2048]{1,0:T(8,128)}, f32[512,2048]{1,0:T(8,128)}, u32[]{:S(2)}, u32[]{:S(2)}) collective-permute-start(f32[512,2048]{1,0:T(8,128)} %collective-permute-done), channel_id=1, source_target_pairs={{0,8},{8,16},{16,24},{24,28},{28,20},{20,12},{12,4},{4,0},{1,9},{9... | collective-permute-start | bytes 12582920 | tf_op jit(solution)/shard_map/ppermute | solution.py:19
  65.7 15.8 %collective-permute-start.3 = (f32[512,256]{1,0:T(8,128)}, f32[512,256]{1,0:T(8,128)}, u32[]{:S(2)}, u32[]{:S(2)}) collective-permute-start(f32[512,256]{1,0:T(8,128)} %get-tuple-element.75), channel_id=1, source_target_pairs={{1,0},{3,2},{5,4},{7,6},{8,9},{10,11},{12,13},{14,15},{17,16},{19,... | collective-permute-start | bytes 1572872 | tf_op jit(solution)/shard_map/ppermute | solution.py:50
  69.9 14.2 %collective-permute-start.5 = (f32[512,256]{1,0:T(8,128)}, f32[512,256]{1,0:T(8,128)}, u32[]{:S(2)}, u32[]{:S(2)}) collective-permute-start(f32[512,256]{1,0:T(8,128)} %get-tuple-element.76), channel_id=1, source_target_pairs={{2,0},{3,1},{6,4},{7,5},{10,8},{11,9},{14,12},{15,13},{16,18},{17,... | collective-permute-start | bytes 1572872 | tf_op jit(solution)/shard_map/ppermute | solution.py:50
  78.9 15.6 %collective-permute-start.7 = (f32[512,256]{1,0:T(8,128)S(1)}, f32[512,256]{1,0:T(8,128)S(1)}, u32[]{:S(2)}, u32[]{:S(2)}) collective-permute-start(f32[512,256]{1,0:T(8,128)S(1)} %get-tuple-element.71), channel_id=1, source_target_pairs={{1,0},{3,2},{4,5},{6,7},{9,8},{11,10},{13,12},{15,14},{16,17},{18,... | collective-permute-start | bytes 1572872 | tf_op jit(solution)/shard_map/ppermute | solution.py:50
  80.2 15.0 %collective-permute-start.9 = (f32[512,256]{1,0:T(8,128)S(1)}, f32[512,256]{1,0:T(8,128)S(1)}, u32[]{:S(2)}, u32[]{:S(2)}) collective-permute-start(f32[512,256]{1,0:T(8,128)S(1)} %get-tuple-element.72), channel_id=1, source_target_pairs={{2,0},{3,1},{6,4},{7,5},{10,8},{11,9},{12,14},{13,15},{18,16},{19,... | collective-permute-start | bytes 1572872 | tf_op jit(solution)/shard_map/ppermute | solution.py:50
  85.5 10.6 %collective-permute-start.6 = (f32[512,256]{1,0:T(8,128)S(1)}, f32[512,256]{1,0:T(8,128)S(1)}, u32[]{:S(2)}, u32[]{:S(2)}) collective-permute-start(f32[512,256]{1,0:T(8,128)S(1)} %get-tuple-element.74), channel_id=1, source_target_pairs={{1,0},{5,4},{8,9},{12,13},{19,18},{23,22},{26,27},{30,31}} | collective-permute-start | bytes 1572872 | tf_op jit(solution)/shard_map/ppermute | solution.py:50
  86.2 27.1 %collective-permute-start.2 = (f32[512,512]{1,0:T(8,128)S(1)}, f32[512,512]{1,0:T(8,128)S(1)}, u32[]{:S(2)}, u32[]{:S(2)}) collective-permute-start(f32[512,512]{1,0:T(8,128)S(1)} %fusion.10), channel_id=1, source_target_pairs={{0,4},{8,0},{16,8},{24,16},{28,24},{20,28},{12,20},{4,12},{1,5},{9... | collective-permute-start | bytes 3145736 | tf_op jit(solution)/shard_map/ppermute | solution.py:19
  94.5 8.3 %collective-permute-start.4 = (f32[512,256]{1,0:T(8,128)S(1)}, f32[512,256]{1,0:T(8,128)S(1)}, u32[]{:S(2)}, u32[]{:S(2)}) collective-permute-start(f32[512,256]{1,0:T(8,128)S(1)} %get-tuple-element.73), channel_id=1, source_target_pairs={{2,0},{6,4},{11,9},{15,13},{16,18},{20,22},{25,27},{29,31}} | collective-permute-start | bytes 1572872 | tf_op jit(solution)/shard_map/ppermute | solution.py:50
  95.4 7.5 %collective-permute-start.10 = (f32[512,256]{1,0:T(8,128)S(1)}, f32[512,256]{1,0:T(8,128)S(1)}, u32[]{:S(2)}, u32[]{:S(2)}) collective-permute-start(f32[512,256]{1,0:T(8,128)S(1)} %get-tuple-element.70), channel_id=1, source_target_pairs={{1,0},{4,5},{9,8},{15,14},{16,17},{22,23},{27,26},{30,31}} | collective-permute-start | bytes 1572872 | tf_op jit(solution)/shard_map/ppermute | solution.py:50
  96.1 13.3 %collective-permute-start.8 = (f32[512,256]{1,0:T(8,128)S(1)}, f32[512,256]{1,0:T(8,128)S(1)}, u32[]{:S(2)}, u32[]{:S(2)}) collective-permute-start(f32[512,256]{1,0:T(8,128)S(1)} %get-tuple-element.69), channel_id=1, source_target_pairs={{2,0},{7,5},{10,8},{12,14},{19,17},{21,23},{24,26},{29,31}} | collective-permute-start | bytes 1572872 | tf_op jit(solution)/shard_map/ppermute | solution.py:50
  103.0 25.4 %copy-start.1 = (f32[512,2048]{1,0:T(8,128)S(1)}, f32[512,2048]{1,0:T(8,128)}, u32[]{:S(2)}) copy-start(f32[512,2048]{1,0:T(8,128)} %param.1) | copy-start | bytes 12582916
  113.3 11.4 %copy-start.9 = (f32[512,512]{1,0:T(8,128)}, f32[512,512]{1,0:T(8,128)S(1)}, u32[]{:S(2)}) copy-start(f32[512,512]{1,0:T(8,128)S(1)} %collective-permute-done.2) | copy-start | bytes 3145732
  124.7 68.8 %collective-permute-start.11 = (f32[512,2048]{1,0:T(8,128)}, f32[512,2048]{1,0:T(8,128)}, u32[]{:S(2)}, u32[]{:S(2)}) collective-permute-start(f32[512,2048]{1,0:T(8,128)} %collective-permute-done.1), channel_id=1, source_target_pairs={{0,8},{8,16},{16,24},{24,28},{28,20},{20,12},{12,4},{4,0},{1,9},{9... | collective-permute-start | bytes 12582920 | tf_op jit(solution)/shard_map/ppermute | solution.py:19
  125.8 17.7 %collective-permute-start.13 = (f32[512,256]{1,0:T(8,128)}, f32[512,256]{1,0:T(8,128)}, u32[]{:S(2)}, u32[]{:S(2)}) collective-permute-start(f32[512,256]{1,0:T(8,128)} %get-tuple-element.67), channel_id=1, source_target_pairs={{0,1},{2,3},{5,4},{7,6},{9,8},{11,10},{13,12},{15,14},{16,17},{18,... | collective-permute-start | bytes 1572872 | tf_op jit(solution)/shard_map/ppermute | solution.py:50
  127.0 16.4 %collective-permute-start.15 = (f32[512,256]{1,0:T(8,128)}, f32[512,256]{1,0:T(8,128)}, u32[]{:S(2)}, u32[]{:S(2)}) collective-permute-start(f32[512,256]{1,0:T(8,128)} %get-tuple-element.68), channel_id=1, source_target_pairs={{2,0},{3,1},{6,4},{7,5},{8,10},{9,11},{14,12},{15,13},{16,18},{17,... | collective-permute-start | bytes 1572872 | tf_op jit(solution)/shard_map/ppermute | solution.py:50
  136.6 9.9 %copy-start.10 = (f32[512,512]{1,0:T(8,128)S(1)}, f32[512,512]{1,0:T(8,128)}, u32[]{:S(2)}) copy-start(f32[512,512]{1,0:T(8,128)} %fusion.11) | copy-start | bytes 3145732
  136.6 20.1 %collective-permute-start.17 = (f32[512,256]{1,0:T(8,128)S(1)}, f32[512,256]{1,0:T(8,128)S(1)}, u32[]{:S(2)}, u32[]{:S(2)}) collective-permute-start(f32[512,256]{1,0:T(8,128)S(1)} %get-tuple-element.63), channel_id=1, source_target_pairs={{0,1},{2,3},{5,4},{7,6},{9,8},{11,10},{12,13},{14,15},{17,16},{19,... | collective-permute-start | bytes 1572872 | tf_op jit(solution)/shard_map/ppermute | solution.py:50
  138.1 20.0 %collective-permute-start.19 = (f32[512,256]{1,0:T(8,128)S(1)}, f32[512,256]{1,0:T(8,128)S(1)}, u32[]{:S(2)}, u32[]{:S(2)}) collective-permute-start(f32[512,256]{1,0:T(8,128)S(1)} %get-tuple-element.64), channel_id=1, source_target_pairs={{2,0},{3,1},{4,6},{5,7},{10,8},{11,9},{12,14},{13,15},{18,16},{19,... | collective-permute-start | bytes 1572872 | tf_op jit(solution)/shard_map/ppermute | solution.py:50
  145.1 13.8 %collective-permute-start.16 = (f32[512,256]{1,0:T(8,128)S(1)}, f32[512,256]{1,0:T(8,128)S(1)}, u32[]{:S(2)}, u32[]{:S(2)}) collective-permute-start(f32[512,256]{1,0:T(8,128)S(1)} %get-tuple-element.66), channel_id=1, source_target_pairs={{0,1},{5,4},{11,10},{13,12},{18,19},{20,21},{26,27},{31,30}} | collective-permute-start | bytes 1572872 | tf_op jit(solution)/shard_map/ppermute | solution.py:50
  146.4 43.8 %collective-permute-start.12 = (f32[512,512]{1,0:T(8,128)S(1)}, f32[512,512]{1,0:T(8,128)}, u32[]{:S(2)}, u32[]{:S(2)}) collective-permute-start(f32[512,512]{1,0:T(8,128)S(1)} %copy-done.10), channel_id=1, source_target_pairs={{0,12},{8,4},{16,0},{24,8},{28,16},{20,24},{12,28},{4,20},{1,13},{... | collective-permute-start | bytes 3145736 | tf_op jit(solution)/shard_map/ppermute | solution.py:19
  156.8 11.1 %collective-permute-start.14 = (f32[512,256]{1,0:T(8,128)S(1)}, f32[512,256]{1,0:T(8,128)S(1)}, u32[]{:S(2)}, u32[]{:S(2)}) collective-permute-start(f32[512,256]{1,0:T(8,128)S(1)} %get-tuple-element.65), channel_id=1, source_target_pairs={{3,1},{6,4},{8,10},{14,12},{17,19},{23,21},{25,27},{28,30}} | collective-permute-start | bytes 1572872 | tf_op jit(solution)/shard_map/ppermute | solution.py:50
  158.2 9.7 %collective-permute-start.20 = (f32[512,256]{1,0:T(8,128)S(1)}, f32[512,256]{1,0:T(8,128)S(1)}, u32[]{:S(2)}, u32[]{:S(2)}) collective-permute-start(f32[512,256]{1,0:T(8,128)S(1)} %get-tuple-element.62), channel_id=1, source_target_pairs={{0,1},{7,6},{9,8},{14,15},{17,16},{22,23},{24,25},{31,30}} | collective-permute-start | bytes 1572872 | tf_op jit(solution)/shard_map/ppermute | solution.py:50
  158.9 11.9 %collective-permute-start.18 = (f32[512,256]{1,0:T(8,128)S(1)}, f32[512,256]{1,0:T(8,128)S(1)}, u32[]{:S(2)}, u32[]{:S(2)}) collective-permute-start(f32[512,256]{1,0:T(8,128)S(1)} %get-tuple-element.61), channel_id=1, source_target_pairs={{3,1},{4,6},{10,8},{13,15},{18,16},{21,23},{27,25},{28,30}} | collective-permute-start | bytes 1572872 | tf_op jit(solution)/shard_map/ppermute | solution.py:50
  164.2 31.8 %copy-start.2 = (f32[512,2048]{1,0:T(8,128)S(1)}, f32[512,2048]{1,0:T(8,128)}, u32[]{:S(2)}) copy-start(f32[512,2048]{1,0:T(8,128)} %param.1) | copy-start | bytes 12582916
  193.5 102.8 %collective-permute-start.21 = (f32[512,2048]{1,0:T(8,128)}, f32[512,2048]{1,0:T(8,128)}, u32[]{:S(2)}, u32[]{:S(2)}) collective-permute-start(f32[512,2048]{1,0:T(8,128)} %collective-permute-done.11), channel_id=1, source_target_pairs={{0,8},{8,16},{16,24},{24,28},{28,20},{20,12},{12,4},{4,0},{1,9},{9... | collective-permute-start | bytes 12582920 | tf_op jit(solution)/shard_map/ppermute | solution.py:19
  202.7 61.3 %collective-permute-start.26 = (f32[512,512]{1,0:T(8,128)}, f32[512,512]{1,0:T(8,128)}, u32[]{:S(2)}, u32[]{:S(2)}) collective-permute-start(f32[512,512]{1,0:T(8,128)} %fusion.12), channel_id=1, source_target_pairs={{0,20},{8,12},{16,4},{24,0},{28,8},{20,16},{12,24},{4,28},{1,21},{... | collective-permute-start | bytes 3145736 | tf_op jit(solution)/shard_map/ppermute | solution.py:19
  210.5 57.2 %collective-permute-start.22 = (f32[512,256]{1,0:T(8,128)S(1)}, f32[512,256]{1,0:T(8,128)S(1)}, u32[]{:S(2)}, u32[]{:S(2)}) collective-permute-start(f32[512,256]{1,0:T(8,128)S(1)} %get-tuple-element.59), channel_id=1, source_target_pairs={{1,0},{3,2},{4,5},{6,7},{8,9},{10,11},{13,12},{15,14},{16,17},{18,... | collective-permute-start | bytes 1572872 | tf_op jit(solution)/shard_map/ppermute | solution.py:50
  213.9 57.2 %collective-permute-start.24 = (f32[512,256]{1,0:T(8,128)S(1)}, f32[512,256]{1,0:T(8,128)S(1)}, u32[]{:S(2)}, u32[]{:S(2)}) collective-permute-start(f32[512,256]{1,0:T(8,128)S(1)} %get-tuple-element.60), channel_id=1, source_target_pairs={{0,2},{1,3},{6,4},{7,5},{8,10},{9,11},{14,12},{15,13},{16,18},{17,... | collective-permute-start | bytes 1572872 | tf_op jit(solution)/shard_map/ppermute | solution.py:50
  215.3 58.5 %collective-permute-start.31 = (f32[512,256]{1,0:T(8,128)S(1)}, f32[512,256]{1,0:T(8,128)S(1)}, u32[]{:S(2)}, u32[]{:S(2)}) collective-permute-start(f32[512,256]{1,0:T(8,128)S(1)} %get-tuple-element.51), channel_id=1, source_target_pairs={{1,0},{3,2},{4,5},{6,7},{8,9},{10,11},{12,13},{14,15},{17,16},{19,... | collective-permute-start | bytes 1572872 | tf_op jit(solution)/shard_map/ppermute | solution.py:50
  264.0 11.2 %collective-permute-start.33 = (f32[512,256]{1,0:T(8,128)S(1)}, f32[512,256]{1,0:T(8,128)S(1)}, u32[]{:S(2)}, u32[]{:S(2)}) collective-permute-start(f32[512,256]{1,0:T(8,128)S(1)} %get-tuple-element.52), channel_id=1, source_target_pairs={{0,2},{1,3},{4,6},{5,7},{10,8},{11,9},{12,14},{13,15},{18,16},{19,... | collective-permute-start | bytes 1572872 | tf_op jit(solution)/shard_map/ppermute | solution.py:50
  267.7 10.1 %collective-permute-start.27 = (f32[512,256]{1,0:T(8,128)S(1)}, f32[512,256]{1,0:T(8,128)S(1)}, u32[]{:S(2)}, u32[]{:S(2)}) collective-permute-start(f32[512,256]{1,0:T(8,128)S(1)} %get-tuple-element.55), channel_id=1, source_target_pairs={{0,1},{2,3},{5,4},{7,6},{8,9},{10,11},{12,13},{14,15},{17,16},{19,... | collective-permute-start | bytes 1572872 | tf_op jit(solution)/shard_map/ppermute | solution.py:50
  271.2 11.1 %collective-permute-start.29 = (f32[512,256]{1,0:T(8,128)S(1)}, f32[512,256]{1,0:T(8,128)S(1)}, u32[]{:S(2)}, u32[]{:S(2)}) collective-permute-start(f32[512,256]{1,0:T(8,128)S(1)} %get-tuple-element.56), channel_id=1, source_target_pairs={{0,2},{1,3},{4,6},{5,7},{8,10},{9,11},{14,12},{15,13},{16,18},{17,... | collective-permute-start | bytes 1572872 | tf_op jit(solution)/shard_map/ppermute | solution.py:50
  273.8 10.5 %collective-permute-start.25 = (f32[512,256]{1,0:T(8,128)S(1)}, f32[512,256]{1,0:T(8,128)S(1)}, u32[]{:S(2)}, u32[]{:S(2)}) collective-permute-start(f32[512,256]{1,0:T(8,128)S(1)} %get-tuple-element.58), channel_id=1, source_target_pairs={{3,2},{4,5},{10,11},{13,12},{18,19},{21,20},{27,26},{28,29}} | collective-permute-start | bytes 1572872 | tf_op jit(solution)/shard_map/ppermute | solution.py:50
  275.2 13.2 %collective-permute-start.23 = (f32[512,256]{1,0:T(8,128)S(1)}, f32[512,256]{1,0:T(8,128)S(1)}, u32[]{:S(2)}, u32[]{:S(2)}) collective-permute-start(f32[512,256]{1,0:T(8,128)S(1)} %get-tuple-element.57), channel_id=1, source_target_pairs={{0,2},{7,5},{9,11},{14,12},{17,19},{22,20},{24,26},{31,29}} | collective-permute-start | bytes 1572872 | tf_op jit(solution)/shard_map/ppermute | solution.py:50
  277.8 11.4 %collective-permute-start.34 = (f32[512,256]{1,0:T(8,128)S(1)}, f32[512,256]{1,0:T(8,128)S(1)}, u32[]{:S(2)}, u32[]{:S(2)}) collective-permute-start(f32[512,256]{1,0:T(8,128)S(1)} %get-tuple-element.50), channel_id=1, source_target_pairs={{3,2},{6,7},{8,9},{14,15},{17,16},{23,22},{25,24},{28,29}} | collective-permute-start | bytes 1572872 | tf_op jit(solution)/shard_map/ppermute | solution.py:50
  282.2 7.1 %collective-permute-start.32 = (f32[512,256]{1,0:T(8,128)S(1)}, f32[512,256]{1,0:T(8,128)S(1)}, u32[]{:S(2)}, u32[]{:S(2)}) collective-permute-start(f32[512,256]{1,0:T(8,128)S(1)} %get-tuple-element.49), channel_id=1, source_target_pairs={{0,2},{5,7},{11,9},{13,15},{18,16},{20,22},{26,24},{31,29}} | collective-permute-start | bytes 1572872 | tf_op jit(solution)/shard_map/ppermute | solution.py:50
  284.3 10.7 %collective-permute-start.30 = (f32[512,256]{1,0:T(8,128)S(1)}, f32[512,256]{1,0:T(8,128)S(1)}, u32[]{:S(2)}, u32[]{:S(2)}) collective-permute-start(f32[512,256]{1,0:T(8,128)S(1)} %get-tuple-element.54), channel_id=1, source_target_pairs={{2,3},{7,6},{10,11},{12,13},{19,18},{21,20},{24,25},{29,28}} | collective-permute-start | bytes 1572872 | tf_op jit(solution)/shard_map/ppermute | solution.py:50
  288.4 6.7 %collective-permute-start.28 = (f32[512,256]{1,0:T(8,128)S(1)}, f32[512,256]{1,0:T(8,128)S(1)}, u32[]{:S(2)}, u32[]{:S(2)}) collective-permute-start(f32[512,256]{1,0:T(8,128)S(1)} %get-tuple-element.53), channel_id=1, source_target_pairs={{1,3},{4,6},{9,11},{15,13},{16,18},{22,20},{27,25},{30,28}} | collective-permute-start | bytes 1572872 | tf_op jit(solution)/shard_map/ppermute | solution.py:50
  289.4 6.9 %copy-start.3 = (f32[512,2048]{1,0:T(8,128)S(1)}, f32[512,2048]{1,0:T(8,128)}, u32[]{:S(2)}) copy-start(f32[512,2048]{1,0:T(8,128)} %param.1) | copy-start | bytes 12582916
  302.1 32.7 %copy-start.4 = (f32[512,512]{1,0:T(8,128)S(1)}, f32[512,512]{1,0:T(8,128)}, u32[]{:S(2)}) copy-start(f32[512,512]{1,0:T(8,128)} %pad_maximum_fusion.2) | copy-start | bytes 3145732
  302.2 16.2 %collective-permute-start.35 = (f32[512,256]{1,0:T(8,128)S(1)}, f32[512,256]{1,0:T(8,128)S(1)}, u32[]{:S(2)}, u32[]{:S(2)}) collective-permute-start(f32[512,256]{1,0:T(8,128)S(1)} %get-tuple-element.47), channel_id=1, source_target_pairs={{0,1},{2,3},{4,5},{6,7},{9,8},{11,10},{13,12},{15,14},{16,17},{18,... | collective-permute-start | bytes 1572872 | tf_op jit(solution)/shard_map/ppermute | solution.py:50
  303.6 14.8 %collective-permute-start.37 = (f32[512,256]{1,0:T(8,128)S(1)}, f32[512,256]{1,0:T(8,128)S(1)}, u32[]{:S(2)}, u32[]{:S(2)}) collective-permute-start(f32[512,256]{1,0:T(8,128)S(1)} %get-tuple-element.48), channel_id=1, source_target_pairs={{0,2},{1,3},{4,6},{5,7},{8,10},{9,11},{12,14},{13,15},{18,16},{19,... | collective-permute-start | bytes 1572872 | tf_op jit(solution)/shard_map/ppermute | solution.py:50
  319.6 12.7 %collective-permute-start.38 = (f32[512,256]{1,0:T(8,128)}, f32[512,256]{1,0:T(8,128)}, u32[]{:S(2)}, u32[]{:S(2)}) collective-permute-start(f32[512,256]{1,0:T(8,128)} %get-tuple-element.46), channel_id=1, source_target_pairs={{2,3},{6,7},{11,10},{15,14},{16,17},{20,21},{25,24},{29,28}} | collective-permute-start | bytes 1572872 | tf_op jit(solution)/shard_map/ppermute | solution.py:50
  320.9 12.7 %collective-permute-start.36 = (f32[512,256]{1,0:T(8,128)}, f32[512,256]{1,0:T(8,128)}, u32[]{:S(2)}, u32[]{:S(2)}) collective-permute-start(f32[512,256]{1,0:T(8,128)} %get-tuple-element.45), channel_id=1, source_target_pairs={{1,3},{5,7},{8,10},{12,14},{19,17},{23,21},{26,24},{30,28}} | collective-permute-start | bytes 1572872 | tf_op jit(solution)/shard_map/ppermute | solution.py:50
  334.8 1.2 copy-start.5
  334.9 1.5 copy-start.6
  334.9 1.8 copy-start.7
  334.9 2.1 copy-start.8

commit v6 on v5

--- a/solution.py
+++ b/solution.py
@@ -61,9 +61,8 @@
     held = passed_along(grads, "blk", 1)
     squares = lax.psum(jnp.sum(grads * grads, axis=1), "feat")
     every = lax.all_gather(squares, "blk", axis=0, tiled=True)
-    piece = tile_of(grads, grads)
-    held, squares, every, piece = lax.optimization_barrier((held, squares, every, piece))
-    waiting = (0, piece)
+    grads, held, squares, every = lax.optimization_barrier((grads, held, squares, every))
+    waiting = (0, tile_of(grads, grads))
     for step in range(1, half + 1):
         piece = tile_of(grads, held)
         shift = (blocks - step) % blocks
@@ -73,9 +72,8 @@
             sums[waiting[0]] = summed_at(waiting[1], waiting[0])
             sums[shift] = summed_at(piece, shift)
             if step == half - 1:
+                held, sums = lax.optimization_barrier((coming, sums))
                 sums[step] = summed_at(back, step)
-                coming, sums = lax.optimization_barrier((coming, sums))
-                held = coming
                 continue
             held, back, sums[waiting[0]], sums[shift] = lax.optimization_barrier(
                 (coming, back, sums[waiting[0]], sums[shift])

time: 343 us -> 317 us (0.924)
  waiting for transfers between devices: 139 us -> 111 us
  starting transfers between devices: 82.8 us -> 88.9 us
  matrix products: 32.1 us -> 28.2 us
  other arithmetic: 22.8 us -> 26.3 us
    ppermute x7, waiting for transfers between devices: 82.7 us -> 65.8 us  [passed_along(): return lax.ppermute(value, axis, pairs)]
    ppermute x32, waiting for transfers between devices: 55.9 us -> 45 us  [summed_at(): value = value + lax.ppermute(value, ('blk', 'feat'), pairs)]
    add x24, other arithmetic: 10.7 us -> 17 us  [summed_at(): value = value + lax.ppermute(value, ('blk', 'feat'), pairs)]
    ppermute x32, starting transfers between devices: 63.4 us -> 67.9 us  [summed_at(): value = value + lax.ppermute(value, ('blk', 'feat'), pairs)]
    dot_general x5, matrix products: 32.1 us -> 28.2 us  [tile_of(): lax.dot_general(left, right, (((1,), (1,)), ((), ())), precision=lax.Prec...]
  transfers between devices with their start and end apart: 39 -> 39, of which waited for: 15 -> 15; matrix products, arithmetic and copies ran while one was open for 15% -> 18% of each run, Pallas kernels for 0% -> 0%
where the time goes in v6:
time: 317 us; the launch traced here: 316 us
  waiting for transfers between devices  111 us (35%)
  starting transfers between devices  88.9 us (28%)
  blocking collectives  52.8 us (17%)
  matrix products  28.2 us (9%)
  other arithmetic  26.3 us (8%)
  local copies, waits for them, and re-layouts  8.28 us (3%)
    ppermute x32, starting transfers between devices, summed_at(): value = value + lax.ppermute(value, ('blk', 'feat'), pairs)  67.9 us
    ppermute x7, waiting for transfers between devices, passed_along(): return lax.ppermute(value, axis, pairs)  65.8 us
    ppermute x32, waiting for transfers between devices, summed_at(): value = value + lax.ppermute(value, ('blk', 'feat'), pairs)  45 us
    all_gather x1, blocking collectives, local(): every = lax.all_gather(squares, 'blk', axis=0, tiled=True)  43.9 us
    dot_general x5, matrix products, tile_of(): lax.dot_general(left, right, (((1,), (1,)), ((), ())), precision=lax.Prec...  28.2 us
    ppermute x7, starting transfers between devices, passed_along(): return lax.ppermute(value, axis, pairs)  21 us
    add x24, other arithmetic, summed_at(): value = value + lax.ppermute(value, ('blk', 'feat'), pairs)  17 us
    psum x1, blocking collectives, local(): squares = lax.psum(jnp.sum(grads * grads, axis=1), 'feat')  8.96 us
  transfers between devices with their start and end apart: 39, of which 15 were waited for; matrix products, arithmetic and copies ran while one was open for 18% of the time, Pallas kernels for 0%

profile of v6, /device:TPU:12, one launch (start us, length us, event | category | flops | bytes accessed | tf_op | source)
XLA Modules:
  0.0 316.2 jit_solution(8473726502165618709)
XLA Ops:
  0.0 1.6 collective-permute-start
  1.6 2.6 multiply_reduce_fusion
  4.1 9.0 %psum.7 = f32[512]{0:T(512)S(1)} all-reduce(f32[512]{0:T(512)S(1)} %multiply_reduce_fusion), channel_id=1, replica_groups=mesh['blk'=8,'feat'=4] {'feat'}, use_global_device_ids=true, to_apply=%region_1.0 | all-reduce | flops 512 | bytes 4096 | tf_op jit(solution)/shard_map/psum | solution.py:62
  13.1 43.9 %all-gather = f32[8,1,512]{2,1,0:T(1,128)S(1)} all-gather(f32[1,1,512]{2,1,0:T(1,128)S(1)} %bitcast.19), channel_id=1, replica_groups=mesh['blk'=8,'feat'=4] {'blk'}, dimensions={0}, use_global_device_ids=true | all-gather | bytes 18432 | tf_op jit(solution)/shard_map/all_gather | solution.py:63
  57.0 7.1 %fusion.10 = f32[512,512]{0,1:T(8,128)S(1)} fusion(f32[512,2048]{1,0:T(8,128)} %param.1), kind=kOutput, calls=%fused_computation.40 | convolution fusion | flops 3221225472 | bytes 5242880 | tf_op jit(solution)/shard_map/dot_general | solution.py:23
  64.2 3.4 %collective-permute-start.3 = (f32[512,256]{0,1:T(8,128)S(1)}, f32[512,256]{0,1:T(8,128)S(1)}, u32[]{:S(2)}, u32[]{:S(2)}) collective-permute-start(f32[512,256]{0,1:T(8,128)S(1)} %get-tuple-element.73), channel_id=1, source_target_pairs={{1,0},{3,2},{5,4},{7,6},{8,9},{10,11},{12,13},{14,15},{17,16},{19,... | collective-permute-start | bytes 1572872 | tf_op jit(solution)/shard_map/ppermute | solution.py:50
  67.6 2.4 collective-permute-start.5
  70.1 5.3 %fusion.9 = f32[512,512]{0,1:T(8,128)S(1)} fusion(f32[512,2048]{1,0:T(8,128)S(1)} %copy-done, f32[512,2048]{1,0:T(8,128)} %collective-permute-done), kind=kOutput, calls=%fused_computation.39 | convolution fusion | flops 3221225472 | bytes 9437184 | tf_op jit(solution)/shard_map/dot_general | solution.py:23
  76.4 1.3 collective-permute-start.7
  77.7 2.1 collective-permute-start.9
  79.8 1.7 collective-permute-done.5
  81.8 1.5 collective-permute-start.6
  83.6 8.7 %collective-permute-done.7 = f32[512,256]{0,1:T(8,128)} collective-permute-done((f32[512,256]{0,1:T(8,128)}, f32[512,256]{0,1:T(8,128)}, u32[]{:S(2)}, u32[]{:S(2)}) %collective-permute-start.7) | collective-permute-done | bytes 524320 | tf_op jit(solution)/shard_map/ppermute | solution.py:50
  93.0 1.4 slice_add_fusion.9
  95.2 4.3 %collective-permute-start.8 = (f32[512,256]{0,1:T(8,128)S(1)}, f32[512,256]{0,1:T(8,128)S(1)}, u32[]{:S(2)}, u32[]{:S(2)}) collective-permute-start(f32[512,256]{0,1:T(8,128)S(1)} %get-tuple-element.67), channel_id=1, source_target_pairs={{2,0},{7,5},{10,8},{12,14},{19,17},{21,23},{24,26},{29,31}} | collective-permute-start | bytes 1572872 | tf_op jit(solution)/shard_map/ppermute | solution.py:50
  100.8 5.3 %collective-permute-done.8 = f32[512,256]{0,1:T(8,128)S(1)} collective-permute-done((f32[512,256]{0,1:T(8,128)S(1)}, f32[512,256]{0,1:T(8,128)S(1)}, u32[]{:S(2)}, u32[]{:S(2)}) %collective-permute-start.8) | collective-permute-done | bytes 524320 | tf_op jit(solution)/shard_map/ppermute | solution.py:50
  106.4 5.1 %collective-permute-done.2 = f32[512,512]{0,1:T(8,128)S(1)} collective-permute-done((f32[512,512]{0,1:T(8,128)S(1)}, f32[512,512]{0,1:T(8,128)S(1)}, u32[]{:S(2)}, u32[]{:S(2)}) %collective-permute-start.2) | collective-permute-done | bytes 1048608 | tf_op jit(solution)/shard_map/ppermute | solution.py:19
  111.5 5.5 %collective-permute-done.1 = f32[512,2048]{1,0:T(8,128)} collective-permute-done((f32[512,2048]{1,0:T(8,128)}, f32[512,2048]{1,0:T(8,128)}, u32[]{:S(2)}, u32[]{:S(2)}) %collective-permute-start.1) | collective-permute-done | bytes 4194336 | tf_op jit(solution)/shard_map/ppermute | solution.py:19
  117.1 1.3 collective-permute-start.13
  118.4 1.3 collective-permute-start.15
  119.7 5.3 %fusion.11 = f32[512,512]{0,1:T(8,128)S(1)} fusion(f32[512,2048]{1,0:T(8,128)S(1)} %copy-done.1, f32[512,2048]{1,0:T(8,128)} %collective-permute-done.1), kind=kOutput, calls=%fused_computation.41 | convolution fusion | flops 3221225472 | bytes 9437184 | tf_op jit(solution)/shard_map/dot_general | solution.py:23
  126.1 1.3 collective-permute-start.17
  127.4 5.4 %collective-permute-start.19 = (f32[512,256]{0,1:T(8,128)}, f32[512,256]{0,1:T(8,128)}, u32[]{:S(2)}, u32[]{:S(2)}) collective-permute-start(f32[512,256]{0,1:T(8,128)} %get-tuple-element.62), channel_id=1, source_target_pairs={{2,0},{3,1},{4,6},{5,7},{10,8},{11,9},{12,14},{13,15},{18,16},{19,... | collective-permute-start | bytes 1572872 | tf_op jit(solution)/shard_map/ppermute | solution.py:50
  133.9 1.3 collective-permute-start.16
  135.2 1.3 copy.7
  136.5 11.0 %collective-permute-start.12 = (f32[512,512]{0,1:T(8,128)}, f32[512,512]{0,1:T(8,128)S(1)}, u32[]{:S(2)}, u32[]{:S(2)}) collective-permute-start(f32[512,512]{0,1:T(8,128)} %bitcast.16), channel_id=1, source_target_pairs={{0,12},{8,4},{16,0},{24,8},{28,16},{20,24},{12,28},{4,20},{1,13},{... | collective-permute-start | bytes 3145736 | tf_op jit(solution)/shard_map/ppermute | solution.py:19
  147.6 1.3 collective-permute-start.14
  148.9 1.4 slice_add_fusion.7
  151.0 5.2 %collective-permute-start.18 = (f32[512,256]{0,1:T(8,128)S(1)}, f32[512,256]{0,1:T(8,128)S(1)}, u32[]{:S(2)}, u32[]{:S(2)}) collective-permute-start(f32[512,256]{0,1:T(8,128)S(1)} %get-tuple-element.59), channel_id=1, source_target_pairs={{3,1},{4,6},{10,8},{13,15},{18,16},{21,23},{27,25},{28,30}} | collective-permute-start | bytes 1572872 | tf_op jit(solution)/shard_map/ppermute | solution.py:50
  156.2 1.3 add.166
  157.5 1.4 collective-permute-done.14
  159.1 3.8 %collective-permute-done.18 = f32[512,256]{0,1:T(8,128)S(1)} collective-permute-done((f32[512,256]{0,1:T(8,128)S(1)}, f32[512,256]{0,1:T(8,128)S(1)}, u32[]{:S(2)}, u32[]{:S(2)}) %collective-permute-start.18) | collective-permute-done | bytes 524320 | tf_op jit(solution)/shard_map/ppermute | solution.py:50
  165.0 16.3 %collective-permute-done.12 = f32[512,512]{0,1:T(8,128)S(1)} collective-permute-done((f32[512,512]{0,1:T(8,128)}, f32[512,512]{0,1:T(8,128)S(1)}, u32[]{:S(2)}, u32[]{:S(2)}) %collective-permute-start.12) | collective-permute-done | bytes 1048608 | tf_op jit(solution)/shard_map/ppermute | solution.py:19
  181.3 4.5 %collective-permute-done.11 = f32[512,2048]{1,0:T(8,128)} collective-permute-done((f32[512,2048]{1,0:T(8,128)}, f32[512,2048]{1,0:T(8,128)}, u32[]{:S(2)}, u32[]{:S(2)}) %collective-permute-start.11) | collective-permute-done | bytes 4194336 | tf_op jit(solution)/shard_map/ppermute | solution.py:19
  185.9 2.5 collective-permute-start.21
  189.4 4.2 %collective-permute-start.22 = (f32[512,256]{0,1:T(8,128)}, f32[512,256]{0,1:T(8,128)}, u32[]{:S(2)}, u32[]{:S(2)}) collective-permute-start(f32[512,256]{0,1:T(8,128)} %get-tuple-element.57), channel_id=1, source_target_pairs={{1,0},{3,2},{4,5},{6,7},{8,9},{10,11},{13,12},{15,14},{16,17},{18,... | collective-permute-start | bytes 1572872 | tf_op jit(solution)/shard_map/ppermute | solution.py:50
  193.6 1.5 collective-permute-start.24
  195.1 5.3 %fusion.12 = f32[512,512]{0,1:T(8,128)S(1)} fusion(f32[512,2048]{1,0:T(8,128)S(1)} %copy-done.2, f32[512,2048]{1,0:T(8,128)} %collective-permute-done.11), kind=kOutput, calls=%fused_computation.42 | convolution fusion | flops 3221225472 | bytes 9437184 | tf_op jit(solution)/shard_map/dot_general | solution.py:23
  200.4 1.3 copy.8
  201.7 5.9 %collective-permute-start.34 = (f32[512,512]{0,1:T(8,128)}, f32[512,512]{0,1:T(8,128)S(1)}, u32[]{:S(2)}, u32[]{:S(2)}) collective-permute-start(f32[512,512]{0,1:T(8,128)} %bitcast.17), channel_id=1, source_target_pairs={{0,20},{8,12},{16,4},{24,0},{28,8},{20,16},{12,24},{4,28},{1,21},{... | collective-permute-start | bytes 3145736 | tf_op jit(solution)/shard_map/ppermute | solution.py:19
  207.6 3.4 %collective-permute-start.26 = (f32[512,256]{0,1:T(8,128)S(1)}, f32[512,256]{0,1:T(8,128)S(1)}, u32[]{:S(2)}, u32[]{:S(2)}) collective-permute-start(f32[512,256]{0,1:T(8,128)S(1)} %get-tuple-element.53), channel_id=1, source_target_pairs={{1,0},{3,2},{4,5},{6,7},{8,9},{10,11},{12,13},{14,15},{17,16},{19,... | collective-permute-start | bytes 1572872 | tf_op jit(solution)/shard_map/ppermute | solution.py:50
  211.0 2.5 collective-permute-start.28
  213.6 1.7 slice_add_fusion.13
  215.3 1.3 collective-permute-start.25
  216.6 5.9 %collective-permute-done.26 = f32[512,256]{0,1:T(8,128)S(1)} collective-permute-done((f32[512,256]{0,1:T(8,128)S(1)}, f32[512,256]{0,1:T(8,128)S(1)}, u32[]{:S(2)}, u32[]{:S(2)}) %collective-permute-start.26) | collective-permute-done | bytes 524320 | tf_op jit(solution)/shard_map/ppermute | solution.py:50
  224.1 32.1 %collective-permute-done.34 = f32[512,512]{0,1:T(8,128)S(1)} collective-permute-done((f32[512,512]{0,1:T(8,128)}, f32[512,512]{0,1:T(8,128)S(1)}, u32[]{:S(2)}, u32[]{:S(2)}) %collective-permute-start.34) | collective-permute-done | bytes 1048608 | tf_op jit(solution)/shard_map/ppermute | solution.py:19
  257.0 5.2 %collective-permute-start.35 = (f32[512,256]{0,1:T(8,128)S(1)}, f32[512,256]{0,1:T(8,128)S(1)}, u32[]{:S(2)}, u32[]{:S(2)}) collective-permute-start(f32[512,256]{0,1:T(8,128)S(1)} %get-tuple-element.49), channel_id=1, source_target_pairs={{0,1},{2,3},{5,4},{7,6},{8,9},{10,11},{12,13},{14,15},{17,16},{19,... | collective-permute-start | bytes 1572872 | tf_op jit(solution)/shard_map/ppermute | solution.py:50
  262.3 1.6 collective-permute-start.37
  266.3 2.1 collective-permute-done.21
  268.4 5.3 %fusion.13 = f32[512,512]{0,1:T(8,128)S(1)} fusion(f32[512,2048]{1,0:T(8,128)S(1)} %copy-done.3, f32[512,2048]{1,0:T(8,128)} %collective-permute-done.21), kind=kOutput, calls=%fused_computation.43 | convolution fusion | flops 3221225472 | bytes 9437184 | tf_op jit(solution)/shard_map/dot_general | solution.py:23
  273.8 1.3 collective-permute-start.30
  275.1 1.3 collective-permute-start.32
  277.6 5.4 %collective-permute-start.38 = (f32[512,256]{0,1:T(8,128)}, f32[512,256]{0,1:T(8,128)}, u32[]{:S(2)}, u32[]{:S(2)}) collective-permute-start(f32[512,256]{0,1:T(8,128)} %get-tuple-element.48), channel_id=1, source_target_pairs={{2,3},{7,6},{10,11},{12,13},{19,18},{21,20},{24,25},{29,28}} | collective-permute-start | bytes 1572872 | tf_op jit(solution)/shard_map/ppermute | solution.py:50
  283.0 1.6 collective-permute-start.36
  284.5 5.6 %collective-permute-done.30 = f32[512,256]{0,1:T(8,128)S(1)} collective-permute-done((f32[512,256]{0,1:T(8,128)S(1)}, f32[512,256]{0,1:T(8,128)S(1)}, u32[]{:S(2)}, u32[]{:S(2)}) %collective-permute-start.30) | collective-permute-done | bytes 524320 | tf_op jit(solution)/shard_map/ppermute | solution.py:50
  290.2 1.3 collective-permute-done.32
  292.7 1.3 collective-permute-start.33
  294.0 1.3 collective-permute-start.31
  295.4 1.4 add.186
  296.9 1.3 add.184
  298.2 11.2 %collective-permute-done.33 = f32[512,256]{0,1:T(8,128)} collective-permute-done((f32[512,256]{0,1:T(8,128)}, f32[512,256]{0,1:T(8,128)}, u32[]{:S(2)}, u32[]{:S(2)}) %collective-permute-start.33) | collective-permute-done | bytes 524320 | tf_op jit(solution)/shard_map/ppermute | solution.py:50
  309.4 1.3 add.182
  310.7 1.3 add.180
  314.4 1.8 copy.9
  (89 shorter events, 20.7 us)
Async XLA Ops:
  0.0 57.0 %collective-permute-start = (f32[512,2048]{1,0:T(8,128)}, f32[512,2048]{1,0:T(8,128)}, u32[]{:S(2)}, u32[]{:S(2)}) collective-permute-start(f32[512,2048]{1,0:T(8,128)} %param.1), channel_id=1, source_target_pairs={{0,8},{8,16},{16,24},{24,28},{28,20},{20,12},{12,4},{4,0},{1,9},{9... | collective-permute-start | bytes 12582920 | tf_op jit(solution)/shard_map/ppermute | solution.py:19
  57.0 13.1 %copy-start = (f32[512,2048]{1,0:T(8,128)S(1)}, f32[512,2048]{1,0:T(8,128)}, u32[]{:S(2)}) copy-start(f32[512,2048]{1,0:T(8,128)} %param.1) | copy-start | bytes 12582916
  57.0 60.1 %collective-permute-start.1 = (f32[512,2048]{1,0:T(8,128)}, f32[512,2048]{1,0:T(8,128)}, u32[]{:S(2)}, u32[]{:S(2)}) collective-permute-start(f32[512,2048]{1,0:T(8,128)} %collective-permute-done), channel_id=1, source_target_pairs={{0,8},{8,16},{16,24},{24,28},{28,20},{20,12},{12,4},{4,0},{1,9},{9... | collective-permute-start | bytes 12582920 | tf_op jit(solution)/shard_map/ppermute | solution.py:19
  64.2 15.6 %collective-permute-start.3 = (f32[512,256]{0,1:T(8,128)S(1)}, f32[512,256]{0,1:T(8,128)S(1)}, u32[]{:S(2)}, u32[]{:S(2)}) collective-permute-start(f32[512,256]{0,1:T(8,128)S(1)} %get-tuple-element.73), channel_id=1, source_target_pairs={{1,0},{3,2},{5,4},{7,6},{8,9},{10,11},{12,13},{14,15},{17,16},{19,... | collective-permute-start | bytes 1572872 | tf_op jit(solution)/shard_map/ppermute | solution.py:50
  67.6 13.9 %collective-permute-start.5 = (f32[512,256]{0,1:T(8,128)S(1)}, f32[512,256]{0,1:T(8,128)S(1)}, u32[]{:S(2)}, u32[]{:S(2)}) collective-permute-start(f32[512,256]{0,1:T(8,128)S(1)} %get-tuple-element.74), channel_id=1, source_target_pairs={{2,0},{3,1},{6,4},{7,5},{10,8},{11,9},{14,12},{15,13},{16,18},{17,... | collective-permute-start | bytes 1572872 | tf_op jit(solution)/shard_map/ppermute | solution.py:50
  76.4 15.9 %collective-permute-start.7 = (f32[512,256]{0,1:T(8,128)}, f32[512,256]{0,1:T(8,128)}, u32[]{:S(2)}, u32[]{:S(2)}) collective-permute-start(f32[512,256]{0,1:T(8,128)} %get-tuple-element.69), channel_id=1, source_target_pairs={{1,0},{3,2},{4,5},{6,7},{9,8},{11,10},{13,12},{15,14},{16,17},{18,... | collective-permute-start | bytes 1572872 | tf_op jit(solution)/shard_map/ppermute | solution.py:50
  77.7 15.3 %collective-permute-start.9 = (f32[512,256]{0,1:T(8,128)}, f32[512,256]{0,1:T(8,128)}, u32[]{:S(2)}, u32[]{:S(2)}) collective-permute-start(f32[512,256]{0,1:T(8,128)} %get-tuple-element.70), channel_id=1, source_target_pairs={{2,0},{3,1},{6,4},{7,5},{10,8},{11,9},{12,14},{13,15},{18,16},{19,... | collective-permute-start | bytes 1572872 | tf_op jit(solution)/shard_map/ppermute | solution.py:50
  81.8 13.4 %collective-permute-start.6 = (f32[512,256]{0,1:T(8,128)S(1)}, f32[512,256]{0,1:T(8,128)}, u32[]{:S(2)}, u32[]{:S(2)}) collective-permute-start(f32[512,256]{0,1:T(8,128)S(1)} %get-tuple-element.72), channel_id=1, source_target_pairs={{1,0},{5,4},{8,9},{12,13},{19,18},{23,22},{26,27},{30,31}} | collective-permute-start | bytes 1572872 | tf_op jit(solution)/shard_map/ppermute | solution.py:50
  83.6 27.9 %collective-permute-start.2 = (f32[512,512]{0,1:T(8,128)S(1)}, f32[512,512]{0,1:T(8,128)S(1)}, u32[]{:S(2)}, u32[]{:S(2)}) collective-permute-start(f32[512,512]{0,1:T(8,128)S(1)} %bitcast.15), channel_id=1, source_target_pairs={{0,4},{8,0},{16,8},{24,16},{28,24},{20,28},{12,20},{4,12},{1,5},{9... | collective-permute-start | bytes 3145736 | tf_op jit(solution)/shard_map/ppermute | solution.py:19
  92.3 8.3 %collective-permute-start.4 = (f32[512,256]{0,1:T(8,128)S(1)}, f32[512,256]{0,1:T(8,128)S(1)}, u32[]{:S(2)}, u32[]{:S(2)}) collective-permute-start(f32[512,256]{0,1:T(8,128)S(1)} %get-tuple-element.71), channel_id=1, source_target_pairs={{2,0},{6,4},{11,9},{15,13},{16,18},{20,22},{25,27},{29,31}} | collective-permute-start | bytes 1572872 | tf_op jit(solution)/shard_map/ppermute | solution.py:50
  94.5 6.2 %collective-permute-start.10 = (f32[512,256]{0,1:T(8,128)S(1)}, f32[512,256]{0,1:T(8,128)S(1)}, u32[]{:S(2)}, u32[]{:S(2)}) collective-permute-start(f32[512,256]{0,1:T(8,128)S(1)} %get-tuple-element.68), channel_id=1, source_target_pairs={{1,0},{4,5},{9,8},{15,14},{16,17},{22,23},{27,26},{30,31}} | collective-permute-start | bytes 1572872 | tf_op jit(solution)/shard_map/ppermute | solution.py:50
  95.2 11.0 %collective-permute-start.8 = (f32[512,256]{0,1:T(8,128)S(1)}, f32[512,256]{0,1:T(8,128)S(1)}, u32[]{:S(2)}, u32[]{:S(2)}) collective-permute-start(f32[512,256]{0,1:T(8,128)S(1)} %get-tuple-element.67), channel_id=1, source_target_pairs={{2,0},{7,5},{10,8},{12,14},{19,17},{21,23},{24,26},{29,31}} | collective-permute-start | bytes 1572872 | tf_op jit(solution)/shard_map/ppermute | solution.py:50
  100.8 18.9 %copy-start.1 = (f32[512,2048]{1,0:T(8,128)S(1)}, f32[512,2048]{1,0:T(8,128)}, u32[]{:S(2)}) copy-start(f32[512,2048]{1,0:T(8,128)} %param.1) | copy-start | bytes 12582916
  117.0 68.8 %collective-permute-start.11 = (f32[512,2048]{1,0:T(8,128)}, f32[512,2048]{1,0:T(8,128)}, u32[]{:S(2)}, u32[]{:S(2)}) collective-permute-start(f32[512,2048]{1,0:T(8,128)} %collective-permute-done.1), channel_id=1, source_target_pairs={{0,8},{8,16},{16,24},{24,28},{28,20},{20,12},{12,4},{4,0},{1,9},{9... | collective-permute-start | bytes 12582920 | tf_op jit(solution)/shard_map/ppermute | solution.py:19
  117.1 15.6 %collective-permute-start.13 = (f32[512,256]{0,1:T(8,128)S(1)}, f32[512,256]{0,1:T(8,128)S(1)}, u32[]{:S(2)}, u32[]{:S(2)}) collective-permute-start(f32[512,256]{0,1:T(8,128)S(1)} %get-tuple-element.65), channel_id=1, source_target_pairs={{0,1},{2,3},{5,4},{7,6},{9,8},{11,10},{13,12},{15,14},{16,17},{18,... | collective-permute-start | bytes 1572872 | tf_op jit(solution)/shard_map/ppermute | solution.py:50
  118.4 14.3 %collective-permute-start.15 = (f32[512,256]{0,1:T(8,128)S(1)}, f32[512,256]{0,1:T(8,128)S(1)}, u32[]{:S(2)}, u32[]{:S(2)}) collective-permute-start(f32[512,256]{0,1:T(8,128)S(1)} %get-tuple-element.66), channel_id=1, source_target_pairs={{2,0},{3,1},{6,4},{7,5},{8,10},{9,11},{14,12},{15,13},{16,18},{17,... | collective-permute-start | bytes 1572872 | tf_op jit(solution)/shard_map/ppermute | solution.py:50
  126.1 21.5 %collective-permute-start.17 = (f32[512,256]{0,1:T(8,128)}, f32[512,256]{0,1:T(8,128)}, u32[]{:S(2)}, u32[]{:S(2)}) collective-permute-start(f32[512,256]{0,1:T(8,128)} %get-tuple-element.61), channel_id=1, source_target_pairs={{0,1},{2,3},{5,4},{7,6},{9,8},{11,10},{12,13},{14,15},{17,16},{19,... | collective-permute-start | bytes 1572872 | tf_op jit(solution)/shard_map/ppermute | solution.py:50
  127.4 21.5 %collective-permute-start.19 = (f32[512,256]{0,1:T(8,128)}, f32[512,256]{0,1:T(8,128)}, u32[]{:S(2)}, u32[]{:S(2)}) collective-permute-start(f32[512,256]{0,1:T(8,128)} %get-tuple-element.62), channel_id=1, source_target_pairs={{2,0},{3,1},{4,6},{5,7},{10,8},{11,9},{12,14},{13,15},{18,16},{19,... | collective-permute-start | bytes 1572872 | tf_op jit(solution)/shard_map/ppermute | solution.py:50
  133.9 17.1 %collective-permute-start.16 = (f32[512,256]{0,1:T(8,128)}, f32[512,256]{0,1:T(8,128)}, u32[]{:S(2)}, u32[]{:S(2)}) collective-permute-start(f32[512,256]{0,1:T(8,128)} %get-tuple-element.64), channel_id=1, source_target_pairs={{0,1},{5,4},{11,10},{13,12},{18,19},{20,21},{26,27},{31,30}} | collective-permute-start | bytes 1572872 | tf_op jit(solution)/shard_map/ppermute | solution.py:50
  136.5 22.3 %copy-start.9 = (f32[512,256]{0,1:T(8,128)S(1)}, f32[512,256]{0,1:T(8,128)}, u32[]{:S(2)}) copy-start(f32[512,256]{0,1:T(8,128)} %get-tuple-element.63) | copy-start | bytes 1572868
  136.5 44.8 %collective-permute-start.12 = (f32[512,512]{0,1:T(8,128)}, f32[512,512]{0,1:T(8,128)S(1)}, u32[]{:S(2)}, u32[]{:S(2)}) collective-permute-start(f32[512,512]{0,1:T(8,128)} %bitcast.16), channel_id=1, source_target_pairs={{0,12},{8,4},{16,0},{24,8},{28,16},{20,24},{12,28},{4,20},{1,13},{... | collective-permute-start | bytes 3145736 | tf_op jit(solution)/shard_map/ppermute | solution.py:19
  147.6 11.3 %collective-permute-start.14 = (f32[512,256]{0,1:T(8,128)}, f32[512,256]{0,1:T(8,128)S(1)}, u32[]{:S(2)}, u32[]{:S(2)}) collective-permute-start(f32[512,256]{0,1:T(8,128)} %get-tuple-element.63), channel_id=1, source_target_pairs={{3,1},{6,4},{8,10},{14,12},{17,19},{23,21},{25,27},{28,30}} | collective-permute-start | bytes 1572872 | tf_op jit(solution)/shard_map/ppermute | solution.py:50
  150.3 8.7 %collective-permute-start.20 = (f32[512,256]{0,1:T(8,128)S(1)}, f32[512,256]{0,1:T(8,128)S(1)}, u32[]{:S(2)}, u32[]{:S(2)}) collective-permute-start(f32[512,256]{0,1:T(8,128)S(1)} %get-tuple-element.60), channel_id=1, source_target_pairs={{0,1},{7,6},{9,8},{14,15},{17,16},{22,23},{24,25},{31,30}} | collective-permute-start | bytes 1572872 | tf_op jit(solution)/shard_map/ppermute | solution.py:50
  151.0 11.9 %collective-permute-start.18 = (f32[512,256]{0,1:T(8,128)S(1)}, f32[512,256]{0,1:T(8,128)S(1)}, u32[]{:S(2)}, u32[]{:S(2)}) collective-permute-start(f32[512,256]{0,1:T(8,128)S(1)} %get-tuple-element.59), channel_id=1, source_target_pairs={{3,1},{4,6},{10,8},{13,15},{18,16},{21,23},{27,25},{28,30}} | collective-permute-start | bytes 1572872 | tf_op jit(solution)/shard_map/ppermute | solution.py:50
  159.0 36.0 %copy-start.2 = (f32[512,2048]{1,0:T(8,128)S(1)}, f32[512,2048]{1,0:T(8,128)}, u32[]{:S(2)}) copy-start(f32[512,2048]{1,0:T(8,128)} %param.1) | copy-start | bytes 12582916
  181.3 12.3 %copy-start.8 = (f32[512,512]{0,1:T(8,128)}, f32[512,512]{0,1:T(8,128)S(1)}, u32[]{:S(2)}) copy-start(f32[512,512]{0,1:T(8,128)S(1)} %collective-permute-done.12) | copy-start | bytes 3145732
  185.9 82.5 %collective-permute-start.21 = (f32[512,2048]{1,0:T(8,128)}, f32[512,2048]{1,0:T(8,128)}, u32[]{:S(2)}, u32[]{:S(2)}) collective-permute-start(f32[512,2048]{1,0:T(8,128)} %collective-permute-done.11), channel_id=1, source_target_pairs={{0,8},{8,16},{16,24},{24,28},{28,20},{20,12},{12,4},{4,0},{1,9},{9... | collective-permute-start | bytes 12582920 | tf_op jit(solution)/shard_map/ppermute | solution.py:19
  189.4 21.6 %collective-permute-start.22 = (f32[512,256]{0,1:T(8,128)}, f32[512,256]{0,1:T(8,128)}, u32[]{:S(2)}, u32[]{:S(2)}) collective-permute-start(f32[512,256]{0,1:T(8,128)} %get-tuple-element.57), channel_id=1, source_target_pairs={{1,0},{3,2},{4,5},{6,7},{8,9},{10,11},{13,12},{15,14},{16,17},{18,... | collective-permute-start | bytes 1572872 | tf_op jit(solution)/shard_map/ppermute | solution.py:50
  193.6 19.9 %collective-permute-start.24 = (f32[512,256]{0,1:T(8,128)}, f32[512,256]{0,1:T(8,128)}, u32[]{:S(2)}, u32[]{:S(2)}) collective-permute-start(f32[512,256]{0,1:T(8,128)} %get-tuple-element.58), channel_id=1, source_target_pairs={{0,2},{1,3},{6,4},{7,5},{8,10},{9,11},{14,12},{15,13},{16,18},{17,... | collective-permute-start | bytes 1572872 | tf_op jit(solution)/shard_map/ppermute | solution.py:50
  201.7 54.5 %collective-permute-start.34 = (f32[512,512]{0,1:T(8,128)}, f32[512,512]{0,1:T(8,128)S(1)}, u32[]{:S(2)}, u32[]{:S(2)}) collective-permute-start(f32[512,512]{0,1:T(8,128)} %bitcast.17), channel_id=1, source_target_pairs={{0,20},{8,12},{16,4},{24,0},{28,8},{20,16},{12,24},{4,28},{1,21},{... | collective-permute-start | bytes 3145736 | tf_op jit(solution)/shard_map/ppermute | solution.py:19
  207.6 14.9 %collective-permute-start.26 = (f32[512,256]{0,1:T(8,128)S(1)}, f32[512,256]{0,1:T(8,128)S(1)}, u32[]{:S(2)}, u32[]{:S(2)}) collective-permute-start(f32[512,256]{0,1:T(8,128)S(1)} %get-tuple-element.53), channel_id=1, source_target_pairs={{1,0},{3,2},{4,5},{6,7},{8,9},{10,11},{12,13},{14,15},{17,16},{19,... | collective-permute-start | bytes 1572872 | tf_op jit(solution)/shard_map/ppermute | solution.py:50
  211.0 12.1 %collective-permute-start.28 = (f32[512,256]{0,1:T(8,128)S(1)}, f32[512,256]{0,1:T(8,128)S(1)}, u32[]{:S(2)}, u32[]{:S(2)}) collective-permute-start(f32[512,256]{0,1:T(8,128)S(1)} %get-tuple-element.54), channel_id=1, source_target_pairs={{0,2},{1,3},{4,6},{5,7},{10,8},{11,9},{12,14},{13,15},{18,16},{19,... | collective-permute-start | bytes 1572872 | tf_op jit(solution)/shard_map/ppermute | solution.py:50
  215.3 41.7 %collective-permute-start.25 = (f32[512,256]{0,1:T(8,128)S(1)}, f32[512,256]{0,1:T(8,128)S(1)}, u32[]{:S(2)}, u32[]{:S(2)}) collective-permute-start(f32[512,256]{0,1:T(8,128)S(1)} %get-tuple-element.56), channel_id=1, source_target_pairs={{3,2},{4,5},{10,11},{13,12},{18,19},{21,20},{27,26},{28,29}} | collective-permute-start | bytes 1572872 | tf_op jit(solution)/shard_map/ppermute | solution.py:50
  222.5 39.8 %collective-permute-start.23 = (f32[512,256]{0,1:T(8,128)S(1)}, f32[512,256]{0,1:T(8,128)S(1)}, u32[]{:S(2)}, u32[]{:S(2)}) collective-permute-start(f32[512,256]{0,1:T(8,128)S(1)} %get-tuple-element.55), channel_id=1, source_target_pairs={{0,2},{7,5},{9,11},{14,12},{17,19},{22,20},{24,26},{31,29}} | collective-permute-start | bytes 1572872 | tf_op jit(solution)/shard_map/ppermute | solution.py:50
  223.4 40.6 %collective-permute-start.29 = (f32[512,256]{0,1:T(8,128)S(1)}, f32[512,256]{0,1:T(8,128)S(1)}, u32[]{:S(2)}, u32[]{:S(2)}) collective-permute-start(f32[512,256]{0,1:T(8,128)S(1)} %get-tuple-element.52), channel_id=1, source_target_pairs={{3,2},{6,7},{8,9},{14,15},{17,16},{23,22},{25,24},{28,29}} | collective-permute-start | bytes 1572872 | tf_op jit(solution)/shard_map/ppermute | solution.py:50
  256.2 7.8 %collective-permute-start.27 = (f32[512,256]{0,1:T(8,128)S(1)}, f32[512,256]{0,1:T(8,128)S(1)}, u32[]{:S(2)}, u32[]{:S(2)}) collective-permute-start(f32[512,256]{0,1:T(8,128)S(1)} %get-tuple-element.51), channel_id=1, source_target_pairs={{0,2},{5,7},{11,9},{13,15},{18,16},{20,22},{26,24},{31,29}} | collective-permute-start | bytes 1572872 | tf_op jit(solution)/shard_map/ppermute | solution.py:50
  257.0 19.3 %collective-permute-start.35 = (f32[512,256]{0,1:T(8,128)S(1)}, f32[512,256]{0,1:T(8,128)S(1)}, u32[]{:S(2)}, u32[]{:S(2)}) collective-permute-start(f32[512,256]{0,1:T(8,128)S(1)} %get-tuple-element.49), channel_id=1, source_target_pairs={{0,1},{2,3},{5,4},{7,6},{8,9},{10,11},{12,13},{14,15},{17,16},{19,... | collective-permute-start | bytes 1572872 | tf_op jit(solution)/shard_map/ppermute | solution.py:50
  262.3 6.1 %copy-start.3 = (f32[512,2048]{1,0:T(8,128)S(1)}, f32[512,2048]{1,0:T(8,128)}, u32[]{:S(2)}) copy-start(f32[512,2048]{1,0:T(8,128)} %param.1) | copy-start | bytes 12582916
  262.3 14.1 %collective-permute-start.37 = (f32[512,256]{0,1:T(8,128)S(1)}, f32[512,256]{0,1:T(8,128)S(1)}, u32[]{:S(2)}, u32[]{:S(2)}) collective-permute-start(f32[512,256]{0,1:T(8,128)S(1)} %get-tuple-element.50), channel_id=1, source_target_pairs={{0,2},{1,3},{4,6},{5,7},{8,10},{9,11},{14,12},{15,13},{16,18},{17,... | collective-permute-start | bytes 1572872 | tf_op jit(solution)/shard_map/ppermute | solution.py:50
  273.8 16.4 %collective-permute-start.30 = (f32[512,256]{0,1:T(8,128)S(1)}, f32[512,256]{0,1:T(8,128)S(1)}, u32[]{:S(2)}, u32[]{:S(2)}) collective-permute-start(f32[512,256]{0,1:T(8,128)S(1)} %get-tuple-element.45), channel_id=1, source_target_pairs={{0,1},{2,3},{4,5},{6,7},{9,8},{11,10},{13,12},{15,14},{16,17},{18,... | collective-permute-start | bytes 1572872 | tf_op jit(solution)/shard_map/ppermute | solution.py:50
  275.1 16.4 %collective-permute-start.32 = (f32[512,256]{0,1:T(8,128)S(1)}, f32[512,256]{0,1:T(8,128)S(1)}, u32[]{:S(2)}, u32[]{:S(2)}) collective-permute-start(f32[512,256]{0,1:T(8,128)S(1)} %get-tuple-element.46), channel_id=1, source_target_pairs={{0,2},{1,3},{4,6},{5,7},{8,10},{9,11},{12,14},{13,15},{18,16},{19,... | collective-permute-start | bytes 1572872 | tf_op jit(solution)/shard_map/ppermute | solution.py:50
  277.6 17.8 %collective-permute-start.38 = (f32[512,256]{0,1:T(8,128)}, f32[512,256]{0,1:T(8,128)}, u32[]{:S(2)}, u32[]{:S(2)}) collective-permute-start(f32[512,256]{0,1:T(8,128)} %get-tuple-element.48), channel_id=1, source_target_pairs={{2,3},{7,6},{10,11},{12,13},{19,18},{21,20},{24,25},{29,28}} | collective-permute-start | bytes 1572872 | tf_op jit(solution)/shard_map/ppermute | solution.py:50
  283.0 29.0 %copy-start.4 = (f32[512,512]{0,1:T(8,128)S(1)}, f32[512,512]{0,1:T(8,128)}, u32[]{:S(2)}) copy-start(f32[512,512]{0,1:T(8,128)} %pad_maximum_fusion.2) | copy-start | bytes 3145732
  283.0 13.9 %collective-permute-start.36 = (f32[512,256]{0,1:T(8,128)}, f32[512,256]{0,1:T(8,128)}, u32[]{:S(2)}, u32[]{:S(2)}) collective-permute-start(f32[512,256]{0,1:T(8,128)} %get-tuple-element.47), channel_id=1, source_target_pairs={{1,3},{4,6},{9,11},{15,13},{16,18},{22,20},{27,25},{30,28}} | collective-permute-start | bytes 1572872 | tf_op jit(solution)/shard_map/ppermute | solution.py:50
  292.7 16.7 %collective-permute-start.33 = (f32[512,256]{0,1:T(8,128)}, f32[512,256]{0,1:T(8,128)}, u32[]{:S(2)}, u32[]{:S(2)}) collective-permute-start(f32[512,256]{0,1:T(8,128)} %get-tuple-element.44), channel_id=1, source_target_pairs={{2,3},{6,7},{11,10},{15,14},{16,17},{20,21},{25,24},{29,28}} | collective-permute-start | bytes 1572872 | tf_op jit(solution)/shard_map/ppermute | solution.py:50
  294.0 16.7 %collective-permute-start.31 = (f32[512,256]{0,1:T(8,128)}, f32[512,256]{0,1:T(8,128)}, u32[]{:S(2)}, u32[]{:S(2)}) collective-permute-start(f32[512,256]{0,1:T(8,128)} %get-tuple-element.43), channel_id=1, source_target_pairs={{1,3},{5,7},{8,10},{12,14},{19,17},{23,21},{26,24},{30,28}} | collective-permute-start | bytes 1572872 | tf_op jit(solution)/shard_map/ppermute | solution.py:50
  295.4 16.6 %copy-start.5 = (f32[512,512]{0,1:T(8,128)S(1)}, f32[512,512]{0,1:T(8,128)}, u32[]{:S(2)}) copy-start(f32[512,512]{0,1:T(8,128)} %pad_maximum_fusion.3) | copy-start | bytes 3145732
  295.4 16.6 %copy-start.6 = (f32[512,512]{0,1:T(8,128)S(1)}, f32[512,512]{0,1:T(8,128)}, u32[]{:S(2)}) copy-start(f32[512,512]{0,1:T(8,128)} %pad_maximum_fusion.4) | copy-start | bytes 3145732
  295.4 16.6 %copy-start.7 = (f32[512,512]{0,1:T(8,128)S(1)}, f32[512,512]{0,1:T(8,128)}, u32[]{:S(2)}) copy-start(f32[512,512]{0,1:T(8,128)} %pad_maximum_fusion.5) | copy-start | bytes 3145732
